TPU v7x, 32 devices: a whole 2x2x4 slice. The times are simulated.
32 devices in a mesh: seq: 8 (over y, x, core), head: 4 (over z).
Axes of the slice: x: 2, y: 2, z: 4, core: 2. Of those that a mesh axis runs over, the one named last changes fastest.
Arguments:
- queries: bfloat16 [8192, 1024], P('seq', 'head'), may hold values from -6 to 6
- values: bfloat16 [8192, 1024], P('seq', 'head'), may hold values from -6 to 6
- w_out: bfloat16 [1024, 1024], P('head'), may hold values from -0.1875 to 0.1875
- out_grad: bfloat16 [8192, 1024], P('seq', 'head'), may hold values from -6 to 6
- slots: int32 [2, 16, 8192], P(None, 'head', 'seq'), may hold values from 0 to 8191, as said below
Outputs:
- output: bfloat16 [8192, 1024], P('seq', 'head')
- query_grad: bfloat16 [8192, 1024], P('seq', 'head')
- value_grad: bfloat16 [8192, 1024], P('seq', 'head')
- w_out_grad: float32 [1024, 1024], P('head')
Inputs may be any that keep to these rules, and one draw needn't show every extreme that they name: slots[r, h] is a permutation of the token positions: each token's place in round r's stable sort of head h's bucket ids. Of the 1024 tokens of one device of seq, exactly 192 have places among the 1024 places of one device of seq (possibly itself), 64 among those of the next device cyclically, and 128 among those of each other device.
All inputs are finite; a program needn't handle non-finite values.
Results may differ from a plain program's by a relative error of at most 0.024.
Values may be sent and summed in bfloat16 or wider, within the bound.
No kernel may reach another device: no remote copies, remote signals or barrier semaphores. Data moves between devices by JAX's collectives and lax.ppermute only.
A program may use at most 64 MiB of HBM per device.

v0:
```python
import functools

import jax
import jax.numpy as jnp
from jax import lax
from jax.experimental import pallas as pl
from jax.experimental.pallas import tpu as pltpu
from jax.sharding import PartitionSpec as P

DH = 64
SPAN = 128
LANES = 128
GROUP = 8
SUB = 4
F32 = jnp.float32
BF16 = jnp.bfloat16
NT = (((1,), (1,)), ((), ()))
TN = (((0,), (0,)), ((), ()))
MIB = 1 << 20


def whole(space):
    return pl.BlockSpec(memory_space=space)


def fixed(shape):
    return pl.BlockSpec(shape, lambda g: (0,) * len(shape), pipeline_mode=pl.Buffered(1))


def lane_of(shape):
    return lax.broadcasted_iota(jnp.int32, shape, len(shape) - 1)


def places_kernel(mine_ref, addr_ref, key_place, query_place, sign_ref):
    sources, _, lanes = mine_ref.shape
    blocks = addr_ref.shape[0]
    rows = mine_ref.shape[1] - 16
    parts = (mine_ref.shape[1] - rows) // 2
    core = lax.rem(lax.axis_index("seq"), 2)
    block_row = lax.broadcasted_iota(jnp.int32, (blocks, lanes), 0).astype(F32)
    place_row = lax.broadcasted_iota(jnp.int32, (lanes, lanes), 0).astype(F32)
    token_low = lane_of((blocks, lanes)).astype(F32)
    total = jnp.zeros((2 * blocks, lanes), F32)
    for s in range(sources):
        slots = mine_ref[s, rows:, :].astype(F32)
        tall = []
        wide = []
        for j in range(parts):
            in_block = block_row == slots[j : j + 1, :]
            token_high = float(s * parts + j)
            tall.append(
                jnp.concatenate(
                    [jnp.where(in_block, token_high, 0.0), jnp.where(in_block, token_low, 0.0)],
                    axis=0,
                ).astype(BF16)
            )
            wide.append((place_row == slots[parts + j : parts + j + 1, :]).astype(BF16))
        total += lax.dot_general(
            jnp.concatenate(tall, axis=1),
            jnp.concatenate(wide, axis=1),
            NT,
            preferred_element_type=F32,
        )
    place = total[:blocks] * float(lanes) + total[blocks:]
    token = place.astype(jnp.int32)
    source = token // (2 * rows)
    within = token - source * (2 * rows)
    part = within // rows
    addr_ref[...] = ((part ^ core) * sources + source) * rows + (within - part * rows)
    before = pltpu.roll(place, 1, 0)
    least = jnp.minimum(
        jnp.min(place, axis=1, keepdims=True), jnp.min(before, axis=1, keepdims=True)
    )
    window = jnp.concatenate([before, place], axis=1)
    window = jnp.where(window == least, window - 0.5, window)
    for c in range(blocks):
        key_place[c] = window[c : c + 1, :]
    columns = jnp.transpose(place)
    alone = jnp.transpose(jnp.where(place == least, -1.0, 1.0))
    for g in range(blocks // GROUP):
        query_place[g] = columns[:, g * GROUP : (g + 1) * GROUP]
        sign_ref[g] = alone[:, g * GROUP : (g + 1) * GROUP]


def find_places(mine):
    sources, rows, lanes = mine.shape
    blocks = 2 * sources * (rows - 16) // lanes
    column = jax.ShapeDtypeStruct((blocks // GROUP, lanes, GROUP), F32)
    return pl.pallas_call(
        places_kernel,
        out_shape=[
            jax.ShapeDtypeStruct((blocks, lanes), jnp.int32),
            jax.ShapeDtypeStruct((blocks, 1, 2 * lanes), F32),
            column,
            column,
        ],
        compiler_params=pltpu.CompilerParams(vmem_limit_bytes=10 * MIB),
        name="find_places",
    )(mine)


def gather_rows(addr_ref, block, source, target):
    for j in range(SPAN):
        target[pl.ds(j, 1), :] = source[pl.ds(addr_ref[block, j], 1), :]


def scatter_rows(addr_ref, block, source, target):
    for j in range(SPAN):
        target[pl.ds(addr_ref[block, j], 1), :] = source[pl.ds(j, 1), :]


def split_sum(product, chosen):
    high = product.astype(BF16)
    rest = (product - high.astype(F32)).astype(BF16)
    return jnp.dot(
        jnp.concatenate([high, rest], axis=1),
        jnp.concatenate([chosen, chosen], axis=0),
        preferred_element_type=F32,
    )


def low_lanes(scale=1.0):
    row = lax.broadcasted_iota(jnp.int32, (LANES, LANES), 0)
    return jnp.where(row < DH, scale, 0.0).astype(BF16)


def inverse_of(rows):
    return lax.rsqrt(split_sum(rows * rows, low_lanes(1.0 / DH)) + 1e-06)


def forward_kernel(
    addr_ref, mine_ref, other_ref, key_place, query_place, sign_ref,
    home_ref, away_ref, prob_ref, qv_ref, key_ref,
    tokens, result, in_even, in_odd, out_even, out_odd, grown_ref, qv_win, key_win,
):
    step = pl.program_id(0)
    last = pl.num_programs(0) - 1
    sources = mine_ref.shape[0]
    rows = mine_ref.shape[1] - 16
    half = sources * rows
    blocks = 2 * half // SPAN
    score_scale = DH ** (-0.5) * 1.4426950408889634
    rows_in = (in_even, in_odd)
    rows_out = (out_even, out_odd)

    def place_rows(values, at):
        low = lane_of(values.shape) < DH
        qv_win[at] = values.astype(BF16)
        key_win[at] = jnp.where(low, values * inverse_of(values), 0.0).astype(BF16)

    @pl.when(step == 0)
    def _():
        for s in range(sources):
            tokens[s * rows : (s + 1) * rows, :] = mine_ref[s, :rows, :].astype(F32)
            tokens[half + s * rows : half + (s + 1) * rows, :] = other_ref[s, :rows, :].astype(F32)
        gather_rows(addr_ref, blocks - 1, tokens, in_odd.at[0])
        place_rows(in_odd[0], slice(0, SPAN))
        for b in range(SUB):
            gather_rows(addr_ref, b, tokens, in_even.at[b])

    ones = jnp.ones((2 * SPAN, LANES), BF16)
    low = lane_of((SPAN, LANES)) < DH
    first = lane_of((SPAN, LANES)) == 0
    for p in range(GROUP // SUB):
        here = step * GROUP + p * SUB
        coming = jnp.minimum(here + SUB, blocks - SUB)
        gone = jnp.maximum(here - SUB, 0)
        now, then = p % 2, 1 - p % 2
        spans = slice((p * SUB + 1) * SPAN, ((p + 1) * SUB + 1) * SPAN)
        place_rows(rows_in[now][...].reshape(SUB * SPAN, LANES), spans)
        for i in range(SUB):
            b = p * SUB + i
            own = slice((b + 1) * SPAN, (b + 2) * SPAN)
            window = slice(b * SPAN, (b + 2) * SPAN)
            raw = lax.dot_general(qv_win[own], key_win[window], NT, preferred_element_type=F32)
            seen = key_place[b] < query_place[0, :, b : b + 1]
            grown_ref[i] = jnp.where(seen, jnp.exp2(raw * score_scale), 0.0)
            gather_rows(addr_ref, coming + i, tokens, rows_in[then].at[i])
        for i in range(SUB):
            b = p * SUB + i
            window = slice(b * SPAN, (b + 2) * SPAN)
            grown = grown_ref[i]
            mixed = jnp.dot(
                grown.astype(BF16),
                jnp.concatenate([qv_win[window], ones], axis=1),
                preferred_element_type=F32,
            )
            sums = mixed[:, LANES:]
            recip = 1.0 / sums
            prob_ref[b] = (grown * jnp.concatenate([recip, recip], axis=1)).astype(BF16)
            signed = sums * sign_ref[0, :, b : b + 1]
            rest = signed - signed.astype(BF16).astype(F32)
            rows_out[now][i] = jnp.where(
                low, jnp.where(first, signed, rest), mixed[:, :LANES] * recip
            )
            scatter_rows(addr_ref, gone + i, rows_out[then].at[i], result)

    qv_ref[...] = qv_win[SPAN:]
    key_ref[...] = key_win[SPAN:]
    qv_win[:SPAN] = qv_win[GROUP * SPAN :]
    key_win[:SPAN] = key_win[GROUP * SPAN :]

    @pl.when(step == last)
    def _():
        for i in range(SUB):
            scatter_rows(addr_ref, blocks - SUB + i, out_odd.at[i], result)
        home_ref[...] = result[:half, :].astype(BF16)
        away_ref[...] = result[half:, :].astype(BF16)


def forward(addr, mine, other, key_place, query_place, sign):
    half = mine.shape[0] * (mine.shape[1] - 16)
    total = 2 * half
    blocks = total // SPAN
    rows = GROUP * SPAN
    return pl.pallas_call(
        forward_kernel,
        grid=(blocks // GROUP,),
        out_shape=[
            jax.ShapeDtypeStruct((half, LANES), BF16),
            jax.ShapeDtypeStruct((half, LANES), BF16),
            jax.ShapeDtypeStruct((blocks, SPAN, 2 * SPAN), BF16),
            jax.ShapeDtypeStruct((total, LANES), BF16),
            jax.ShapeDtypeStruct((total, LANES), BF16),
        ],
        in_specs=[
            whole(pltpu.SMEM),
            fixed(mine.shape),
            fixed(mine.shape),
            pl.BlockSpec((GROUP, 1, 2 * SPAN), lambda g: (g, 0, 0)),
            pl.BlockSpec((1, SPAN, GROUP), lambda g: (g, 0, 0)),
            pl.BlockSpec((1, SPAN, GROUP), lambda g: (g, 0, 0)),
        ],
        out_specs=[
            fixed((half, LANES)),
            fixed((half, LANES)),
            pl.BlockSpec((GROUP, SPAN, 2 * SPAN), lambda g: (g, 0, 0)),
            pl.BlockSpec((rows, LANES), lambda g: (g, 0)),
            pl.BlockSpec((rows, LANES), lambda g: (g, 0)),
        ],
        scratch_shapes=[
            pltpu.VMEM((total, LANES), F32),
            pltpu.VMEM((total, LANES), F32),
            *[pltpu.VMEM((SUB, SPAN, LANES), F32)] * 4,
            pltpu.VMEM((SUB, SPAN, 2 * SPAN), F32),
            pltpu.VMEM((rows + SPAN, LANES), BF16),
            pltpu.VMEM((rows + SPAN, LANES), BF16),
        ],
        compiler_params=pltpu.CompilerParams(vmem_limit_bytes=22 * MIB),
        cost_estimate=pl.CostEstimate(flops=0, bytes_accessed=64 * MIB, transcendentals=0),
        name="span_forward",
    )(addr, mine, other, key_place, query_place, sign)


def share_of(own, peer):
    row = lax.broadcasted_iota(jnp.int32, (LANES, LANES), 0)
    pick = (row < 2).astype(BF16)
    own_sum = jnp.dot(own, pick, preferred_element_type=F32)
    peer_sum = jnp.dot(peer, pick, preferred_element_type=F32)
    both = own_sum / (own_sum + peer_sum)
    own_alone = own_sum < 0.0
    peer_alone = peer_sum < 0.0
    return jnp.where(
        own_alone, jnp.where(peer_alone, both, 0.0), jnp.where(peer_alone, 1.0, both)
    )


def combined_rows(own, peer, share):
    high = lane_of(own.shape) >= DH
    own = own.astype(F32)
    peer = peer.astype(F32)
    return jnp.where(high, share * own + (1.0 - share) * peer, 0.0)


def mix_attention_kernel(own_ref, peer_ref, att_ref):
    half = own_ref.shape[0] // 2
    own = own_ref[...]
    peer = peer_ref[...]
    combined = combined_rows(own, peer, share_of(own, peer))
    att_ref[0] = (pltpu.roll(combined[:half], DH, 1) + combined[half:]).astype(BF16)


def mix_grad_kernel(own_ref, peer_ref, grad_ref, grad_own, grad_peer):
    own = own_ref[...]
    peer = peer_ref[...]
    share = share_of(own, peer)
    combined = combined_rows(own, peer, share)
    packed = grad_ref[0].astype(F32)
    grad = jnp.concatenate([pltpu.roll(packed, DH, 1), packed], axis=0)
    inner = split_sum(grad * combined, jnp.ones((LANES, LANES), BF16))
    lane = lane_of(grad.shape)
    for mix, out in ((share, grad_own), (1.0 - share, grad_peer)):
        delta = -(mix * inner)
        rest = delta - delta.astype(BF16).astype(F32)
        tail = jnp.where(lane == 0, delta, jnp.where(lane == 1, rest, 0.0))
        out[...] = jnp.where(lane < DH, tail, mix * grad).astype(BF16)


def mixing(home, peer, grad=None):
    half = peer.shape[0]
    pieces = lax.axis_size("seq")
    rows = half // pieces
    by_rows = pl.BlockSpec((rows, LANES), lambda g: (g, 0))
    packed = pl.BlockSpec((1, rows // 2, LANES), lambda g: (g, 0, 0))
    cost = pl.CostEstimate(flops=0, bytes_accessed=10 * MIB, transcendentals=0)
    if grad is None:
        return pl.pallas_call(
            mix_attention_kernel,
            grid=(pieces,),
            out_shape=jax.ShapeDtypeStruct((pieces, rows // 2, LANES), BF16),
            in_specs=[by_rows, by_rows],
            out_specs=packed,
            cost_estimate=cost,
            name="mix_attention",
        )(home, peer)
    return pl.pallas_call(
        mix_grad_kernel,
        grid=(pieces,),
        out_shape=[jax.ShapeDtypeStruct((half, LANES), BF16)] * 2,
        in_specs=[by_rows, by_rows, packed],
        out_specs=[by_rows, by_rows],
        cost_estimate=cost,
        name="mix_grad",
    )(home, peer, grad)


def pack_kernel(query_ref, value_ref, slot_ref, out_ref):
    rounds, heads, rows = slot_ref.shape
    half = rows // 2
    for h in range(heads):
        columns = slice(h * DH, (h + 1) * DH)
        pair = jnp.concatenate([query_ref[:, columns], value_ref[:, columns]], axis=1)
        for r in range(rounds):
            out_ref[2 * h + r, :half] = pair[r * half : (r + 1) * half]
            slots = slot_ref[r, h : h + 1, :]
            high = slots // LANES
            parts = [high, slots - high * LANES]
            lines = [p[:, j : j + LANES] for p in parts for j in range(0, rows, LANES)]
            out_ref[2 * h + r, half:] = jnp.concatenate(lines, axis=0).astype(F32).astype(BF16)


def pack_heads(queries, values, slots):
    rounds, heads, rows = slots.shape
    return pl.pallas_call(
        pack_kernel,
        out_shape=jax.ShapeDtypeStruct((rounds * heads, rows // 2 + 16, 2 * DH), BF16),
        compiler_params=pltpu.CompilerParams(vmem_limit_bytes=10 * MIB),
        name="pack_heads",
    )(queries, values, slots)


def unpack_kernel(in_ref, query_ref, value_ref):
    for h in range(in_ref.shape[0]):
        columns = slice(h * DH, (h + 1) * DH)
        query_ref[:, columns] = in_ref[h, :, :DH]
        value_ref[:, columns] = in_ref[h, :, DH:]


def unpack_heads(rows):
    heads, count, _ = rows.shape
    return pl.pallas_call(
        unpack_kernel,
        out_shape=[jax.ShapeDtypeStruct((count, heads * DH), BF16)] * 2,
        name="unpack_heads",
    )(rows)


def member(step, groups):
    return lax.rem(lax.axis_index("head") + (groups - step), groups)


def columns_of(index, width):
    return pl.ds(pl.multiple_of(index * width, width), width)


def members(refs, groups):
    place = lax.axis_index("head")
    own, ups, downs = refs[0], refs[1:groups], refs[groups:]
    out = [own[...]]
    for k in range(1, groups):
        out.append(jnp.where(place >= k, ups[k - 1][...], downs[groups - k - 1][...]))
    return out


def back_kernel(weight_ref, *refs):
    *grads, out_ref = refs
    groups = (len(grads) + 1) // 2
    grads = members(grads, groups)
    rows, width = grads[0].shape
    total = 0.0
    for k in range(groups):
        weight = weight_ref[:, columns_of(member(k, groups), width)]
        total += lax.dot_general(grads[k], weight, NT, preferred_element_type=F32)
    total = total.astype(BF16)
    quarter = rows // 4
    for h in range(width // DH):
        columns = slice(h * DH, (h + 1) * DH)
        for c in range(2):
            first = total[2 * c * quarter : (2 * c + 1) * quarter, columns]
            second = total[(2 * c + 1) * quarter : (2 * c + 2) * quarter, columns]
            out_ref[2 * h + c] = jnp.concatenate([first, second], axis=1)


def back_projection(weight, grads):
    rows, width = grads[0].shape
    return pl.pallas_call(
        back_kernel,
        out_shape=jax.ShapeDtypeStruct((2 * width // DH, rows // 4, 2 * DH), BF16),
        compiler_params=pltpu.CompilerParams(vmem_limit_bytes=10 * MIB),
        name="back_projection",
    )(weight, *grads)


def project_kernel(weight_ref, packed_ref, att_ref, *outs):
    groups = len(outs) // 2
    rows, width = att_ref.shape
    quarter = rows // 4
    for h in range(width // DH):
        columns = slice(h * DH, (h + 1) * DH)
        for c in range(2):
            packed = packed_ref[2 * h + c]
            att_ref[2 * c * quarter : (2 * c + 1) * quarter, columns] = packed[:, :DH]
            att_ref[(2 * c + 1) * quarter : (2 * c + 2) * quarter, columns] = packed[:, DH:]
    for k in range(groups):
        weight = weight_ref[:, columns_of(member(groups - k, groups), width)]
        for c in range(2):
            part = att_ref[2 * c * quarter : 2 * (c + 1) * quarter]
            outs[2 * k + c][...] = jnp.dot(part, weight, preferred_element_type=F32).astype(BF16)


def project(weight, packed):
    count, quarter, _ = packed.shape
    rows, width = 4 * quarter, count * DH // 2
    groups = weight.shape[1] // width
    return pl.pallas_call(
        project_kernel,
        out_shape=[jax.ShapeDtypeStruct((rows, width), BF16)]
        + [jax.ShapeDtypeStruct((rows // 2, width), BF16)] * (2 * groups),
        compiler_params=pltpu.CompilerParams(vmem_limit_bytes=10 * MIB),
        name="project",
    )(weight, packed)


def weight_grad_kernel(att_ref, *refs):
    *grads, keep_ref, give_ref = refs
    groups = (len(grads) + 1) // 2
    grads = members(grads, groups)
    width = grads[0].shape[1]
    part = keep_ref.shape[0]
    core = lax.rem(lax.axis_index("seq"), 2)
    for index, out_ref in ((core, keep_ref), (1 - core, give_ref)):
        att = att_ref[:, columns_of(index, part)]
        for k in range(groups):
            out_ref[:, columns_of(member(k, groups), width)] = lax.dot_general(
                att, grads[k], TN, preferred_element_type=F32
            ).astype(BF16)


def weight_grad(att, grads):
    width = att.shape[1]
    groups = (len(grads) + 1) // 2
    return pl.pallas_call(
        weight_grad_kernel,
        out_shape=[jax.ShapeDtypeStruct((width // 2, width * groups), BF16)] * 2,
        compiler_params=pltpu.CompilerParams(vmem_limit_bytes=10 * MIB),
        name="weight_grad",
    )(att, *grads)


def finished_rows(rows, query_part, key_value):
    low = lane_of(rows.shape) < DH
    scale = DH ** (-0.5)
    query = jnp.where(low, rows.astype(F32), 0.0)
    inverse = inverse_of(query)
    key = query * inverse
    term = key_value * (inverse * scale)
    along = split_sum(key * term, low_lanes(1.0 / DH))
    return jnp.where(low, query_part * scale + term - key * along, key_value)


def backward_kernel(
    addr_ref, mine_ref, other_ref, prob_ref, qv_ref, qv_before, key_ref, key_before,
    home_ref, away_ref,
    tokens, result, in_even, in_odd, out_even, out_odd, qv_win, key_win, tall, sums, query_sums,
    first_sums,
):
    step = pl.program_id(0)
    last = pl.num_programs(0) - 1
    half = mine_ref.shape[0]
    blocks = 2 * half // SPAN
    rows_in = (in_even, in_odd)
    rows_out = (out_even, out_odd)

    @pl.when(step == 0)
    def _():
        tokens[:half, :] = mine_ref[...].astype(F32)
        tokens[half:, :] = other_ref[...].astype(F32)
        for b in range(SUB):
            gather_rows(addr_ref, b, tokens, in_even.at[b])

    qv_win[:SPAN] = qv_before[...]
    qv_win[SPAN:] = qv_ref[...]
    key_win[:SPAN] = key_before[...]
    key_win[SPAN:] = key_ref[...]
    low = lane_of((SPAN, LANES)) < DH
    zero = jnp.zeros((SPAN, LANES), BF16)
    for p in range(GROUP // SUB):
        here = step * GROUP + p * SUB
        coming = jnp.minimum(here + SUB, blocks - SUB)
        gone = here + (blocks - SUB - 1)
        now, then = p % 2, 1 - p % 2
        spans = slice(p * SUB * SPAN, ((p + 1) * SUB + 1) * SPAN)
        everything = qv_win[spans]
        high = lane_of(everything.shape) >= DH
        value_one = jnp.where(high, everything, jnp.ones_like(everything))
        for i in range(SUB):
            b = p * SUB + i
            prob = prob_ref[b]
            dot_grad = lax.dot_general(
                rows_in[now][i].astype(BF16),
                value_one[i * SPAN : (i + 2) * SPAN],
                NT,
                preferred_element_type=F32,
            )
            tall[i, :SPAN] = (prob.astype(F32) * dot_grad).astype(BF16)
            tall[i, SPAN:] = prob
            gather_rows(addr_ref, coming + i, tokens, rows_in[then].at[i])
        for i in range(SUB):
            b = p * SUB + i
            own = slice((b + 1) * SPAN, (b + 2) * SPAN)
            window = slice(b * SPAN, (b + 2) * SPAN)
            query_sums[own] = jnp.dot(
                tall[i, :SPAN], key_win[window], preferred_element_type=F32
            )
            grad_high = jnp.where(low, 0.0, rows_in[now][i]).astype(BF16)
            key_value = lax.dot_general(
                tall[i],
                jnp.concatenate([jnp.where(low, qv_win[own], zero), grad_high], axis=0),
                TN,
                preferred_element_type=F32,
            )
            if b == 0:

                @pl.when(step == 0)
                def _():
                    first_sums[...] = key_value[:SPAN]

            sums[b * SPAN : (b + 1) * SPAN] += key_value[:SPAN]
            sums[own] = key_value[SPAN:]
            scatter_rows(addr_ref, lax.rem(gone + i, blocks), rows_out[then].at[i], result)
        spans = slice(p * SUB * SPAN, (p + 1) * SUB * SPAN)
        finished = finished_rows(qv_win[spans], query_sums[spans], sums[spans])
        rows_out[now][...] = finished.reshape(SUB, SPAN, LANES)
    sums[:SPAN] = sums[GROUP * SPAN :]
    query_sums[:SPAN] = query_sums[GROUP * SPAN :]

    @pl.when(step == last)
    def _():
        for i in range(SUB):
            scatter_rows(addr_ref, blocks - SUB - 1 + i, out_odd.at[i], result)
        out_even[0] = finished_rows(
            qv_win[GROUP * SPAN :], query_sums[:SPAN], sums[:SPAN] + first_sums[...]
        )
        scatter_rows(addr_ref, blocks - 1, out_even.at[0], result)
        home_ref[...] = result[:half, :].astype(BF16)
        away_ref[...] = result[half:, :].astype(BF16)


def backward(addr, mine, other, prob, query_key, value_one):
    half = mine.shape[0]
    total = 2 * half
    blocks = total // SPAN
    rows = GROUP * SPAN
    by_rows = pl.BlockSpec((rows, LANES), lambda g: (g, 0))
    before = pl.BlockSpec((SPAN, LANES), lambda g: (lax.rem(g * GROUP + blocks - 1, blocks), 0))
    return pl.pallas_call(
        backward_kernel,
        grid=(blocks // GROUP,),
        out_shape=[jax.ShapeDtypeStruct((half, LANES), BF16)] * 2,
        in_specs=[
            whole(pltpu.SMEM),
            fixed((half, LANES)),
            fixed((half, LANES)),
            pl.BlockSpec((GROUP, SPAN, 2 * SPAN), lambda g: (g, 0, 0)),
            by_rows,
            before,
            by_rows,
            before,
        ],
        out_specs=[fixed((half, LANES))] * 2,
        scratch_shapes=[
            pltpu.VMEM((total, LANES), F32),
            pltpu.VMEM((total, LANES), F32),
            *[pltpu.VMEM((SUB, SPAN, LANES), F32)] * 4,
            pltpu.VMEM((rows + SPAN, LANES), BF16),
            pltpu.VMEM((rows + SPAN, LANES), BF16),
            pltpu.VMEM((SUB, 2 * SPAN, 2 * SPAN), BF16),
            pltpu.VMEM((rows + SPAN, LANES), F32),
            pltpu.VMEM((rows + SPAN, LANES), F32),
            pltpu.VMEM((SPAN, LANES), F32),
        ],
        compiler_params=pltpu.CompilerParams(vmem_limit_bytes=22 * MIB),
        cost_estimate=pl.CostEstimate(flops=0, bytes_accessed=64 * MIB, transcendentals=0),
        name="span_backward",
    )(addr, mine, other, prob, query_key, query_key, value_one, value_one)


def swap(value, distance=1):
    count = lax.axis_size("seq")
    return lax.ppermute(value, "seq", [(i, i ^ distance) for i in range(count)])


def to_all(value):
    return lax.all_to_all(value, "seq", split_axis=0, concat_axis=0, tiled=True)


def rotate(value, step):
    count = lax.axis_size("head")
    return lax.ppermute(value, "head", [(i, (i + step) % count) for i in range(count)])


def step_along(value, step, count, way):
    pairs = [(i, i + 1) for i in range(step - 1, count - 1)]
    if way < 0:
        pairs = [(count - 1 - i, count - 1 - j) for i, j in pairs]
    return lax.ppermute(value, "head", pairs)


def after(values, *earlier):
    return lax.optimization_barrier((values, earlier))[0]


def by_sequence(queries, values, w_out, out_grad, slots):
    rows = queries.shape[0]
    _, heads, _ = slots.shape
    shards = lax.axis_size("seq")
    groups = lax.axis_size("head")
    core = lax.rem(lax.axis_index("seq"), 2)
    total = shards * rows
    half_rows = rows // 2

    packed = pack_heads(queries, values, slots)
    mine = to_all(packed)
    places = find_places(mine)

    ups, downs = [out_grad], [out_grad]
    for k in range(1, groups):
        ups.append(step_along(ups[-1], k, groups, 1))
        downs.append(step_along(downs[-1], k, groups, -1))
        if k == groups - 2:
            mine = after(mine, ups[-1], downs[-1])
    grads = [*ups, *downs[1:]]

    home, away, prob, query_key, value_one = forward(places[0], mine, swap(mine), *places[1:])
    away, *grads = after([away, *grads])
    peer = swap(away)

    grad_half = to_all(back_projection(w_out, grads))
    att_half, grad_half = after([mixing(home, peer), grad_half])
    att_packed = to_all(att_half)
    grad_own, grad_peer = mixing(home, peer, grad_half)
    grad_peer, att_packed = after([grad_peer, att_packed])
    grad_other = swap(grad_peer)

    att, *shares = project(w_out, att_packed)
    early = [rotate(shares[2 * k], k) for k in range(1, groups)]
    weight, give = weight_grad(att, grads)
    got = swap(give)

    own, others = backward(places[0], grad_own, grad_other, prob, query_key, value_one)
    others, got, *early = after([others, got, *early])
    late = after([shares[2 * k + 1] for k in range(1, groups)], own)
    late = [rotate(late[k - 1], k) for k in range(1, groups)]

    summed = (own.astype(F32) + swap(others).astype(F32)).astype(BF16)
    summed = to_all(summed.reshape(shards, half_rows, LANES))
    query_grad, value_grad = unpack_heads(summed.reshape(heads, rows, LANES))

    weight = (weight.astype(F32) + got.astype(F32)).astype(BF16)
    distance = 2
    while distance < shards:
        weight = (weight.astype(F32) + swap(weight, distance).astype(F32)).astype(BF16)
        distance *= 2
    rest = swap(weight)
    weight = jnp.where(
        core == 0,
        jnp.concatenate([weight, rest], axis=0),
        jnp.concatenate([rest, weight], axis=0),
    )
    w_out_grad = weight.astype(F32) * total ** (-0.5)

    output = []
    for c, received in enumerate((early, late)):
        part = shares[c].astype(F32)
        for share in received:
            part = part + share.astype(F32)
        output.append(part.astype(BF16))
    return (jnp.concatenate(output, axis=0), query_grad, value_grad, w_out_grad)


def shifted(value, axis, steps):
    count = lax.axis_size(axis)
    pairs = [(source, (source + steps) % count) for source in range(count)]
    return lax.ppermute(value, axis, pairs)


def with_before(blocks, before):
    earlier = jnp.concatenate([before[:, None], blocks[:, :-1]], axis=1)
    return jnp.concatenate([blocks, earlier], axis=2)


def normalized(query_rows):
    query_float = query_rows.astype(jnp.float32)
    inverse = lax.rsqrt(jnp.mean(query_float * query_float, axis=-1, keepdims=True) + 1e-06)
    return ((query_float * inverse).astype(jnp.bfloat16), query_float, inverse)


def move_wide(matrix, data, form):
    return jnp.einsum(form, matrix, data, preferred_element_type=jnp.float32).astype(jnp.bfloat16)


def move_exact(matrix, data, form):
    return jnp.einsum(form, matrix, data.astype(jnp.float32), precision=lax.Precision.HIGHEST)


def by_span(queries, values, w_out, out_grad, slots):
    row_count = queries.shape[0]
    head_width = DH
    rounds = slots.shape[0]
    head_group = queries.shape[1] // head_width
    batch_size = rounds * head_group
    shards = lax.axis_size("seq")
    my_index = lax.axis_index("seq")
    even_share = row_count // shards
    capacity = even_share * 3 // 2
    slot_total = shards * capacity
    block_count = row_count // SPAN
    score_scale = head_width ** (-0.5)

    def per_head(matrix):
        split_heads = matrix.reshape(row_count, head_group, head_width).transpose(1, 0, 2)
        return jnp.concatenate([split_heads] * rounds, axis=0)

    flat_slot = slots.reshape(batch_size, row_count)
    target = flat_slot // row_count
    local_slot = flat_slot - target * row_count
    onehot_target = (
        target[:, :, None] == jnp.arange(shards, dtype=jnp.int32)[None, None, :]
    ).astype(jnp.int32)
    earlier_count = jnp.sum(jnp.cumsum(onehot_target, axis=1) * onehot_target, axis=2) - 1
    send_spot = target * capacity + earlier_count
    positions = my_index * row_count + jnp.arange(row_count, dtype=jnp.int32)
    position_rows = jnp.broadcast_to(positions[None, :], (batch_size, row_count))
    pack_float = (
        send_spot[:, None, :] == jnp.arange(slot_total, dtype=jnp.int32)[None, :, None]
    ).astype(jnp.float32)
    pack_half = pack_float.astype(jnp.bfloat16)
    full_grad = lax.all_gather(out_grad, "head", axis=1, tiled=True)
    back_attn = lax.dot_general(
        full_grad, w_out, (((1,), (1,)), ((), ())), preferred_element_type=jnp.float32
    ).astype(jnp.bfloat16)
    query_value = jnp.concatenate([per_head(queries), per_head(values)], axis=2)
    packed_rows = move_wide(pack_half, query_value, "bsr,brd->bsd").reshape(
        batch_size, shards, capacity, 2 * head_width
    )
    packed_place = (
        move_exact(pack_float, position_rows, "bsr,br->bs")
        .astype(jnp.int32)
        .reshape(batch_size, shards, capacity)
    )
    packed_slot = (
        move_exact(pack_float, local_slot + 1, "bsr,br->bs")
        .astype(jnp.int32)
        .reshape(batch_size, shards, capacity)
    )
    got_rows, got_place, got_slot = (
        lax.all_to_all(packed_rows, "seq", split_axis=1, concat_axis=1, tiled=True),
        lax.all_to_all(packed_place, "seq", split_axis=1, concat_axis=1, tiled=True),
        lax.all_to_all(packed_slot, "seq", split_axis=1, concat_axis=1, tiled=True),
    )
    got_spot = got_slot.reshape(batch_size, slot_total)
    got_spot = jnp.where(got_spot == 0, row_count, got_spot - 1)
    sort_float = (
        got_spot[:, :, None] == jnp.arange(row_count, dtype=jnp.int32)[None, None, :]
    ).astype(jnp.float32)
    sort_half = sort_float.astype(jnp.bfloat16)
    sorted_rows = move_wide(
        sort_half, got_rows.reshape(batch_size, slot_total, 2 * head_width), "bsr,bsd->brd"
    )
    sorted_place = move_exact(
        sort_float, got_place.reshape(batch_size, slot_total), "bsr,bs->br"
    ).astype(jnp.int32)
    last_rows = sorted_rows[:, row_count - SPAN :]
    last_place = sorted_place[:, row_count - SPAN :]
    before_rows, before_place = shifted((last_rows, last_place), "seq", 1)
    sorted_query = sorted_rows[:, :, :head_width]
    sorted_value = sorted_rows[:, :, head_width:]
    sorted_key, query_float, inverse = normalized(sorted_query)
    before_key = normalized(before_rows[:, :, :head_width])[0]
    query_blocks = sorted_query.reshape(batch_size, block_count, SPAN, head_width)
    key_window = with_before(
        sorted_key.reshape(batch_size, block_count, SPAN, head_width), before_key
    )
    value_window = with_before(
        sorted_value.reshape(batch_size, block_count, SPAN, head_width),
        before_rows[:, :, head_width:],
    )
    place_blocks = sorted_place.reshape(batch_size, block_count, SPAN)
    place_window = with_before(place_blocks, before_place)
    own_token = (jnp.arange(SPAN)[:, None] == jnp.arange(2 * SPAN)[None, :]).astype(jnp.float32)
    future = (place_window[:, :, None, :] > place_blocks[:, :, :, None]).astype(jnp.float32)

    def score_of():
        raw_scores = (
            jnp.einsum(
                "bcqd,bckd->bcqk", query_blocks, key_window, preferred_element_type=jnp.float32
            )
            * score_scale
        )
        return raw_scores - 100000.0 * own_token - 1000000000.0 * future

    scores = score_of()
    row_top = jnp.max(scores, axis=-1)
    log_total = row_top + jnp.log(jnp.sum(jnp.exp(scores - row_top[..., None]), axis=-1))
    weights = jnp.exp(scores - log_total[..., None])
    rounded_probs = weights.astype(jnp.bfloat16)
    block_out = jnp.einsum(
        "bcqk,bckd->bcqd", rounded_probs, value_window, preferred_element_type=jnp.float32
    ).astype(jnp.bfloat16)
    out_rows = block_out.reshape(batch_size, row_count, head_width)
    home_out = move_wide(sort_half, out_rows, "bsr,brd->bsd").reshape(
        batch_size, shards, capacity // 2, 2 * head_width
    )
    home_log = move_exact(
        sort_float, log_total.reshape(batch_size, row_count), "bsr,br->bs"
    ).reshape(batch_size, shards, capacity)
    back_out, back_log = (
        lax.all_to_all(home_out, "seq", split_axis=1, concat_axis=1, tiled=True),
        lax.all_to_all(
            home_log.astype(jnp.bfloat16), "seq", split_axis=1, concat_axis=1, tiled=True
        ).astype(home_log.dtype),
    )
    round_out = move_wide(
        pack_half, back_out.reshape(batch_size, slot_total, head_width), "bsr,bsd->brd"
    ).reshape(rounds, head_group, row_count, head_width)
    round_log = move_exact(
        pack_float, back_log.reshape(batch_size, slot_total), "bsr,bs->br"
    ).reshape(rounds, head_group, row_count)
    mixing = jax.nn.softmax(round_log, axis=0)
    combined = jnp.sum(mixing[..., None] * round_out.astype(jnp.float32), axis=0)
    attention = (
        combined.astype(jnp.bfloat16).transpose(1, 0, 2).reshape(row_count, head_group * head_width)
    )
    head_term = jnp.dot(attention, w_out, preferred_element_type=jnp.float32)
    output = lax.psum_scatter(
        head_term.astype(jnp.bfloat16), "head", scatter_dimension=1, tiled=True
    )
    weight_term = lax.dot_general(
        attention, full_grad, (((0,), (0,)), ((), ())), preferred_element_type=jnp.float32
    )
    w_out_grad = lax.psum(weight_term.astype(jnp.bfloat16), "seq").astype(jnp.float32) * (
        shards * row_count
    ) ** (-0.5)
    back_heads = (
        back_attn.reshape(row_count, head_group, head_width).transpose(1, 0, 2).astype(jnp.float32)
    )
    inner_rows = jnp.sum(back_heads * combined, axis=-1)
    delta_rows = (mixing * inner_rows[None]).reshape(batch_size, row_count)
    grad_rows = (
        (mixing[..., None] * back_heads[None])
        .astype(jnp.bfloat16)
        .reshape(batch_size, row_count, head_width)
    )
    packed_grad = move_wide(pack_half, grad_rows, "bsr,brd->bsd").reshape(
        batch_size, shards, capacity // 2, 2 * head_width
    )
    packed_delta = move_exact(pack_float, delta_rows, "bsr,br->bs").reshape(
        batch_size, shards, capacity
    )
    got_grad, got_delta = (
        lax.all_to_all(packed_grad, "seq", split_axis=1, concat_axis=1, tiled=True),
        lax.all_to_all(
            packed_delta.astype(jnp.bfloat16), "seq", split_axis=1, concat_axis=1, tiled=True
        ).astype(packed_delta.dtype),
    )
    sorted_grad = move_wide(
        sort_half, got_grad.reshape(batch_size, slot_total, head_width), "bsr,bsd->brd"
    )
    sorted_delta = move_exact(sort_float, got_delta.reshape(batch_size, slot_total), "bsr,bs->br")
    kept_weights = jnp.exp(score_of() - log_total[..., None])
    grad_blocks = sorted_grad.reshape(batch_size, block_count, SPAN, head_width)
    delta_blocks = sorted_delta.reshape(batch_size, block_count, SPAN)
    dot_grad = jnp.einsum(
        "bcqd,bckd->bcqk", grad_blocks, value_window, preferred_element_type=jnp.float32
    )
    score_grad = (kept_weights * (dot_grad - delta_blocks[..., None])).astype(jnp.bfloat16)
    query_part = (
        jnp.einsum("bcqk,bckd->bcqd", score_grad, key_window, preferred_element_type=jnp.float32)
        * score_scale
    )
    key_part = (
        jnp.einsum("bcqk,bcqd->bckd", score_grad, query_blocks, preferred_element_type=jnp.float32)
        * score_scale
    )
    value_part = jnp.einsum(
        "bcqk,bcqd->bckd", rounded_probs, grad_blocks, preferred_element_type=jnp.float32
    )
    spill_rows = jnp.concatenate([key_part[:, 0, SPAN:], value_part[:, 0, SPAN:]], axis=2)
    arrived = shifted(spill_rows.astype(jnp.bfloat16), "seq", -1).astype(spill_rows.dtype)
    key_grad = key_part[:, :, :SPAN] + jnp.concatenate(
        [key_part[:, 1:, SPAN:], arrived[:, None, :, :head_width]], axis=1
    )
    value_sum = value_part[:, :, :SPAN] + jnp.concatenate(
        [value_part[:, 1:, SPAN:], arrived[:, None, :, head_width:]], axis=1
    )
    key_grad = key_grad.reshape(batch_size, row_count, head_width)
    value_sum = value_sum.reshape(batch_size, row_count, head_width)
    query_total = (
        query_part.reshape(batch_size, row_count, head_width)
        + inverse * key_grad
        - query_float
        * (inverse * inverse * inverse)
        * jnp.mean(query_float * key_grad, axis=-1, keepdims=True)
    )
    both_grads = jnp.concatenate(
        [query_total.astype(jnp.bfloat16), value_sum.astype(jnp.bfloat16)], axis=2
    )
    home_grads = move_wide(sort_half, both_grads, "bsr,brd->bsd").reshape(
        batch_size, shards, capacity, 2 * head_width
    )
    back_grads = lax.all_to_all(home_grads, "seq", split_axis=1, concat_axis=1, tiled=True)
    own_grads = move_wide(
        pack_half, back_grads.reshape(batch_size, slot_total, 2 * head_width), "bsr,bsd->brd"
    ).astype(jnp.float32)
    own_grads = own_grads.reshape(rounds, head_group, row_count, 2 * head_width)
    summed = jnp.sum(own_grads, axis=0).astype(jnp.bfloat16)
    query_grad = (
        summed[:, :, :head_width].transpose(1, 0, 2).reshape(row_count, head_group * head_width)
    )
    value_grad = (
        summed[:, :, head_width:].transpose(1, 0, 2).reshape(row_count, head_group * head_width)
    )
    return (output, query_grad, value_grad, w_out_grad)


def per_device(queries, values, w_out, out_grad, slots):
    if lax.axis_size("seq") == slots.shape[0] * slots.shape[1] and slots.shape[0] == 2:
        return by_sequence(queries, values, w_out, out_grad, slots)
    return by_span(queries, values, w_out, out_grad, slots)


def solution(mesh):
    placed = (
        P("seq", "head"),
        P("seq", "head"),
        P("head", None),
        P("seq", "head"),
        P(None, "head", "seq"),
    )
    return jax.shard_map(
        per_device,
        mesh=mesh,
        in_specs=placed,
        out_specs=(P("seq", "head"), P("seq", "head"), P("seq", "head"), P("head", None)),
        check_vma=False,
    )
```

profile of v0, /device:TPU:0, one launch (start us, length us, event | category | flops | bytes accessed | tf_op | source)
XLA Modules:
  0.0 173.2 jit_solution(4236726809890787039)
XLA Ops:
  0.6 5.0 %collective-permute-start = (bf16[1024,256]{1,0:T(8,128)(2,1)}, bf16[1024,256]{1,0:T(8,128)(2,1)S(1)}, u32[]{:S(2)}, u32[]{:S(2)}) collective-permute-start(bf16[1024,256]{1,0:T(8,128)(2,1)} %refs_0_.1), channel_id=1, source_target_pairs={{0,1},{1,2},{2,3},{4,5},{5,6},{6,7},{8,9},{9,10},{10,11},{12,13},{... | collective-permute-start | bytes 1572872 | tf_op jit(solution)/shard_map/ppermute | solution.py:626
  5.6 1.3 collective-permute-start.2
  6.9 1.0 copy-done.20
  7.9 1.0 copy-done.21
  9.7 1.4 pack_heads.1
  11.1 3.7 %all-to-all-start = ((bf16[8,528,128]{2,1,0:T(8,128)(2,1)}), bf16[8,528,128]{2,1,0:T(8,128)(2,1)S(1)}, u32[]{:S(2)}, u32[]{:S(2)}) async-start(bf16[8,528,128]{2,1,0:T(8,128)(2,1)} %pack_heads.1), calls=%async_computation | async-start | bytes 2162688 | tf_op jit(solution)/shard_map/all_to_all | solution.py:614
  14.9 2.2 %collective-permute-done.refs_1_ = bf16[1024,256]{1,0:T(8,128)(2,1)S(1)} collective-permute-done((bf16[1024,256]{1,0:T(8,128)(2,1)}, bf16[1024,256]{1,0:T(8,128)(2,1)S(1)}, u32[]{:S(2)}, u32[]{:S(2)}) %collective-permute-start) | collective-permute-done | bytes 524320 | tf_op jit(solution)/shard_map/ppermute | solution.py:626
  17.1 1.5 collective-permute-start.1
  18.5 2.6 %collective-permute-done.2.refs_4_ = bf16[1024,256]{1,0:T(8,128)(2,1)S(1)} collective-permute-done((bf16[1024,256]{1,0:T(8,128)(2,1)}, bf16[1024,256]{1,0:T(8,128)(2,1)S(1)}, u32[]{:S(2)}, u32[]{:S(2)}) %collective-permute-start.2) | collective-permute-done | bytes 524320 | tf_op jit(solution)/shard_map/ppermute | solution.py:626
  21.1 1.3 collective-permute-start.3
  22.4 8.2 %all-to-all-done.mine_ref = bf16[8,528,128]{2,1,0:T(8,128)(2,1)S(1)} async-done(((bf16[8,528,128]{2,1,0:T(8,128)(2,1)}), bf16[8,528,128]{2,1,0:T(8,128)(2,1)S(1)}, u32[]{:S(2)}, u32[]{:S(2)}) %all-to-all-start) | async-done | bytes 1081376 | tf_op jit(solution)/shard_map/all_to_all | solution.py:614
  30.6 5.9 %collective-permute-done.3.refs_5_ = bf16[1024,256]{1,0:T(8,128)(2,1)} collective-permute-done((bf16[1024,256]{1,0:T(8,128)(2,1)S(1)}, bf16[1024,256]{1,0:T(8,128)(2,1)}, u32[]{:S(2)}, u32[]{:S(2)}) %collective-permute-start.3) | collective-permute-done | bytes 524320 | tf_op jit(solution)/shard_map/ppermute | solution.py:626
  37.2 1.3 collective-permute-start.6
  38.5 1.2 find_places.1
  39.7 21.4 %span_forward.1 = (bf16[4096,128]{1,0:T(8,128)(2,1)S(1)}, bf16[4096,128]{1,0:T(8,128)(2,1)}, bf16[64,128,256]{2,1,0:T(8,128)(2,1)S(1)}, bf16[8192,128]{1,0:T(8,128)(2,1)S(1)}, bf16[8192,128]{1,0:T(8,128)(2,1)S(1)}) custom-call(s32[64,128]{1,0:T(8,128)S(1)} %get-tuple-element.51.addr_ref, bf16[8,528,128]{2,1,0:T(8,128)(2,1)S(1)} %all-to-all-done.mine_ref, ...), custom_call_target="tpu_custom_call" | custom-call | bytes 67108864 | tf_op jit(solution)/shard_map/span_forward/pallas_call | solution.py:216
  61.1 1.4 copy-done
  62.5 2.0 %copy-done.2 = bf16[64,128,256]{2,1,0:T(8,128)(2,1)} copy-done((bf16[64,128,256]{2,1,0:T(8,128)(2,1)}, bf16[64,128,256]{2,1,0:T(8,128)(2,1)S(1)}, u32[]{:S(2)}) %copy-start.2) | copy-done | bytes 4194328
  66.0 1.0 copy-done.5
  67.0 1.0 copy-done.7
  68.0 2.8 %back_projection.1 = bf16[8,256,128]{2,1,0:T(8,128)(2,1)} custom-call(bf16[256,1024]{1,0:T(8,128)(2,1)S(1)} %copy-done.5, bf16[1024,256]{1,0:T(8,128)(2,1)S(1)} %copy-done.7, bf16[1024,256]{1,0:T(8,128)(2,1)S(1)} %copy-done.10, bf16[1024,256]{1,0:T(8,128)(2,1)} %collective-permute-done.1.refs_2_, bf16[1024,256]{1,0:T(8,128)(2,1)S(1)} %collective-permute-done.5.refs_3_, ...), custom_call_target="tpu_custom_call" | custom-call | tf_op jit(solution)/shard_map/back_projection/pallas_call | solution.py:406
  72.4 4.1 %all-to-all-start.1 = ((bf16[8,256,128]{2,1,0:T(8,128)(2,1)}), bf16[8,256,128]{2,1,0:T(8,128)(2,1)}, u32[]{:S(2)}, u32[]{:S(2)}) async-start(bf16[8,256,128]{2,1,0:T(8,128)(2,1)} %back_projection.1), calls=%async_computation.1 | async-start | bytes 1048576 | tf_op jit(solution)/shard_map/all_to_all | solution.py:614
  77.5 6.4 %mix_attention.1 = bf16[8,256,128]{2,1,0:T(8,128)(2,1)} custom-call(bf16[4096,128]{1,0:T(8,128)(2,1)} %copy-done.4, bf16[4096,128]{1,0:T(8,128)(2,1)} %copy-done.29), custom_call_target="tpu_custom_call" | custom-call | bytes 10485760 | tf_op jit(solution)/shard_map/mix_attention/pallas_call | solution.py:307
  83.9 2.4 %all-to-all-done.1.grad_ref = bf16[8,256,128]{2,1,0:T(8,128)(2,1)} async-done(((bf16[8,256,128]{2,1,0:T(8,128)(2,1)}), bf16[8,256,128]{2,1,0:T(8,128)(2,1)}, u32[]{:S(2)}, u32[]{:S(2)}) %all-to-all-start.1) | async-done | bytes 524320 | tf_op jit(solution)/shard_map/all_to_all | solution.py:614
  86.3 3.5 %all-to-all-start.2 = ((bf16[8,256,128]{2,1,0:T(8,128)(2,1)}), bf16[8,256,128]{2,1,0:T(8,128)(2,1)S(1)}, u32[]{:S(2)}, u32[]{:S(2)}) async-start(bf16[8,256,128]{2,1,0:T(8,128)(2,1)} %mix_attention.1), calls=%async_computation.2 | async-start | bytes 1048576 | tf_op jit(solution)/shard_map/all_to_all | solution.py:614
  89.8 7.5 %mix_grad.1 = (bf16[4096,128]{1,0:T(8,128)(2,1)}, bf16[4096,128]{1,0:T(8,128)(2,1)}) custom-call(bf16[4096,128]{1,0:T(8,128)(2,1)} %copy-done.4, bf16[4096,128]{1,0:T(8,128)(2,1)} %copy-done.29, bf16[8,256,128]{2,1,0:T(8,128)(2,1)} %all-to-all-done.1.grad_ref), custom_call_target="tpu_custom_call" | custom-call | bytes 10485760 | tf_op jit(solution)/shard_map/mix_grad/pallas_call | solution.py:316
  97.3 2.2 %all-to-all-done.2.packed_ref = bf16[8,256,128]{2,1,0:T(8,128)(2,1)S(1)} async-done(((bf16[8,256,128]{2,1,0:T(8,128)(2,1)}), bf16[8,256,128]{2,1,0:T(8,128)(2,1)S(1)}, u32[]{:S(2)}, u32[]{:S(2)}) %all-to-all-start.2) | async-done | bytes 524320 | tf_op jit(solution)/shard_map/all_to_all | solution.py:614
  103.3 1.0 copy-done.8
  104.3 1.0 copy-done.11
  105.3 1.0 copy-done.14
  106.4 1.0 copy-done.16
  107.4 1.0 copy-done.18
  108.5 2.1 %weight_grad.1 = (bf16[128,1024]{1,0:T(8,128)(2,1)S(1)}, bf16[128,1024]{1,0:T(8,128)(2,1)S(1)}) custom-call(bf16[1024,256]{1,0:T(8,128)(2,1)S(1)} %get-tuple-element.77.att_ref, bf16[1024,256]{1,0:T(8,128)(2,1)S(1)} %copy-done.8, bf16[1024,256]{1,0:T(8,128)(2,1)S(1)} %copy-done.11, bf16[1024,256]{1,0:T(8,128)(2,1)} %collective-permute-done.1.refs_2_, ...), custom_call_target="tpu_custom_call" | custom-call | tf_op jit(solution)/shard_map/weight_grad/pallas_call | solution.py:462
  111.2 2.4 %collective-permute-start.10 = (bf16[512,256]{1,0:T(8,128)(2,1)S(1)}, bf16[512,256]{1,0:T(8,128)(2,1)S(1)}, u32[]{:S(2)}, u32[]{:S(2)}) collective-permute-start(bf16[512,256]{1,0:T(8,128)(2,1)S(1)} %get-tuple-element.79), channel_id=1, source_target_pairs={{0,1},{1,2},{2,3},{3,0},{4,5},{5,6},{6,7},{7,4},{8,9},{9,10},{10,1... | collective-permute-start | bytes 786440 | tf_op jit(solution)/shard_map/ppermute | solution.py:619
  113.5 2.4 %collective-permute-start.12 = (bf16[512,256]{1,0:T(8,128)(2,1)S(1)}, bf16[512,256]{1,0:T(8,128)(2,1)S(1)}, u32[]{:S(2)}, u32[]{:S(2)}) collective-permute-start(bf16[512,256]{1,0:T(8,128)(2,1)S(1)} %get-tuple-element.81), channel_id=1, source_target_pairs={{0,3},{1,0},{2,1},{3,2},{4,7},{5,4},{6,5},{7,6},{8,11},{9,8},{10,9... | collective-permute-start | bytes 786440 | tf_op jit(solution)/shard_map/ppermute | solution.py:619
  115.9 2.2 %copy-done.3 = bf16[64,128,256]{2,1,0:T(8,128)(2,1)S(1)} copy-done((bf16[64,128,256]{2,1,0:T(8,128)(2,1)S(1)}, bf16[64,128,256]{2,1,0:T(8,128)(2,1)}, u32[]{:S(2)}) %copy-start.3) | copy-done | bytes 4194328
  118.1 21.5 %span_backward.1 = (bf16[4096,128]{1,0:T(8,128)(2,1)S(1)}, bf16[4096,128]{1,0:T(8,128)(2,1)}) custom-call(s32[64,128]{1,0:T(8,128)S(1)} %get-tuple-element.51.addr_ref, bf16[4096,128]{1,0:T(8,128)(2,1)S(1)} %copy-done.19, bf16[4096,128]{1,0:T(8,128)(2,1)S(1)} %collective-permute-done.8.other_ref, bf16[64,128,256]{2,1,0:T(8,128)(2,1)S(1)} %copy-done.3, ...), custom_call_target="tpu_custom_call" | custom-call | bytes 67108864 | tf_op jit(solution)/shard_map/span_backward/pallas_call | solution.py:576
  140.9 2.6 %collective-permute-start.14 = (bf16[512,256]{1,0:T(8,128)(2,1)}, bf16[512,256]{1,0:T(8,128)(2,1)}, u32[]{:S(2)}, u32[]{:S(2)}) collective-permute-start(bf16[512,256]{1,0:T(8,128)(2,1)} %copy-done.26), channel_id=1, source_target_pairs={{0,2},{1,3},{2,0},{3,1},{4,6},{5,7},{6,4},{7,5},{8,10},{9,11},{10,... | collective-permute-start | bytes 786440 | tf_op jit(solution)/shard_map/ppermute | solution.py:619
  143.5 1.4 collective-permute-start.15
  144.9 3.7 %collective-permute-done.17 = bf16[128,1024]{1,0:T(8,128)(2,1)S(1)} collective-permute-done((bf16[128,1024]{1,0:T(8,128)(2,1)S(1)}, bf16[128,1024]{1,0:T(8,128)(2,1)S(1)}, u32[]{:S(2)}, u32[]{:S(2)}) %collective-permute-start.17) | collective-permute-done | bytes 262176 | tf_op jit(solution)/shard_map/ppermute | solution.py:610
  149.3 1.3 add_convert_fusion
  150.6 3.6 %all-to-all-start.3 = ((bf16[8,512,128]{2,1,0:T(8,128)(2,1)}), bf16[8,512,128]{2,1,0:T(8,128)(2,1)S(1)}, u32[]{:S(2)}, u32[]{:S(2)}) async-start(bf16[8,512,128]{2,1,0:T(8,128)(2,1)} %bitcast), calls=%async_computation.3 | async-start | bytes 2097152 | tf_op jit(solution)/shard_map/all_to_all | solution.py:614
  154.2 1.1 add_convert_fusion.5
  155.3 1.1 collective-permute-done.18
  157.6 4.8 %collective-permute-done.14 = bf16[512,256]{1,0:T(8,128)(2,1)} collective-permute-done((bf16[512,256]{1,0:T(8,128)(2,1)}, bf16[512,256]{1,0:T(8,128)(2,1)}, u32[]{:S(2)}, u32[]{:S(2)}) %collective-permute-start.14) | collective-permute-done | bytes 262176 | tf_op jit(solution)/shard_map/ppermute | solution.py:619
  162.4 1.2 add_convert_fusion.4
  164.5 1.1 convert_multiply_fusion
  165.6 3.9 %all-to-all-done.3 = bf16[8,512,128]{2,1,0:T(8,128)(2,1)S(1)} async-done(((bf16[8,512,128]{2,1,0:T(8,128)(2,1)}), bf16[8,512,128]{2,1,0:T(8,128)(2,1)S(1)}, u32[]{:S(2)}, u32[]{:S(2)}) %all-to-all-start.3) | async-done | bytes 1048608 | tf_op jit(solution)/shard_map/all_to_all | solution.py:614
  170.6 2.7 %unpack_heads.1 = (bf16[1024,256]{1,0:T(8,128)(2,1)}, bf16[1024,256]{1,0:T(8,128)(2,1)}) custom-call(bf16[4,1024,128]{2,1,0:T(8,128)(2,1)} %bitcast.2), custom_call_target="tpu_custom_call" | custom-call | tf_op jit(solution)/shard_map/unpack_heads/pallas_call | solution.py:361
  (88 shorter events, 14.7 us)
Async XLA Ops:
  0.6 16.4 %collective-permute-start = (bf16[1024,256]{1,0:T(8,128)(2,1)}, bf16[1024,256]{1,0:T(8,128)(2,1)S(1)}, u32[]{:S(2)}, u32[]{:S(2)}) collective-permute-start(bf16[1024,256]{1,0:T(8,128)(2,1)} %refs_0_.1), channel_id=1, source_target_pairs={{0,1},{1,2},{2,3},{4,5},{5,6},{6,7},{8,9},{9,10},{10,11},{12,13},{... | collective-permute-start | bytes 1572872 | tf_op jit(solution)/shard_map/ppermute | solution.py:626
  5.6 15.5 %collective-permute-start.2 = (bf16[1024,256]{1,0:T(8,128)(2,1)}, bf16[1024,256]{1,0:T(8,128)(2,1)S(1)}, u32[]{:S(2)}, u32[]{:S(2)}) collective-permute-start(bf16[1024,256]{1,0:T(8,128)(2,1)} %refs_0_.1), channel_id=1, source_target_pairs={{3,2},{2,1},{1,0},{7,6},{6,5},{5,4},{11,10},{10,9},{9,8},{15,14},{... | collective-permute-start | bytes 1572872 | tf_op jit(solution)/shard_map/ppermute | solution.py:626
  6.9 1.0 copy-start.20
  7.9 1.0 copy-start.21
  11.1 19.5 %all-to-all-start = ((bf16[8,528,128]{2,1,0:T(8,128)(2,1)}), bf16[8,528,128]{2,1,0:T(8,128)(2,1)S(1)}, u32[]{:S(2)}, u32[]{:S(2)}) async-start(bf16[8,528,128]{2,1,0:T(8,128)(2,1)} %pack_heads.1), calls=%async_computation | async-start | bytes 2162688 | tf_op jit(solution)/shard_map/all_to_all | solution.py:614
  17.0 22.7 %copy-start.9 = (bf16[1024,256]{1,0:T(8,128)(2,1)}, bf16[1024,256]{1,0:T(8,128)(2,1)S(1)}, u32[]{:S(2)}) copy-start(bf16[1024,256]{1,0:T(8,128)(2,1)S(1)} %collective-permute-done.refs_1_) | copy-start | bytes 1572868
  17.1 13.6 %collective-permute-start.1 = (bf16[1024,256]{1,0:T(8,128)(2,1)S(1)}, bf16[1024,256]{1,0:T(8,128)(2,1)}, u32[]{:S(2)}, u32[]{:S(2)}) collective-permute-start(bf16[1024,256]{1,0:T(8,128)(2,1)S(1)} %collective-permute-done.refs_1_), channel_id=1, source_target_pairs={{1,2},{2,3},{5,6},{6,7},{9,10},{10,11},{13,14},{14,15},{17,18},{18... | collective-permute-start | bytes 1572872 | tf_op jit(solution)/shard_map/ppermute | solution.py:626
  21.1 18.6 %copy-start.12 = (bf16[1024,256]{1,0:T(8,128)(2,1)}, bf16[1024,256]{1,0:T(8,128)(2,1)S(1)}, u32[]{:S(2)}) copy-start(bf16[1024,256]{1,0:T(8,128)(2,1)S(1)} %collective-permute-done.2.refs_4_) | copy-start | bytes 1572868
  21.1 15.4 %collective-permute-start.3 = (bf16[1024,256]{1,0:T(8,128)(2,1)S(1)}, bf16[1024,256]{1,0:T(8,128)(2,1)}, u32[]{:S(2)}, u32[]{:S(2)}) collective-permute-start(bf16[1024,256]{1,0:T(8,128)(2,1)S(1)} %collective-permute-done.2.refs_4_), channel_id=1, source_target_pairs={{2,1},{1,0},{6,5},{5,4},{10,9},{9,8},{14,13},{13,12},{18,17},{17,1... | collective-permute-start | bytes 1572872 | tf_op jit(solution)/shard_map/ppermute | solution.py:626
  36.5 3.2 %collective-permute-start.4 = (bf16[8,528,128]{2,1,0:T(8,128)(2,1)S(1)}, bf16[8,528,128]{2,1,0:T(8,128)(2,1)S(1)}, u32[]{:S(2)}, u32[]{:S(2)}) collective-permute-start(bf16[8,528,128]{2,1,0:T(8,128)(2,1)S(1)} %all-to-all-done.mine_ref), channel_id=1, source_target_pairs={{0,4},{4,0},{8,12},{12,8},{16,20},{20,16},{24,28},{28,24},{1,5},{5... | collective-permute-start | bytes 3244040 | tf_op jit(solution)/shard_map/ppermute | solution.py:610
  36.5 28.9 %collective-permute-start.5 = (bf16[1024,256]{1,0:T(8,128)(2,1)}, bf16[1024,256]{1,0:T(8,128)(2,1)S(1)}, u32[]{:S(2)}, u32[]{:S(2)}) collective-permute-start(bf16[1024,256]{1,0:T(8,128)(2,1)} %collective-permute-done.1.refs_2_), channel_id=1, source_target_pairs={{2,3},{6,7},{10,11},{14,15},{18,19},{22,23},{26,27},{30,31}} | collective-permute-start | bytes 1572872 | tf_op jit(solution)/shard_map/ppermute | solution.py:626
  37.2 28.2 %collective-permute-start.6 = (bf16[1024,256]{1,0:T(8,128)(2,1)}, bf16[1024,256]{1,0:T(8,128)(2,1)S(1)}, u32[]{:S(2)}, u32[]{:S(2)}) collective-permute-start(bf16[1024,256]{1,0:T(8,128)(2,1)} %collective-permute-done.3.refs_5_), channel_id=1, source_target_pairs={{1,0},{5,4},{9,8},{13,12},{17,16},{21,20},{25,24},{29,28}} | collective-permute-start | bytes 1572872 | tf_op jit(solution)/shard_map/ppermute | solution.py:626
  39.7 26.2 %copy-start.10 = (bf16[1024,256]{1,0:T(8,128)(2,1)S(1)}, bf16[1024,256]{1,0:T(8,128)(2,1)}, u32[]{:S(2)}) copy-start(bf16[1024,256]{1,0:T(8,128)(2,1)} %copy-done.9) | copy-start | bytes 1572868
  39.7 26.2 %copy-start.13 = (bf16[1024,256]{1,0:T(8,128)(2,1)S(1)}, bf16[1024,256]{1,0:T(8,128)(2,1)}, u32[]{:S(2)}) copy-start(bf16[1024,256]{1,0:T(8,128)(2,1)} %copy-done.12) | copy-start | bytes 1572868
  61.1 1.4 copy-start
  62.5 2.0 %copy-start.2 = (bf16[64,128,256]{2,1,0:T(8,128)(2,1)}, bf16[64,128,256]{2,1,0:T(8,128)(2,1)S(1)}, u32[]{:S(2)}) copy-start(bf16[64,128,256]{2,1,0:T(8,128)(2,1)S(1)} %get-tuple-element.73.prob_ref) | copy-start | bytes 12582916
  65.4 11.1 %collective-permute-start.7 = (bf16[4096,128]{1,0:T(8,128)(2,1)}, bf16[4096,128]{1,0:T(8,128)(2,1)S(1)}, u32[]{:S(2)}, u32[]{:S(2)}) collective-permute-start(bf16[4096,128]{1,0:T(8,128)(2,1)} %get-tuple-element.58), channel_id=1, source_target_pairs={{0,4},{4,0},{8,12},{12,8},{16,20},{20,16},{24,28},{28,24},{1,5},{5... | collective-permute-start | bytes 3145736 | tf_op jit(solution)/shard_map/ppermute | solution.py:610
  65.9 1.0 copy-start.5
  67.0 1.0 copy-start.7
  72.4 13.9 %all-to-all-start.1 = ((bf16[8,256,128]{2,1,0:T(8,128)(2,1)}), bf16[8,256,128]{2,1,0:T(8,128)(2,1)}, u32[]{:S(2)}, u32[]{:S(2)}) async-start(bf16[8,256,128]{2,1,0:T(8,128)(2,1)} %back_projection.1), calls=%async_computation.1 | async-start | bytes 1048576 | tf_op jit(solution)/shard_map/all_to_all | solution.py:614
  83.9 15.5 %copy-start.6 = (bf16[256,1024]{1,0:T(8,128)(2,1)S(1)}, bf16[256,1024]{1,0:T(8,128)(2,1)}, u32[]{:S(2)}) copy-start(bf16[256,1024]{1,0:T(8,128)(2,1)} %weight_ref.3) | copy-start | bytes 1572868
  86.3 13.2 %all-to-all-start.2 = ((bf16[8,256,128]{2,1,0:T(8,128)(2,1)}), bf16[8,256,128]{2,1,0:T(8,128)(2,1)S(1)}, u32[]{:S(2)}, u32[]{:S(2)}) async-start(bf16[8,256,128]{2,1,0:T(8,128)(2,1)} %mix_attention.1), calls=%async_computation.2 | async-start | bytes 1048576 | tf_op jit(solution)/shard_map/all_to_all | solution.py:614
  99.5 16.4 %collective-permute-start.8 = (bf16[4096,128]{1,0:T(8,128)(2,1)}, bf16[4096,128]{1,0:T(8,128)(2,1)S(1)}, u32[]{:S(2)}, u32[]{:S(2)}) collective-permute-start(bf16[4096,128]{1,0:T(8,128)(2,1)} %get-tuple-element.72), channel_id=1, source_target_pairs={{0,4},{4,0},{8,12},{12,8},{16,20},{20,16},{24,28},{28,24},{1,5},{5... | collective-permute-start | bytes 3145736 | tf_op jit(solution)/shard_map/ppermute | solution.py:610
  103.3 1.0 copy-start.8
  104.3 1.0 copy-start.11
  105.3 1.0 copy-start.14
  106.4 1.0 copy-start.16
  107.4 1.0 copy-start.18
  108.5 7.4 %copy-start.1 = (bf16[8192,128]{1,0:T(8,128)(2,1)S(1)}, bf16[8192,128]{1,0:T(8,128)(2,1)}, u32[]{:S(2)}) copy-start(bf16[8192,128]{1,0:T(8,128)(2,1)} %copy-done) | copy-start | bytes 6291460
  108.5 7.4 %copy-start.19 = (bf16[4096,128]{1,0:T(8,128)(2,1)S(1)}, bf16[4096,128]{1,0:T(8,128)(2,1)}, u32[]{:S(2)}) copy-start(bf16[4096,128]{1,0:T(8,128)(2,1)} %get-tuple-element.71.mine_ref) | copy-start | bytes 3145732
  110.6 29.1 %collective-permute-start.9 = (bf16[128,1024]{1,0:T(8,128)(2,1)S(1)}, bf16[128,1024]{1,0:T(8,128)(2,1)S(1)}, u32[]{:S(2)}, u32[]{:S(2)}) collective-permute-start(bf16[128,1024]{1,0:T(8,128)(2,1)S(1)} %get-tuple-element.78), channel_id=1, source_target_pairs={{0,4},{4,0},{8,12},{12,8},{16,20},{20,16},{24,28},{28,24},{1,5},{5... | collective-permute-start | bytes 786440 | tf_op jit(solution)/shard_map/ppermute | solution.py:610
  111.2 28.5 %collective-permute-start.10 = (bf16[512,256]{1,0:T(8,128)(2,1)S(1)}, bf16[512,256]{1,0:T(8,128)(2,1)S(1)}, u32[]{:S(2)}, u32[]{:S(2)}) collective-permute-start(bf16[512,256]{1,0:T(8,128)(2,1)S(1)} %get-tuple-element.79), channel_id=1, source_target_pairs={{0,1},{1,2},{2,3},{3,0},{4,5},{5,6},{6,7},{7,4},{8,9},{9,10},{10,1... | collective-permute-start | bytes 786440 | tf_op jit(solution)/shard_map/ppermute | solution.py:619
  113.5 26.1 %collective-permute-start.11 = (bf16[512,256]{1,0:T(8,128)(2,1)S(1)}, bf16[512,256]{1,0:T(8,128)(2,1)S(1)}, u32[]{:S(2)}, u32[]{:S(2)}) collective-permute-start(bf16[512,256]{1,0:T(8,128)(2,1)S(1)} %get-tuple-element.80), channel_id=1, source_target_pairs={{0,2},{1,3},{2,0},{3,1},{4,6},{5,7},{6,4},{7,5},{8,10},{9,11},{10,... | collective-permute-start | bytes 786440 | tf_op jit(solution)/shard_map/ppermute | solution.py:619
  113.5 26.1 %collective-permute-start.12 = (bf16[512,256]{1,0:T(8,128)(2,1)S(1)}, bf16[512,256]{1,0:T(8,128)(2,1)S(1)}, u32[]{:S(2)}, u32[]{:S(2)}) collective-permute-start(bf16[512,256]{1,0:T(8,128)(2,1)S(1)} %get-tuple-element.81), channel_id=1, source_target_pairs={{0,3},{1,0},{2,1},{3,2},{4,7},{5,4},{6,5},{7,6},{8,11},{9,8},{10,9... | collective-permute-start | bytes 786440 | tf_op jit(solution)/shard_map/ppermute | solution.py:619
  115.9 2.2 %copy-start.3 = (bf16[64,128,256]{2,1,0:T(8,128)(2,1)S(1)}, bf16[64,128,256]{2,1,0:T(8,128)(2,1)}, u32[]{:S(2)}) copy-start(bf16[64,128,256]{2,1,0:T(8,128)(2,1)} %copy-done.2) | copy-start | bytes 12582916
  139.7 1.2 copy-start.32
  139.7 1.2 copy-start.34
  139.7 9.6 %collective-permute-start.16 = (bf16[4096,128]{1,0:T(8,128)(2,1)}, bf16[4096,128]{1,0:T(8,128)(2,1)S(1)}, u32[]{:S(2)}, u32[]{:S(2)}) collective-permute-start(bf16[4096,128]{1,0:T(8,128)(2,1)} %get-tuple-element.93), channel_id=1, source_target_pairs={{0,4},{4,0},{8,12},{12,8},{16,20},{20,16},{24,28},{28,24},{1,5},{5... | collective-permute-start | bytes 3145736 | tf_op jit(solution)/shard_map/ppermute | solution.py:610
  140.4 8.3 %collective-permute-start.17 = (bf16[128,1024]{1,0:T(8,128)(2,1)S(1)}, bf16[128,1024]{1,0:T(8,128)(2,1)S(1)}, u32[]{:S(2)}, u32[]{:S(2)}) collective-permute-start(bf16[128,1024]{1,0:T(8,128)(2,1)S(1)} %add_convert_fusion.3), channel_id=1, source_target_pairs={{0,8},{4,12},{8,0},{12,4},{16,24},{20,28},{24,16},{28,20},{1,9},{5... | collective-permute-start | bytes 786440 | tf_op jit(solution)/shard_map/ppermute | solution.py:610
  140.9 16.6 %collective-permute-start.13 = (bf16[512,256]{1,0:T(8,128)(2,1)}, bf16[512,256]{1,0:T(8,128)(2,1)}, u32[]{:S(2)}, u32[]{:S(2)}) collective-permute-start(bf16[512,256]{1,0:T(8,128)(2,1)} %copy-done.27), channel_id=1, source_target_pairs={{0,1},{1,2},{2,3},{3,0},{4,5},{5,6},{6,7},{7,4},{8,9},{9,10},{10,1... | collective-permute-start | bytes 786440 | tf_op jit(solution)/shard_map/ppermute | solution.py:619
  140.9 21.5 %collective-permute-start.14 = (bf16[512,256]{1,0:T(8,128)(2,1)}, bf16[512,256]{1,0:T(8,128)(2,1)}, u32[]{:S(2)}, u32[]{:S(2)}) collective-permute-start(bf16[512,256]{1,0:T(8,128)(2,1)} %copy-done.26), channel_id=1, source_target_pairs={{0,2},{1,3},{2,0},{3,1},{4,6},{5,7},{6,4},{7,5},{8,10},{9,11},{10,... | collective-permute-start | bytes 786440 | tf_op jit(solution)/shard_map/ppermute | solution.py:619
  143.5 18.9 %collective-permute-start.15 = (bf16[512,256]{1,0:T(8,128)(2,1)}, bf16[512,256]{1,0:T(8,128)(2,1)}, u32[]{:S(2)}, u32[]{:S(2)}) collective-permute-start(bf16[512,256]{1,0:T(8,128)(2,1)} %copy-done.25), channel_id=1, source_target_pairs={{0,3},{1,0},{2,1},{3,2},{4,7},{5,4},{6,5},{7,6},{8,11},{9,8},{10,9... | collective-permute-start | bytes 786440 | tf_op jit(solution)/shard_map/ppermute | solution.py:619
  148.7 5.5 %copy-start.23 = (bf16[512,256]{1,0:T(8,128)(2,1)S(1)}, bf16[512,256]{1,0:T(8,128)(2,1)}, u32[]{:S(2)}) copy-start(bf16[512,256]{1,0:T(8,128)(2,1)} %copy-done.22) | copy-start | bytes 786436
  148.7 5.5 %copy-start.31 = (bf16[512,256]{1,0:T(8,128)(2,1)S(1)}, bf16[512,256]{1,0:T(8,128)(2,1)}, u32[]{:S(2)}) copy-start(bf16[512,256]{1,0:T(8,128)(2,1)} %copy-done.30) | copy-start | bytes 786436
  148.7 5.5 %copy-start.33 = (bf16[512,256]{1,0:T(8,128)(2,1)S(1)}, bf16[512,256]{1,0:T(8,128)(2,1)}, u32[]{:S(2)}) copy-start(bf16[512,256]{1,0:T(8,128)(2,1)} %copy-done.32) | copy-start | bytes 786436
  148.7 7.7 %collective-permute-start.18 = (bf16[128,1024]{1,0:T(8,128)(2,1)S(1)}, bf16[128,1024]{1,0:T(8,128)(2,1)}, u32[]{:S(2)}, u32[]{:S(2)}) collective-permute-start(bf16[128,1024]{1,0:T(8,128)(2,1)S(1)} %add_convert_fusion.2), channel_id=1, source_target_pairs={{0,16},{4,20},{8,24},{12,28},{16,0},{20,4},{24,8},{28,12},{1,17},{... | collective-permute-start | bytes 786440 | tf_op jit(solution)/shard_map/ppermute | solution.py:610
  150.6 18.9 %all-to-all-start.3 = ((bf16[8,512,128]{2,1,0:T(8,128)(2,1)}), bf16[8,512,128]{2,1,0:T(8,128)(2,1)S(1)}, u32[]{:S(2)}, u32[]{:S(2)}) async-start(bf16[8,512,128]{2,1,0:T(8,128)(2,1)} %bitcast), calls=%async_computation.3 | async-start | bytes 2097152 | tf_op jit(solution)/shard_map/all_to_all | solution.py:614
  157.5 7.0 %collective-permute-start.19 = (bf16[128,1024]{1,0:T(8,128)(2,1)S(1)}, bf16[128,1024]{1,0:T(8,128)(2,1)S(1)}, u32[]{:S(2)}, u32[]{:S(2)}) collective-permute-start(bf16[128,1024]{1,0:T(8,128)(2,1)S(1)} %add_convert_fusion.1), channel_id=1, source_target_pairs={{0,4},{4,0},{8,12},{12,8},{16,20},{20,16},{24,28},{28,24},{1,5},{5... | collective-permute-start | bytes 786440 | tf_op jit(solution)/shard_map/ppermute | solution.py:610
  (11 other events, 8.8 us)
where the time goes:
time: 175 us; the launch traced here: 173 us
  Pallas kernels  67.9 us (39%)
  waiting for transfers between devices  37.1 us (21%)
  starting transfers between devices  37 us (21%)
  local copies, waits for them, and re-layouts  23.5 us (13%)
  other arithmetic  6.71 us (4%)
    unnamed x70, local copies, waits for them, and re-layouts  23.5 us
    pallas_call x1, Pallas kernels, backward(): pl.pallas_call(backward_kernel, grid=(blocks // GROUP,), out_shape=[jax.S...  21.5 us
    pallas_call x1, Pallas kernels, forward(): pl.pallas_call(forward_kernel, grid=(blocks // GROUP,), out_shape=[jax.Sh...  21.4 us
    all_to_all x4, waiting for transfers between devices, to_all(): return lax.all_to_all(value, 'seq', split_axis=0, concat_axis=0, tiled=True)  16.7 us
    all_to_all x4, starting transfers between devices, to_all(): return lax.all_to_all(value, 'seq', split_axis=0, concat_axis=0, tiled=True)  14.9 us
    ppermute x6, starting transfers between devices, step_along(): return lax.ppermute(value, 'head', pairs)  11 us
    ppermute x6, waiting for transfers between devices, step_along(): return lax.ppermute(value, 'head', pairs)  10.6 us
    ppermute x6, starting transfers between devices, rotate(): lax.ppermute(value, 'head', [(i, (i + step) % count) for i in range(count)])  8.75 us
  transfers between devices with their start and end apart: 24, of which 10 were waited for; matrix products, arithmetic and copies ran while one was open for 4% of the time, Pallas kernels for 38%

commit v1 on v0

--- a/solution.py
+++ b/solution.py
@@ -21,6 +21,10 @@
 
 def whole(space):
     return pl.BlockSpec(memory_space=space)
+
+
+def in_hbm(value):
+    return pltpu.with_memory_space_constraint(value, pltpu.HBM)
 
 
 def fixed(shape):
@@ -160,7 +164,6 @@
 
     ones = jnp.ones((2 * SPAN, LANES), BF16)
     low = lane_of((SPAN, LANES)) < DH
-    first = lane_of((SPAN, LANES)) == 0
     for p in range(GROUP // SUB):
         here = step * GROUP + p * SUB
         coming = jnp.minimum(here + SUB, blocks - SUB)
@@ -189,10 +192,7 @@
             recip = 1.0 / sums
             prob_ref[b] = (grown * jnp.concatenate([recip, recip], axis=1)).astype(BF16)
             signed = sums * sign_ref[0, :, b : b + 1]
-            rest = signed - signed.astype(BF16).astype(F32)
-            rows_out[now][i] = jnp.where(
-                low, jnp.where(first, signed, rest), mixed[:, :LANES] * recip
-            )
+            rows_out[now][i] = jnp.where(low, signed, mixed[:, :LANES] * recip)
             scatter_rows(addr_ref, gone + i, rows_out[then].at[i], result)
 
     qv_ref[...] = qv_win[SPAN:]
@@ -219,9 +219,9 @@
         out_shape=[
             jax.ShapeDtypeStruct((half, LANES), BF16),
             jax.ShapeDtypeStruct((half, LANES), BF16),
-            jax.ShapeDtypeStruct((blocks, SPAN, 2 * SPAN), BF16),
-            jax.ShapeDtypeStruct((total, LANES), BF16),
-            jax.ShapeDtypeStruct((total, LANES), BF16),
+            pltpu.HBM((blocks, SPAN, 2 * SPAN), BF16),
+            pltpu.HBM((total, LANES), BF16),
+            pltpu.HBM((total, LANES), BF16),
         ],
         in_specs=[
             whole(pltpu.SMEM),
@@ -254,7 +254,7 @@
 
 def share_of(own, peer):
     row = lax.broadcasted_iota(jnp.int32, (LANES, LANES), 0)
-    pick = (row < 2).astype(BF16)
+    pick = (row < 1).astype(BF16)
     own_sum = jnp.dot(own, pick, preferred_element_type=F32)
     peer_sum = jnp.dot(peer, pick, preferred_element_type=F32)
     both = own_sum / (own_sum + peer_sum)
@@ -273,40 +273,45 @@
 
 
 def mix_attention_kernel(own_ref, peer_ref, att_ref):
-    half = own_ref.shape[0] // 2
-    own = own_ref[...]
-    peer = peer_ref[...]
-    combined = combined_rows(own, peer, share_of(own, peer))
-    att_ref[0] = (pltpu.roll(combined[:half], DH, 1) + combined[half:]).astype(BF16)
+    pieces = att_ref.shape[0]
+    rows = own_ref.shape[0] // pieces
+    half = rows // 2
+    for i in range(pieces):
+        own = own_ref[i * rows : (i + 1) * rows]
+        peer = peer_ref[i * rows : (i + 1) * rows]
+        combined = combined_rows(own, peer, share_of(own, peer))
+        att_ref[i] = (pltpu.roll(combined[:half], DH, 1) + combined[half:]).astype(BF16)
 
 
 def mix_grad_kernel(own_ref, peer_ref, grad_ref, grad_own, grad_peer):
-    own = own_ref[...]
-    peer = peer_ref[...]
-    share = share_of(own, peer)
-    combined = combined_rows(own, peer, share)
-    packed = grad_ref[0].astype(F32)
-    grad = jnp.concatenate([pltpu.roll(packed, DH, 1), packed], axis=0)
-    inner = split_sum(grad * combined, jnp.ones((LANES, LANES), BF16))
-    lane = lane_of(grad.shape)
-    for mix, out in ((share, grad_own), (1.0 - share, grad_peer)):
-        delta = -(mix * inner)
-        rest = delta - delta.astype(BF16).astype(F32)
-        tail = jnp.where(lane == 0, delta, jnp.where(lane == 1, rest, 0.0))
-        out[...] = jnp.where(lane < DH, tail, mix * grad).astype(BF16)
+    pieces = grad_ref.shape[0]
+    rows = own_ref.shape[0] // pieces
+    for i in range(pieces):
+        at = slice(i * rows, (i + 1) * rows)
+        own = own_ref[at]
+        peer = peer_ref[at]
+        share = share_of(own, peer)
+        combined = combined_rows(own, peer, share)
+        packed = grad_ref[i].astype(F32)
+        grad = jnp.concatenate([pltpu.roll(packed, DH, 1), packed], axis=0)
+        column = lane_of((LANES, LANES))
+        inner = split_sum(grad * combined, (column < DH).astype(BF16))
+        both = jnp.where(lane_of(grad.shape) < DH, -inner, grad)
+        grad_own[at] = (share * both).astype(BF16)
+        grad_peer[at] = ((1.0 - share) * both).astype(BF16)
 
 
 def mixing(home, peer, grad=None):
     half = peer.shape[0]
     pieces = lax.axis_size("seq")
     rows = half // pieces
-    by_rows = pl.BlockSpec((rows, LANES), lambda g: (g, 0))
-    packed = pl.BlockSpec((1, rows // 2, LANES), lambda g: (g, 0, 0))
+    by_rows = pl.BlockSpec((4 * rows, LANES), lambda g: (g, 0))
+    packed = pl.BlockSpec((4, rows // 2, LANES), lambda g: (g, 0, 0))
     cost = pl.CostEstimate(flops=0, bytes_accessed=10 * MIB, transcendentals=0)
     if grad is None:
         return pl.pallas_call(
             mix_attention_kernel,
-            grid=(pieces,),
+            grid=(pieces // 4,),
             out_shape=jax.ShapeDtypeStruct((pieces, rows // 2, LANES), BF16),
             in_specs=[by_rows, by_rows],
             out_specs=packed,
@@ -315,7 +320,7 @@
         )(home, peer)
     return pl.pallas_call(
         mix_grad_kernel,
-        grid=(pieces,),
+        grid=(pieces // 4,),
         out_shape=[jax.ShapeDtypeStruct((half, LANES), BF16)] * 2,
         in_specs=[by_rows, by_rows, packed],
         out_specs=[by_rows, by_rows],
@@ -346,7 +351,7 @@
         out_shape=jax.ShapeDtypeStruct((rounds * heads, rows // 2 + 16, 2 * DH), BF16),
         compiler_params=pltpu.CompilerParams(vmem_limit_bytes=10 * MIB),
         name="pack_heads",
-    )(queries, values, slots)
+    )(in_hbm(queries), in_hbm(values), slots)
 
 
 def unpack_kernel(in_ref, query_ref, value_ref):
@@ -373,24 +378,14 @@
     return pl.ds(pl.multiple_of(index * width, width), width)
 
 
-def members(refs, groups):
-    place = lax.axis_index("head")
-    own, ups, downs = refs[0], refs[1:groups], refs[groups:]
-    out = [own[...]]
-    for k in range(1, groups):
-        out.append(jnp.where(place >= k, ups[k - 1][...], downs[groups - k - 1][...]))
-    return out
-
-
 def back_kernel(weight_ref, *refs):
     *grads, out_ref = refs
-    groups = (len(grads) + 1) // 2
-    grads = members(grads, groups)
+    groups = len(grads)
     rows, width = grads[0].shape
     total = 0.0
     for k in range(groups):
         weight = weight_ref[:, columns_of(member(k, groups), width)]
-        total += lax.dot_general(grads[k], weight, NT, preferred_element_type=F32)
+        total += lax.dot_general(grads[k][...], weight, NT, preferred_element_type=F32)
     total = total.astype(BF16)
     quarter = rows // 4
     for h in range(width // DH):
@@ -412,7 +407,7 @@
 
 
 def project_kernel(weight_ref, packed_ref, att_ref, *outs):
-    groups = len(outs) // 2
+    groups = len(outs)
     rows, width = att_ref.shape
     quarter = rows // 4
     for h in range(width // DH):
@@ -423,9 +418,7 @@
             att_ref[(2 * c + 1) * quarter : (2 * c + 2) * quarter, columns] = packed[:, DH:]
     for k in range(groups):
         weight = weight_ref[:, columns_of(member(groups - k, groups), width)]
-        for c in range(2):
-            part = att_ref[2 * c * quarter : 2 * (c + 1) * quarter]
-            outs[2 * k + c][...] = jnp.dot(part, weight, preferred_element_type=F32).astype(BF16)
+        outs[k][...] = jnp.dot(att_ref[...], weight, preferred_element_type=F32).astype(BF16)
 
 
 def project(weight, packed):
@@ -434,8 +427,7 @@
     groups = weight.shape[1] // width
     return pl.pallas_call(
         project_kernel,
-        out_shape=[jax.ShapeDtypeStruct((rows, width), BF16)]
-        + [jax.ShapeDtypeStruct((rows // 2, width), BF16)] * (2 * groups),
+        out_shape=[jax.ShapeDtypeStruct((rows, width), BF16)] * (1 + groups),
         compiler_params=pltpu.CompilerParams(vmem_limit_bytes=10 * MIB),
         name="project",
     )(weight, packed)
@@ -443,8 +435,7 @@
 
 def weight_grad_kernel(att_ref, *refs):
     *grads, keep_ref, give_ref = refs
-    groups = (len(grads) + 1) // 2
-    grads = members(grads, groups)
+    groups = len(grads)
     width = grads[0].shape[1]
     part = keep_ref.shape[0]
     core = lax.rem(lax.axis_index("seq"), 2)
@@ -452,13 +443,13 @@
         att = att_ref[:, columns_of(index, part)]
         for k in range(groups):
             out_ref[:, columns_of(member(k, groups), width)] = lax.dot_general(
-                att, grads[k], TN, preferred_element_type=F32
+                att, grads[k][...], TN, preferred_element_type=F32
             ).astype(BF16)
 
 
 def weight_grad(att, grads):
     width = att.shape[1]
-    groups = (len(grads) + 1) // 2
+    groups = len(grads)
     return pl.pallas_call(
         weight_grad_kernel,
         out_shape=[jax.ShapeDtypeStruct((width // 2, width * groups), BF16)] * 2,
@@ -511,8 +502,9 @@
         now, then = p % 2, 1 - p % 2
         spans = slice(p * SUB * SPAN, ((p + 1) * SUB + 1) * SPAN)
         everything = qv_win[spans]
-        high = lane_of(everything.shape) >= DH
-        value_one = jnp.where(high, everything, jnp.ones_like(everything))
+        lane = lane_of(everything.shape)
+        one = jnp.where(lane == 0, 1.0, 0.0).astype(BF16)
+        value_one = jnp.where(lane >= DH, everything, one)
         for i in range(SUB):
             b = p * SUB + i
             prob = prob_ref[b]
@@ -602,7 +594,7 @@
         compiler_params=pltpu.CompilerParams(vmem_limit_bytes=22 * MIB),
         cost_estimate=pl.CostEstimate(flops=0, bytes_accessed=64 * MIB, transcendentals=0),
         name="span_backward",
-    )(addr, mine, other, prob, query_key, query_key, value_one, value_one)
+    )(addr, mine, other, *[in_hbm(x) for x in (prob, query_key, query_key, value_one, value_one)])
 
 
 def swap(value, distance=1):
@@ -617,13 +609,6 @@
 def rotate(value, step):
     count = lax.axis_size("head")
     return lax.ppermute(value, "head", [(i, (i + step) % count) for i in range(count)])
-
-
-def step_along(value, step, count, way):
-    pairs = [(i, i + 1) for i in range(step - 1, count - 1)]
-    if way < 0:
-        pairs = [(count - 1 - i, count - 1 - j) for i, j in pairs]
-    return lax.ppermute(value, "head", pairs)
 
 
 def after(values, *earlier):
@@ -643,13 +628,9 @@
     mine = to_all(packed)
     places = find_places(mine)
 
-    ups, downs = [out_grad], [out_grad]
-    for k in range(1, groups):
-        ups.append(step_along(ups[-1], k, groups, 1))
-        downs.append(step_along(downs[-1], k, groups, -1))
-        if k == groups - 2:
-            mine = after(mine, ups[-1], downs[-1])
-    grads = [*ups, *downs[1:]]
+    first = rotate(out_grad, 1)
+    grads = [out_grad, first, rotate(first, 1), rotate(out_grad, groups - 1)]
+    mine = after(mine, *grads[1:3])
 
     home, away, prob, query_key, value_one = forward(places[0], mine, swap(mine), *places[1:])
     away, *grads = after([away, *grads])
@@ -663,24 +644,24 @@
     grad_other = swap(grad_peer)
 
     att, *shares = project(w_out, att_packed)
-    early = [rotate(shares[2 * k], k) for k in range(1, groups)]
+    early = [rotate(shares[k], k) for k in range(1, groups, 2)]
     weight, give = weight_grad(att, grads)
-    got = swap(give)
+    weight = (weight.astype(F32) + swap(give).astype(F32)).astype(BF16)
+    weights = [weight] + [swap(weight, distance) for distance in range(2, shards, 2)]
 
     own, others = backward(places[0], grad_own, grad_other, prob, query_key, value_one)
-    others, got, *early = after([others, got, *early])
-    late = after([shares[2 * k + 1] for k in range(1, groups)], own)
-    late = [rotate(late[k - 1], k) for k in range(1, groups)]
+    others, *weights = after([others, *weights])
+    others, *early = after([others, *early])
+    late = [rotate(after(shares[k], own), k) for k in range(2, groups, 2)]
 
     summed = (own.astype(F32) + swap(others).astype(F32)).astype(BF16)
     summed = to_all(summed.reshape(shards, half_rows, LANES))
     query_grad, value_grad = unpack_heads(summed.reshape(heads, rows, LANES))
 
-    weight = (weight.astype(F32) + got.astype(F32)).astype(BF16)
-    distance = 2
-    while distance < shards:
-        weight = (weight.astype(F32) + swap(weight, distance).astype(F32)).astype(BF16)
-        distance *= 2
+    weights = [w.astype(F32) for w in weights]
+    while len(weights) > 1:
+        weights = [weights[i] + weights[i + 1] for i in range(0, len(weights), 2)]
+    weight = weights[0].astype(BF16)
     rest = swap(weight)
     weight = jnp.where(
         core == 0,
@@ -689,13 +670,10 @@
     )
     w_out_grad = weight.astype(F32) * total ** (-0.5)
 
-    output = []
-    for c, received in enumerate((early, late)):
-        part = shares[c].astype(F32)
-        for share in received:
-            part = part + share.astype(F32)
-        output.append(part.astype(BF16))
-    return (jnp.concatenate(output, axis=0), query_grad, value_grad, w_out_grad)
+    output = shares[0].astype(F32)
+    for share in early + late:
+        output = output + share.astype(F32)
+    return (output.astype(BF16), query_grad, value_grad, w_out_grad)
 
 
 def shifted(value, axis, steps):

time: 175 us -> 152 us (0.87)
  local copies, waits for them, and re-layouts: 23.5 us -> 4.78 us
  waiting for transfers between devices: 37.1 us -> 51.1 us
  starting transfers between devices: 37 us -> 26.8 us
  Pallas kernels: 67.9 us -> 62.3 us
    ppermute x6, waiting for transfers between devices: 4.86 us -> 27 us  [rotate(): lax.ppermute(value, 'head', [(i, (i + step) % count) for i in range(count)])]
    unnamed x70 -> x24, local copies, waits for them, and re-layouts: 23.5 us -> 4.78 us
    ppermute x6 -> x0, starting transfers between devices: 11 us -> none  [step_along(): return lax.ppermute(value, 'head', pairs)]
    ppermute x6 -> x0, waiting for transfers between devices: 10.6 us -> none  [step_along(): return lax.ppermute(value, 'head', pairs)]
    pallas_call x2, Pallas kernels: 13.9 us -> 8.23 us  [the longest x1 4.87 us: mixing(): pl.pallas_call(mix_grad_kernel, grid=(pieces // 4,), out_shape=[jax.Shape...]
    ppermute x8 -> x9, starting transfers between devices: 2.36 us -> 4.77 us  [swap(): return lax.ppermute(value, 'seq', [(i, i ^ distance) for i in range(count)])]
    all_to_all x4, waiting for transfers between devices: 16.7 us -> 18.8 us  [to_all(): return lax.all_to_all(value, 'seq', split_axis=0, concat_axis=0, tiled=True)]
    ppermute x6, starting transfers between devices: 8.75 us -> 6.98 us  [rotate(): lax.ppermute(value, 'head', [(i, (i + step) % count) for i in range(count)])]
  transfers between devices with their start and end apart: 24 -> 19, of which waited for: 10 -> 9; matrix products, arithmetic and copies ran while one was open for 4% -> 4% of each run, Pallas kernels for 38% -> 39%
where the time goes in v1:
time: 152 us; the launch traced here: 151 us
  Pallas kernels  62.3 us (41%)
  waiting for transfers between devices  51.1 us (34%)
  starting transfers between devices  26.8 us (18%)
  other arithmetic  5.73 us (4%)
  local copies, waits for them, and re-layouts  4.78 us (3%)
    ppermute x6, waiting for transfers between devices, rotate(): lax.ppermute(value, 'head', [(i, (i + step) % count) for i in range(count)])  27 us
    pallas_call x1, Pallas kernels, forward(): pl.pallas_call(forward_kernel, grid=(blocks // GROUP,), out_shape=[jax.Sh...  22.9 us
    pallas_call x1, Pallas kernels, backward(): pl.pallas_call(backward_kernel, grid=(blocks // GROUP,), out_shape=[jax.S...  20.7 us
    all_to_all x4, waiting for transfers between devices, to_all(): return lax.all_to_all(value, 'seq', split_axis=0, concat_axis=0, tiled=True)  18.8 us
    all_to_all x4, starting transfers between devices, to_all(): return lax.all_to_all(value, 'seq', split_axis=0, concat_axis=0, tiled=True)  15.1 us
    ppermute x6, starting transfers between devices, rotate(): lax.ppermute(value, 'head', [(i, (i + step) % count) for i in range(count)])  6.98 us
    ppermute x9, waiting for transfers between devices, swap(): return lax.ppermute(value, 'seq', [(i, i ^ distance) for i in range(count)])  5.24 us
    pallas_call x1, Pallas kernels, mixing(): pl.pallas_call(mix_grad_kernel, grid=(pieces // 4,), out_shape=[jax.Shape...  4.87 us
  transfers between devices with their start and end apart: 19, of which 9 were waited for; matrix products, arithmetic and copies ran while one was open for 4% of the time, Pallas kernels for 39%

profile of v1, /device:TPU:0, one launch (start us, length us, event | category | flops | bytes accessed | tf_op | source)
XLA Modules:
  0.0 151.5 jit_solution(14223908349985790232)
XLA Ops:
  0.6 3.1 %collective-permute-start = (bf16[1024,256]{1,0:T(8,128)(2,1)}, bf16[1024,256]{1,0:T(8,128)(2,1)S(1)}, u32[]{:S(2)}, u32[]{:S(2)}) collective-permute-start(bf16[1024,256]{1,0:T(8,128)(2,1)} %refs_0_.1), channel_id=1, source_target_pairs={{0,1},{1,2},{2,3},{3,0},{4,5},{5,6},{6,7},{7,4},{8,9},{9,10},{10,1... | collective-permute-start | bytes 1572872 | tf_op jit(solution)/shard_map/ppermute | solution.py:611
  3.7 0.8 copy-done.7
  4.5 2.5 %pack_heads.1 = bf16[8,528,128]{2,1,0:T(8,128)(2,1)} custom-call(bf16[1024,256]{1,0:T(8,128)(2,1)} %query_ref.1, bf16[1024,256]{1,0:T(8,128)(2,1)} %value_ref.1, s32[2,4,1024]{2,1,0:T(4,128)S(1)} %copy-done.7), custom_call_target="tpu_custom_call" | custom-call | tf_op jit(solution)/shard_map/pack_heads/pallas_call | solution.py:349
  7.0 3.7 %all-to-all-start = ((bf16[8,528,128]{2,1,0:T(8,128)(2,1)}), bf16[8,528,128]{2,1,0:T(8,128)(2,1)S(1)}, u32[]{:S(2)}, u32[]{:S(2)}) async-start(bf16[8,528,128]{2,1,0:T(8,128)(2,1)} %pack_heads.1), calls=%async_computation | async-start | bytes 2162688 | tf_op jit(solution)/shard_map/all_to_all | solution.py:606
  10.7 7.1 %collective-permute-done.refs_1_ = bf16[1024,256]{1,0:T(8,128)(2,1)S(1)} collective-permute-done((bf16[1024,256]{1,0:T(8,128)(2,1)}, bf16[1024,256]{1,0:T(8,128)(2,1)S(1)}, u32[]{:S(2)}, u32[]{:S(2)}) %collective-permute-start) | collective-permute-done | bytes 524320 | tf_op jit(solution)/shard_map/ppermute | solution.py:611
  17.9 8.6 %all-to-all-done.mine_ref = bf16[8,528,128]{2,1,0:T(8,128)(2,1)S(1)} async-done(((bf16[8,528,128]{2,1,0:T(8,128)(2,1)}), bf16[8,528,128]{2,1,0:T(8,128)(2,1)S(1)}, u32[]{:S(2)}, u32[]{:S(2)}) %all-to-all-start) | async-done | bytes 1081376 | tf_op jit(solution)/shard_map/all_to_all | solution.py:606
  26.5 6.3 %collective-permute-done.1.refs_2_ = bf16[1024,256]{1,0:T(8,128)(2,1)S(1)} collective-permute-done((bf16[1024,256]{1,0:T(8,128)(2,1)S(1)}, bf16[1024,256]{1,0:T(8,128)(2,1)S(1)}, u32[]{:S(2)}, u32[]{:S(2)}) %collective-permute-start.1) | collective-permute-done | bytes 524320 | tf_op jit(solution)/shard_map/ppermute | solution.py:611
  32.8 1.2 find_places.1
  34.0 1.5 collective-permute-done.2.other_ref
  35.5 22.9 %span_forward.1 = (bf16[4096,128]{1,0:T(8,128)(2,1)S(1)}, bf16[4096,128]{1,0:T(8,128)(2,1)}, bf16[64,128,256]{2,1,0:T(8,128)(2,1)}, bf16[8192,128]{1,0:T(8,128)(2,1)}, bf16[8192,128]{1,0:T(8,128)(2,1)}) custom-call(s32[64,128]{1,0:T(8,128)S(1)} %get-tuple-element.45.addr_ref, bf16[8,528,128]{2,1,0:T(8,128)(2,1)S(1)} %all-to-all-done.mine_ref, ...), custom_call_target="tpu_custom_call" | custom-call | bytes 67108864 | tf_op jit(solution)/shard_map/span_forward/pallas_call | solution.py:216
  58.4 1.0 copy-done
  59.4 0.1 collective-permute-start.4
  59.5 1.0 copy-done.2
  60.6 1.6 %back_projection.1 = bf16[8,256,128]{2,1,0:T(8,128)(2,1)} custom-call(bf16[256,1024]{1,0:T(8,128)(2,1)S(1)} %copy-done.2, bf16[1024,256]{1,0:T(8,128)(2,1)S(1)} %copy-done.1, bf16[1024,256]{1,0:T(8,128)(2,1)S(1)} %collective-permute-done.refs_1_, bf16[1024,256]{1,0:T(8,128)(2,1)S(1)} %collective-permute-done.1.refs_2_, ...), custom_call_target="tpu_custom_call" | custom-call | tf_op jit(solution)/shard_map/back_projection/pallas_call | solution.py:401
  62.2 4.2 %all-to-all-start.1 = ((bf16[8,256,128]{2,1,0:T(8,128)(2,1)}), bf16[8,256,128]{2,1,0:T(8,128)(2,1)}, u32[]{:S(2)}, u32[]{:S(2)}) async-start(bf16[8,256,128]{2,1,0:T(8,128)(2,1)} %back_projection.1), calls=%async_computation.1 | async-start | bytes 1048576 | tf_op jit(solution)/shard_map/all_to_all | solution.py:606
  66.3 0.0 copy-start.9
  66.3 1.0 copy-done.9
  67.3 3.4 %mix_attention.1 = bf16[8,256,128]{2,1,0:T(8,128)(2,1)} custom-call(bf16[4096,128]{1,0:T(8,128)(2,1)} %copy-done, bf16[4096,128]{1,0:T(8,128)(2,1)} %copy-done.9), custom_call_target="tpu_custom_call" | custom-call | bytes 10485760 | tf_op jit(solution)/shard_map/mix_attention/pallas_call | solution.py:312
  70.7 5.4 %all-to-all-done.1.grad_ref = bf16[8,256,128]{2,1,0:T(8,128)(2,1)} async-done(((bf16[8,256,128]{2,1,0:T(8,128)(2,1)}), bf16[8,256,128]{2,1,0:T(8,128)(2,1)}, u32[]{:S(2)}, u32[]{:S(2)}) %all-to-all-start.1) | async-done | bytes 524320 | tf_op jit(solution)/shard_map/all_to_all | solution.py:606
  76.1 3.5 %all-to-all-start.2 = ((bf16[8,256,128]{2,1,0:T(8,128)(2,1)}), bf16[8,256,128]{2,1,0:T(8,128)(2,1)S(1)}, u32[]{:S(2)}, u32[]{:S(2)}) async-start(bf16[8,256,128]{2,1,0:T(8,128)(2,1)} %mix_attention.1), calls=%async_computation.2 | async-start | bytes 1048576 | tf_op jit(solution)/shard_map/all_to_all | solution.py:606
  79.6 4.9 %mix_grad.1 = (bf16[4096,128]{1,0:T(8,128)(2,1)}, bf16[4096,128]{1,0:T(8,128)(2,1)}) custom-call(bf16[4096,128]{1,0:T(8,128)(2,1)} %copy-done, bf16[4096,128]{1,0:T(8,128)(2,1)} %copy-done.9, bf16[8,256,128]{2,1,0:T(8,128)(2,1)} %all-to-all-done.1.grad_ref), custom_call_target="tpu_custom_call" | custom-call | bytes 10485760 | tf_op jit(solution)/shard_map/mix_grad/pallas_call | solution.py:321
  84.5 4.8 %all-to-all-done.2.packed_ref = bf16[8,256,128]{2,1,0:T(8,128)(2,1)S(1)} async-done(((bf16[8,256,128]{2,1,0:T(8,128)(2,1)}), bf16[8,256,128]{2,1,0:T(8,128)(2,1)S(1)}, u32[]{:S(2)}, u32[]{:S(2)}) %all-to-all-start.2) | async-done | bytes 524320 | tf_op jit(solution)/shard_map/all_to_all | solution.py:606
  89.3 1.6 %project.1 = (bf16[1024,256]{1,0:T(8,128)(2,1)S(1)}, bf16[1024,256]{1,0:T(8,128)(2,1)S(1)}, bf16[1024,256]{1,0:T(8,128)(2,1)S(1)}, bf16[1024,256]{1,0:T(8,128)(2,1)}, bf16[1024,256]{1,0:T(8,128)(2,1)S(1)}) custom-call(bf16[256,1024]{1,0:T(8,128)(2,1)S(1)} %copy-done.3, bf16[8,256,128]{2,1,0:T(8,128)(2,1)S(1)} %all-to-all-done.2.packed_ref), custom_call_target="tpu_custom_call" | custom-call | tf_op jit(solution)/shard_map/project/pallas_call | solution.py:428
  90.9 0.8 weight_grad.1
  91.7 0.0 copy-done.5
  91.7 0.5 collective-permute-start.6
  92.2 0.7 collective-permute-start.10
  92.9 3.1 %collective-permute-start.11 = (bf16[1024,256]{1,0:T(8,128)(2,1)S(1)}, bf16[1024,256]{1,0:T(8,128)(2,1)S(1)}, u32[]{:S(2)}, u32[]{:S(2)}) collective-permute-start(bf16[1024,256]{1,0:T(8,128)(2,1)S(1)} %get-tuple-element.73), channel_id=1, source_target_pairs={{0,3},{1,0},{2,1},{3,2},{4,7},{5,4},{6,5},{7,6},{8,11},{9,8},{10,9... | collective-permute-start | bytes 1572872 | tf_op jit(solution)/shard_map/ppermute | solution.py:611
  96.1 0.1 add_convert_fusion.3
  96.1 0.6 collective-permute-start.9
  96.8 1.5 collective-permute-start.8
  98.2 1.5 collective-permute-start.7
  99.7 20.7 %span_backward.1 = (bf16[4096,128]{1,0:T(8,128)(2,1)S(1)}, bf16[4096,128]{1,0:T(8,128)(2,1)S(1)}) custom-call(s32[64,128]{1,0:T(8,128)S(1)} %get-tuple-element.45.addr_ref, bf16[4096,128]{1,0:T(8,128)(2,1)S(1)} %copy-done.4, bf16[4096,128]{1,0:T(8,128)(2,1)S(1)} %collective-permute-done.5.other_ref, bf16[64,128,256]{2,1,0:T(8,128)(2,1)} %get-tuple-element.64.prob_ref, ...), custom_call_target="tpu_custom_call" | custom-call | bytes 67108864 | tf_op jit(solution)/shard_map/span_backward/pallas_call | solution.py:568
  120.5 0.0 copy-start.10
  120.5 0.0 copy-start.11
  120.5 0.1 collective-permute-start.13
  120.6 0.1 collective-permute-start.12
  120.7 2.6 %collective-permute-done.13 = bf16[4096,128]{1,0:T(8,128)(2,1)S(1)} collective-permute-done((bf16[4096,128]{1,0:T(8,128)(2,1)S(1)}, bf16[4096,128]{1,0:T(8,128)(2,1)S(1)}, u32[]{:S(2)}, u32[]{:S(2)}) %collective-permute-start.13) | collective-permute-done | bytes 1048608 | tf_op jit(solution)/shard_map/ppermute | solution.py:602
  123.3 1.3 add_convert_fusion
  124.5 3.7 %all-to-all-start.3 = ((bf16[8,512,128]{2,1,0:T(8,128)(2,1)}), bf16[8,512,128]{2,1,0:T(8,128)(2,1)S(1)}, u32[]{:S(2)}, u32[]{:S(2)}) async-start(bf16[8,512,128]{2,1,0:T(8,128)(2,1)} %bitcast), calls=%async_computation.3 | async-start | bytes 2097152 | tf_op jit(solution)/shard_map/all_to_all | solution.py:606
  128.2 1.2 add_convert_fusion.2
  129.4 0.5 collective-permute-start.14
  129.9 1.2 collective-permute-done.14
  131.1 1.1 convert_multiply_fusion
  132.2 13.6 %collective-permute-done.12 = bf16[1024,256]{1,0:T(8,128)(2,1)} collective-permute-done((bf16[1024,256]{1,0:T(8,128)(2,1)}, bf16[1024,256]{1,0:T(8,128)(2,1)}, u32[]{:S(2)}, u32[]{:S(2)}) %collective-permute-start.12) | collective-permute-done | bytes 524320 | tf_op jit(solution)/shard_map/ppermute | solution.py:611
  145.7 2.1 %add_convert_fusion.1 = bf16[1024,256]{1,0:T(8,128)(2,1)} fusion(bf16[1024,256]{1,0:T(8,128)(2,1)} %collective-permute-done.12, bf16[1024,256]{1,0:T(8,128)(2,1)S(1)} %collective-permute-done.11, bf16[1024,256]{1,0:T(8,128)(2,1)S(1)} %collective-permute-done.10, bf16[1024,256]{1,0:T(8,128)(2,1)S(1)} %copy-done.6), kind=kLoop, calls=%fused_computation.2 | loop fusion | flops 2097152 | bytes 2621440 | tf_op jit(solution)/shard_map/convert_element_type | solution.py:676
  147.8 1.0 copy-done.8
  148.8 2.7 %unpack_heads.1 = (bf16[1024,256]{1,0:T(8,128)(2,1)}, bf16[1024,256]{1,0:T(8,128)(2,1)}) custom-call(bf16[4,1024,128]{2,1,0:T(8,128)(2,1)} %bitcast.2), custom_call_target="tpu_custom_call" | custom-call | tf_op jit(solution)/shard_map/unpack_heads/pallas_call | solution.py:366
  (29 shorter events, 0.1 us)
Async XLA Ops:
  0.6 32.2 %copy-start.1 = (bf16[1024,256]{1,0:T(8,128)(2,1)S(1)}, bf16[1024,256]{1,0:T(8,128)(2,1)}, u32[]{:S(2)}) copy-start(bf16[1024,256]{1,0:T(8,128)(2,1)} %refs_0_.1) | copy-start | bytes 1572868
  0.6 17.2 %collective-permute-start = (bf16[1024,256]{1,0:T(8,128)(2,1)}, bf16[1024,256]{1,0:T(8,128)(2,1)S(1)}, u32[]{:S(2)}, u32[]{:S(2)}) collective-permute-start(bf16[1024,256]{1,0:T(8,128)(2,1)} %refs_0_.1), channel_id=1, source_target_pairs={{0,1},{1,2},{2,3},{3,0},{4,5},{5,6},{6,7},{7,4},{8,9},{9,10},{10,1... | collective-permute-start | bytes 1572872 | tf_op jit(solution)/shard_map/ppermute | solution.py:611
  3.7 0.8 copy-start.7
  7.0 19.5 %all-to-all-start = ((bf16[8,528,128]{2,1,0:T(8,128)(2,1)}), bf16[8,528,128]{2,1,0:T(8,128)(2,1)S(1)}, u32[]{:S(2)}, u32[]{:S(2)}) async-start(bf16[8,528,128]{2,1,0:T(8,128)(2,1)} %pack_heads.1), calls=%async_computation | async-start | bytes 2162688 | tf_op jit(solution)/shard_map/all_to_all | solution.py:606
  17.9 14.9 %collective-permute-start.1 = (bf16[1024,256]{1,0:T(8,128)(2,1)S(1)}, bf16[1024,256]{1,0:T(8,128)(2,1)S(1)}, u32[]{:S(2)}, u32[]{:S(2)}) collective-permute-start(bf16[1024,256]{1,0:T(8,128)(2,1)S(1)} %collective-permute-done.refs_1_), channel_id=1, source_target_pairs={{0,1},{1,2},{2,3},{3,0},{4,5},{5,6},{6,7},{7,4},{8,9},{9,10},{10,1... | collective-permute-start | bytes 1572872 | tf_op jit(solution)/shard_map/ppermute | solution.py:611
  32.8 2.7 %collective-permute-start.2 = (bf16[8,528,128]{2,1,0:T(8,128)(2,1)S(1)}, bf16[8,528,128]{2,1,0:T(8,128)(2,1)S(1)}, u32[]{:S(2)}, u32[]{:S(2)}) collective-permute-start(bf16[8,528,128]{2,1,0:T(8,128)(2,1)S(1)} %all-to-all-done.mine_ref), channel_id=1, source_target_pairs={{0,4},{4,0},{8,12},{12,8},{16,20},{20,16},{24,28},{28,24},{1,5},{5... | collective-permute-start | bytes 3244040 | tf_op jit(solution)/shard_map/ppermute | solution.py:602
  32.8 26.6 %collective-permute-start.3 = (bf16[1024,256]{1,0:T(8,128)(2,1)S(1)}, bf16[1024,256]{1,0:T(8,128)(2,1)S(1)}, u32[]{:S(2)}, u32[]{:S(2)}) collective-permute-start(bf16[1024,256]{1,0:T(8,128)(2,1)S(1)} %copy-done.1), channel_id=1, source_target_pairs={{0,3},{1,0},{2,1},{3,2},{4,7},{5,4},{6,5},{7,6},{8,11},{9,8},{10,9... | collective-permute-start | bytes 1572872 | tf_op jit(solution)/shard_map/ppermute | solution.py:611
  58.4 1.0 copy-start
  59.4 6.9 %collective-permute-start.4 = (bf16[4096,128]{1,0:T(8,128)(2,1)}, bf16[4096,128]{1,0:T(8,128)(2,1)S(1)}, u32[]{:S(2)}, u32[]{:S(2)}) collective-permute-start(bf16[4096,128]{1,0:T(8,128)(2,1)} %get-tuple-element.52), channel_id=1, source_target_pairs={{0,4},{4,0},{8,12},{12,8},{16,20},{20,16},{24,28},{28,24},{1,5},{5... | collective-permute-start | bytes 3145736 | tf_op jit(solution)/shard_map/ppermute | solution.py:602
  59.5 1.0 copy-start.2
  62.2 13.9 %all-to-all-start.1 = ((bf16[8,256,128]{2,1,0:T(8,128)(2,1)}), bf16[8,256,128]{2,1,0:T(8,128)(2,1)}, u32[]{:S(2)}, u32[]{:S(2)}) async-start(bf16[8,256,128]{2,1,0:T(8,128)(2,1)} %back_projection.1), calls=%async_computation.1 | async-start | bytes 1048576 | tf_op jit(solution)/shard_map/all_to_all | solution.py:606
  66.3 1.0 copy-start.9
  70.7 18.6 %copy-start.3 = (bf16[256,1024]{1,0:T(8,128)(2,1)S(1)}, bf16[256,1024]{1,0:T(8,128)(2,1)}, u32[]{:S(2)}) copy-start(bf16[256,1024]{1,0:T(8,128)(2,1)} %weight_ref.3) | copy-start | bytes 1572868
  76.1 13.2 %all-to-all-start.2 = ((bf16[8,256,128]{2,1,0:T(8,128)(2,1)}), bf16[8,256,128]{2,1,0:T(8,128)(2,1)S(1)}, u32[]{:S(2)}, u32[]{:S(2)}) async-start(bf16[8,256,128]{2,1,0:T(8,128)(2,1)} %mix_attention.1), calls=%async_computation.2 | async-start | bytes 1048576 | tf_op jit(solution)/shard_map/all_to_all | solution.py:606
  89.3 10.5 %copy-start.4 = (bf16[4096,128]{1,0:T(8,128)(2,1)S(1)}, bf16[4096,128]{1,0:T(8,128)(2,1)}, u32[]{:S(2)}) copy-start(bf16[4096,128]{1,0:T(8,128)(2,1)} %get-tuple-element.62.mine_ref) | copy-start | bytes 3145732
  89.3 9.0 %collective-permute-start.5 = (bf16[4096,128]{1,0:T(8,128)(2,1)}, bf16[4096,128]{1,0:T(8,128)(2,1)S(1)}, u32[]{:S(2)}, u32[]{:S(2)}) collective-permute-start(bf16[4096,128]{1,0:T(8,128)(2,1)} %get-tuple-element.63), channel_id=1, source_target_pairs={{0,4},{4,0},{8,12},{12,8},{16,20},{20,16},{24,28},{28,24},{1,5},{5... | collective-permute-start | bytes 3145736 | tf_op jit(solution)/shard_map/ppermute | solution.py:602
  90.9 0.8 copy-start.5
  91.7 4.4 %collective-permute-start.6 = (bf16[128,1024]{1,0:T(8,128)(2,1)S(1)}, bf16[128,1024]{1,0:T(8,128)(2,1)S(1)}, u32[]{:S(2)}, u32[]{:S(2)}) collective-permute-start(bf16[128,1024]{1,0:T(8,128)(2,1)S(1)} %get-tuple-element.70), channel_id=1, source_target_pairs={{0,4},{4,0},{8,12},{12,8},{16,20},{20,16},{24,28},{28,24},{1,5},{5... | collective-permute-start | bytes 786440 | tf_op jit(solution)/shard_map/ppermute | solution.py:602
  92.2 28.3 %collective-permute-start.10 = (bf16[1024,256]{1,0:T(8,128)(2,1)S(1)}, bf16[1024,256]{1,0:T(8,128)(2,1)S(1)}, u32[]{:S(2)}, u32[]{:S(2)}) collective-permute-start(bf16[1024,256]{1,0:T(8,128)(2,1)S(1)} %get-tuple-element.72), channel_id=1, source_target_pairs={{0,1},{1,2},{2,3},{3,0},{4,5},{5,6},{6,7},{7,4},{8,9},{9,10},{10,1... | collective-permute-start | bytes 1572872 | tf_op jit(solution)/shard_map/ppermute | solution.py:611
  92.9 27.6 %collective-permute-start.11 = (bf16[1024,256]{1,0:T(8,128)(2,1)S(1)}, bf16[1024,256]{1,0:T(8,128)(2,1)S(1)}, u32[]{:S(2)}, u32[]{:S(2)}) collective-permute-start(bf16[1024,256]{1,0:T(8,128)(2,1)S(1)} %get-tuple-element.73), channel_id=1, source_target_pairs={{0,3},{1,0},{2,1},{3,2},{4,7},{5,4},{6,5},{7,6},{8,11},{9,8},{10,9... | collective-permute-start | bytes 1572872 | tf_op jit(solution)/shard_map/ppermute | solution.py:611
  96.1 24.3 %collective-permute-start.9 = (bf16[128,1024]{1,0:T(8,128)(2,1)S(1)}, bf16[128,1024]{1,0:T(8,128)(2,1)S(1)}, u32[]{:S(2)}, u32[]{:S(2)}) collective-permute-start(bf16[128,1024]{1,0:T(8,128)(2,1)S(1)} %add_convert_fusion.3), channel_id=1, source_target_pairs={{0,24},{4,28},{8,16},{12,20},{16,8},{20,12},{24,0},{28,4},{1,25},{... | collective-permute-start | bytes 786440 | tf_op jit(solution)/shard_map/ppermute | solution.py:602
  96.8 23.7 %collective-permute-start.8 = (bf16[128,1024]{1,0:T(8,128)(2,1)S(1)}, bf16[128,1024]{1,0:T(8,128)(2,1)S(1)}, u32[]{:S(2)}, u32[]{:S(2)}) collective-permute-start(bf16[128,1024]{1,0:T(8,128)(2,1)S(1)} %add_convert_fusion.3), channel_id=1, source_target_pairs={{0,16},{4,20},{8,24},{12,28},{16,0},{20,4},{24,8},{28,12},{1,17},{... | collective-permute-start | bytes 786440 | tf_op jit(solution)/shard_map/ppermute | solution.py:602
  98.2 22.3 %collective-permute-start.7 = (bf16[128,1024]{1,0:T(8,128)(2,1)S(1)}, bf16[128,1024]{1,0:T(8,128)(2,1)S(1)}, u32[]{:S(2)}, u32[]{:S(2)}) collective-permute-start(bf16[128,1024]{1,0:T(8,128)(2,1)S(1)} %add_convert_fusion.3), channel_id=1, source_target_pairs={{0,8},{4,12},{8,0},{12,4},{16,24},{20,28},{24,16},{28,20},{1,9},{5... | collective-permute-start | bytes 786440 | tf_op jit(solution)/shard_map/ppermute | solution.py:602
  120.5 4.0 %copy-start.10 = (bf16[128,1024]{1,0:T(8,128)(2,1)}, bf16[128,1024]{1,0:T(8,128)(2,1)S(1)}, u32[]{:S(2)}) copy-start(bf16[128,1024]{1,0:T(8,128)(2,1)S(1)} %collective-permute-done.8) | copy-start | bytes 786436
  120.5 4.0 %copy-start.11 = (bf16[128,1024]{1,0:T(8,128)(2,1)}, bf16[128,1024]{1,0:T(8,128)(2,1)S(1)}, u32[]{:S(2)}) copy-start(bf16[128,1024]{1,0:T(8,128)(2,1)S(1)} %collective-permute-done.7) | copy-start | bytes 786436
  120.5 2.7 %collective-permute-start.13 = (bf16[4096,128]{1,0:T(8,128)(2,1)S(1)}, bf16[4096,128]{1,0:T(8,128)(2,1)S(1)}, u32[]{:S(2)}, u32[]{:S(2)}) collective-permute-start(bf16[4096,128]{1,0:T(8,128)(2,1)S(1)} %get-tuple-element.79), channel_id=1, source_target_pairs={{0,4},{4,0},{8,12},{12,8},{16,20},{20,16},{24,28},{28,24},{1,5},{5... | collective-permute-start | bytes 3145736 | tf_op jit(solution)/shard_map/ppermute | solution.py:602
  120.6 25.1 %collective-permute-start.12 = (bf16[1024,256]{1,0:T(8,128)(2,1)}, bf16[1024,256]{1,0:T(8,128)(2,1)}, u32[]{:S(2)}, u32[]{:S(2)}) collective-permute-start(bf16[1024,256]{1,0:T(8,128)(2,1)} %get-tuple-element.78), channel_id=1, source_target_pairs={{0,2},{1,3},{2,0},{3,1},{4,6},{5,7},{6,4},{7,5},{8,10},{9,11},{10,... | collective-permute-start | bytes 1572872 | tf_op jit(solution)/shard_map/ppermute | solution.py:611
  124.5 21.2 %copy-start.6 = (bf16[1024,256]{1,0:T(8,128)(2,1)S(1)}, bf16[1024,256]{1,0:T(8,128)(2,1)}, u32[]{:S(2)}) copy-start(bf16[1024,256]{1,0:T(8,128)(2,1)} %copy-done.5) | copy-start | bytes 1572868
  124.5 23.3 %all-to-all-start.3 = ((bf16[8,512,128]{2,1,0:T(8,128)(2,1)}), bf16[8,512,128]{2,1,0:T(8,128)(2,1)S(1)}, u32[]{:S(2)}, u32[]{:S(2)}) async-start(bf16[8,512,128]{2,1,0:T(8,128)(2,1)} %bitcast), calls=%async_computation.3 | async-start | bytes 2097152 | tf_op jit(solution)/shard_map/all_to_all | solution.py:606
  129.4 1.6 %collective-permute-start.14 = (bf16[128,1024]{1,0:T(8,128)(2,1)S(1)}, bf16[128,1024]{1,0:T(8,128)(2,1)S(1)}, u32[]{:S(2)}, u32[]{:S(2)}) collective-permute-start(bf16[128,1024]{1,0:T(8,128)(2,1)S(1)} %add_convert_fusion.2), channel_id=1, source_target_pairs={{0,4},{4,0},{8,12},{12,8},{16,20},{20,16},{24,28},{28,24},{1,5},{5... | collective-permute-start | bytes 786440 | tf_op jit(solution)/shard_map/ppermute | solution.py:602
  147.8 1.0 copy-start.8

commit v2 on v1

--- a/solution.py
+++ b/solution.py
@@ -272,27 +272,26 @@
     return jnp.where(high, share * own + (1.0 - share) * peer, 0.0)
 
 
-def mix_attention_kernel(own_ref, peer_ref, att_ref):
-    pieces = att_ref.shape[0]
-    rows = own_ref.shape[0] // pieces
-    half = rows // 2
+def mix_attention_kernel(own_ref, peer_ref, grad_ref, out_ref):
+    pieces, half, _ = grad_ref.shape
+    rows = 2 * half
     for i in range(pieces):
         own = own_ref[i * rows : (i + 1) * rows]
         peer = peer_ref[i * rows : (i + 1) * rows]
         combined = combined_rows(own, peer, share_of(own, peer))
-        att_ref[i] = (pltpu.roll(combined[:half], DH, 1) + combined[half:]).astype(BF16)
-
-
-def mix_grad_kernel(own_ref, peer_ref, grad_ref, grad_own, grad_peer):
-    pieces = grad_ref.shape[0]
-    rows = own_ref.shape[0] // pieces
+        out_ref[i, :half] = (pltpu.roll(combined[:half], DH, 1) + combined[half:]).astype(BF16)
+        out_ref[i, half:] = grad_ref[i]
+
+
+def mix_grad_kernel(own_ref, peer_ref, both_ref, grad_own, grad_peer):
+    pieces, rows, _ = both_ref.shape
     for i in range(pieces):
         at = slice(i * rows, (i + 1) * rows)
         own = own_ref[at]
         peer = peer_ref[at]
         share = share_of(own, peer)
         combined = combined_rows(own, peer, share)
-        packed = grad_ref[i].astype(F32)
+        packed = both_ref[i, rows // 2 :].astype(F32)
         grad = jnp.concatenate([pltpu.roll(packed, DH, 1), packed], axis=0)
         column = lane_of((LANES, LANES))
         inner = split_sum(grad * combined, (column < DH).astype(BF16))
@@ -301,32 +300,27 @@
         grad_peer[at] = ((1.0 - share) * both).astype(BF16)
 
 
-def mixing(home, peer, grad=None):
-    half = peer.shape[0]
-    pieces = lax.axis_size("seq")
-    rows = half // pieces
-    by_rows = pl.BlockSpec((4 * rows, LANES), lambda g: (g, 0))
-    packed = pl.BlockSpec((4, rows // 2, LANES), lambda g: (g, 0, 0))
-    cost = pl.CostEstimate(flops=0, bytes_accessed=10 * MIB, transcendentals=0)
-    if grad is None:
-        return pl.pallas_call(
-            mix_attention_kernel,
-            grid=(pieces // 4,),
-            out_shape=jax.ShapeDtypeStruct((pieces, rows // 2, LANES), BF16),
-            in_specs=[by_rows, by_rows],
-            out_specs=packed,
-            cost_estimate=cost,
-            name="mix_attention",
-        )(home, peer)
+def mix_attention(home, peer, grad):
+    pieces, rows, _ = grad.shape
+    return pl.pallas_call(
+        mix_attention_kernel,
+        out_shape=jax.ShapeDtypeStruct((pieces, 2 * rows, LANES), BF16),
+        in_specs=[whole(pltpu.VMEM)] * 3,
+        out_specs=whole(pltpu.VMEM),
+        compiler_params=pltpu.CompilerParams(vmem_limit_bytes=12 * MIB),
+        name="mix_attention",
+    )(home, peer, grad)
+
+
+def mix_grad(home, peer, both):
     return pl.pallas_call(
         mix_grad_kernel,
-        grid=(pieces // 4,),
-        out_shape=[jax.ShapeDtypeStruct((half, LANES), BF16)] * 2,
-        in_specs=[by_rows, by_rows, packed],
-        out_specs=[by_rows, by_rows],
-        cost_estimate=cost,
+        out_shape=[jax.ShapeDtypeStruct(home.shape, BF16)] * 2,
+        in_specs=[whole(pltpu.VMEM)] * 3,
+        out_specs=[whole(pltpu.VMEM)] * 2,
+        compiler_params=pltpu.CompilerParams(vmem_limit_bytes=12 * MIB),
         name="mix_grad",
-    )(home, peer, grad)
+    )(home, peer, both)
 
 
 def pack_kernel(query_ref, value_ref, slot_ref, out_ref):
@@ -366,6 +360,8 @@
     return pl.pallas_call(
         unpack_kernel,
         out_shape=[jax.ShapeDtypeStruct((count, heads * DH), BF16)] * 2,
+        in_specs=[whole(pltpu.VMEM)],
+        compiler_params=pltpu.CompilerParams(vmem_limit_bytes=10 * MIB),
         name="unpack_heads",
     )(rows)
 
@@ -413,7 +409,7 @@
     for h in range(width // DH):
         columns = slice(h * DH, (h + 1) * DH)
         for c in range(2):
-            packed = packed_ref[2 * h + c]
+            packed = packed_ref[2 * h + c, :quarter]
             att_ref[2 * c * quarter : (2 * c + 1) * quarter, columns] = packed[:, :DH]
             att_ref[(2 * c + 1) * quarter : (2 * c + 2) * quarter, columns] = packed[:, DH:]
     for k in range(groups):
@@ -422,8 +418,8 @@
 
 
 def project(weight, packed):
-    count, quarter, _ = packed.shape
-    rows, width = 4 * quarter, count * DH // 2
+    count, double, _ = packed.shape
+    rows, width = 2 * double, count * DH // 2
     groups = weight.shape[1] // width
     return pl.pallas_call(
         project_kernel,
@@ -431,6 +427,24 @@
         compiler_params=pltpu.CompilerParams(vmem_limit_bytes=10 * MIB),
         name="project",
     )(weight, packed)
+
+
+def add_kernel(*refs):
+    *shares, out_ref = refs
+    total = shares[0][...].astype(F32)
+    for share in shares[1:]:
+        total += share[...].astype(F32)
+    out_ref[...] = total.astype(BF16)
+
+
+def add_shares(shares):
+    return pl.pallas_call(
+        add_kernel,
+        out_shape=jax.ShapeDtypeStruct(shares[0].shape, BF16),
+        in_specs=[whole(pltpu.VMEM)] * len(shares),
+        compiler_params=pltpu.CompilerParams(vmem_limit_bytes=8 * MIB),
+        name="add_shares",
+    )(*shares)
 
 
 def weight_grad_kernel(att_ref, *refs):
@@ -630,20 +644,18 @@
 
     first = rotate(out_grad, 1)
     grads = [out_grad, first, rotate(first, 1), rotate(out_grad, groups - 1)]
-    mine = after(mine, *grads[1:3])
+    mine = after(mine, first)
 
     home, away, prob, query_key, value_one = forward(places[0], mine, swap(mine), *places[1:])
     away, *grads = after([away, *grads])
     peer = swap(away)
 
-    grad_half = to_all(back_projection(w_out, grads))
-    att_half, grad_half = after([mixing(home, peer), grad_half])
-    att_packed = to_all(att_half)
-    grad_own, grad_peer = mixing(home, peer, grad_half)
-    grad_peer, att_packed = after([grad_peer, att_packed])
+    grad_packed = back_projection(w_out, grads)
+    both = to_all(mix_attention(home, peer, grad_packed))
+    grad_own, grad_peer = mix_grad(home, peer, both)
     grad_other = swap(grad_peer)
 
-    att, *shares = project(w_out, att_packed)
+    att, *shares = project(w_out, both)
     early = [rotate(shares[k], k) for k in range(1, groups, 2)]
     weight, give = weight_grad(att, grads)
     weight = (weight.astype(F32) + swap(give).astype(F32)).astype(BF16)

time: 152 us -> 139 us (0.914)
  blocking collectives: 0 us -> 17.9 us
  waiting for transfers between devices: 51.1 us -> 34.4 us
  Pallas kernels: 62.3 us -> 55.5 us
  starting transfers between devices: 26.8 us -> 22.6 us
  local copies, waits for them, and re-layouts: 4.78 us -> 1.56 us
    all_to_all x4 -> x2, waiting for transfers between devices: 18.8 us -> 0.01 us  [to_all(): return lax.all_to_all(value, 'seq', split_axis=0, concat_axis=0, tiled=True)]
    all_to_all x0 -> x1, blocking collectives: none -> 17.9 us  [to_all(): return lax.all_to_all(value, 'seq', split_axis=0, concat_axis=0, tiled=True)]
    all_to_all x4 -> x2, starting transfers between devices: 15.1 us -> 8.73 us  [to_all(): return lax.all_to_all(value, 'seq', split_axis=0, concat_axis=0, tiled=True)]
    pallas_call x2, Pallas kernels: 8.23 us -> 3.69 us  [the longest x1 2.28 us: mix_grad(): pl.pallas_call(mix_grad_kernel, out_shape=[jax.ShapeDtypeStruct(home.shap...]
    unnamed x24 -> x10, local copies, waits for them, and re-layouts: 4.78 us -> 1.56 us
    ppermute x6, waiting for transfers between devices: 27 us -> 29.4 us  [rotate(): lax.ppermute(value, 'head', [(i, (i + step) % count) for i in range(count)])]
    ppermute x6, starting transfers between devices: 6.98 us -> 9.02 us  [rotate(): lax.ppermute(value, 'head', [(i, (i + step) % count) for i in range(count)])]
  transfers between devices with their start and end apart: 19 -> 17, of which waited for: 9 -> 6; matrix products, arithmetic and copies ran while one was open for 4% -> 4% of each run, Pallas kernels for 39% -> 35%
where the time goes in v2:
time: 139 us; the launch traced here: 138 us
  Pallas kernels  55.5 us (40%)
  waiting for transfers between devices  34.4 us (25%)
  starting transfers between devices  22.6 us (16%)
  blocking collectives  17.9 us (13%)
  other arithmetic  5.73 us (4%)
  local copies, waits for them, and re-layouts  1.56 us (1%)
    ppermute x6, waiting for transfers between devices, rotate(): lax.ppermute(value, 'head', [(i, (i + step) % count) for i in range(count)])  29.4 us
    pallas_call x1, Pallas kernels, forward(): pl.pallas_call(forward_kernel, grid=(blocks // GROUP,), out_shape=[jax.Sh...  22.7 us
    pallas_call x1, Pallas kernels, backward(): pl.pallas_call(backward_kernel, grid=(blocks // GROUP,), out_shape=[jax.S...  20.7 us
    all_to_all x1, blocking collectives, to_all(): return lax.all_to_all(value, 'seq', split_axis=0, concat_axis=0, tiled=True)  17.9 us
    ppermute x6, starting transfers between devices, rotate(): lax.ppermute(value, 'head', [(i, (i + step) % count) for i in range(count)])  9.02 us
    all_to_all x2, starting transfers between devices, to_all(): return lax.all_to_all(value, 'seq', split_axis=0, concat_axis=0, tiled=True)  8.73 us
    ppermute x9, waiting for transfers between devices, swap(): return lax.ppermute(value, 'seq', [(i, i ^ distance) for i in range(count)])  5.03 us
    ppermute x9, starting transfers between devices, swap(): return lax.ppermute(value, 'seq', [(i, i ^ distance) for i in range(count)])  4.82 us
  transfers between devices with their start and end apart: 17, of which 6 were waited for; matrix products, arithmetic and copies ran while one was open for 4% of the time, Pallas kernels for 35%

profile of v2, /device:TPU:0, one launch (start us, length us, event | category | flops | bytes accessed | tf_op | source)
XLA Modules:
  0.0 138.4 jit_solution(14659966094770307948)
XLA Ops:
  0.7 0.8 copy-done.2
  1.5 2.5 %pack_heads.1 = bf16[8,528,128]{2,1,0:T(8,128)(2,1)} custom-call(bf16[1024,256]{1,0:T(8,128)(2,1)} %query_ref.1, bf16[1024,256]{1,0:T(8,128)(2,1)} %value_ref.1, s32[2,4,1024]{2,1,0:T(4,128)S(1)} %copy-done.2), custom_call_target="tpu_custom_call" | custom-call | tf_op jit(solution)/shard_map/pack_heads/pallas_call | solution.py:343
  4.0 5.2 %all-to-all-start = ((bf16[8,528,128]{2,1,0:T(8,128)(2,1)}), bf16[8,528,128]{2,1,0:T(8,128)(2,1)S(1)}, u32[]{:S(2)}, u32[]{:S(2)}) async-start(bf16[8,528,128]{2,1,0:T(8,128)(2,1)} %pack_heads.1), calls=%async_computation | async-start | bytes 2162688 | tf_op jit(solution)/shard_map/all_to_all | solution.py:620
  9.2 0.0 copy-start
  9.2 1.6 %collective-permute-start = (bf16[1024,256]{1,0:T(8,128)(2,1)S(1)}, bf16[1024,256]{1,0:T(8,128)(2,1)S(1)}, u32[]{:S(2)}, u32[]{:S(2)}) collective-permute-start(bf16[1024,256]{1,0:T(8,128)(2,1)S(1)} %copy-done.1), channel_id=1, source_target_pairs={{0,1},{1,2},{2,3},{3,0},{4,5},{5,6},{6,7},{7,4},{8,9},{9,10},{10,1... | collective-permute-start | bytes 1572872 | tf_op jit(solution)/shard_map/ppermute | solution.py:625
  10.8 14.6 %collective-permute-done.refs_1_ = bf16[1024,256]{1,0:T(8,128)(2,1)S(1)} collective-permute-done((bf16[1024,256]{1,0:T(8,128)(2,1)S(1)}, bf16[1024,256]{1,0:T(8,128)(2,1)S(1)}, u32[]{:S(2)}, u32[]{:S(2)}) %collective-permute-start) | collective-permute-done | bytes 524320 | tf_op jit(solution)/shard_map/ppermute | solution.py:625
  25.4 3.1 %collective-permute-start.3 = (bf16[1024,256]{1,0:T(8,128)(2,1)S(1)}, bf16[1024,256]{1,0:T(8,128)(2,1)S(1)}, u32[]{:S(2)}, u32[]{:S(2)}) collective-permute-start(bf16[1024,256]{1,0:T(8,128)(2,1)S(1)} %copy-done.1), channel_id=1, source_target_pairs={{0,3},{1,0},{2,1},{3,2},{4,7},{5,4},{6,5},{7,6},{8,11},{9,8},{10,9... | collective-permute-start | bytes 1572872 | tf_op jit(solution)/shard_map/ppermute | solution.py:625
  28.5 0.0 collective-permute-start.2
  28.5 1.2 find_places.1
  29.7 22.7 %span_forward.1 = (bf16[4096,128]{1,0:T(8,128)(2,1)S(1)}, bf16[4096,128]{1,0:T(8,128)(2,1)S(1)}, bf16[64,128,256]{2,1,0:T(8,128)(2,1)}, bf16[8192,128]{1,0:T(8,128)(2,1)}, bf16[8192,128]{1,0:T(8,128)(2,1)}) custom-call(s32[64,128]{1,0:T(8,128)S(1)} %get-tuple-element.41.addr_ref, bf16[8,528,128]{2,1,0:T(8,128)(2,1)S(1)} %all-to-all-done.mine_ref, ...), custom_call_target="tpu_custom_call" | custom-call | bytes 67108864 | tf_op jit(solution)/shard_map/span_forward/pallas_call | solution.py:216
  52.4 0.0 collective-permute-done.3.refs_3_
  52.4 0.1 collective-permute-done.2.refs_2_
  52.5 0.2 collective-permute-start.4
  52.7 0.8 back_projection.1.grad_ref
  53.5 1.6 %collective-permute-done.4.peer_ref = bf16[4096,128]{1,0:T(8,128)(2,1)S(1)} collective-permute-done((bf16[4096,128]{1,0:T(8,128)(2,1)S(1)}, bf16[4096,128]{1,0:T(8,128)(2,1)S(1)}, u32[]{:S(2)}, u32[]{:S(2)}) %collective-permute-start.4) | collective-permute-done | bytes 1048608 | tf_op jit(solution)/shard_map/ppermute | solution.py:616
  55.2 1.4 %mix_attention.1 = bf16[8,512,128]{2,1,0:T(8,128)(2,1)S(1)} custom-call(bf16[4096,128]{1,0:T(8,128)(2,1)S(1)} %get-tuple-element.46.own_ref, bf16[4096,128]{1,0:T(8,128)(2,1)S(1)} %collective-permute-done.4.peer_ref, bf16[8,256,128]{2,1,0:T(8,128)(2,1)S(1)} %back_projection.1.grad_ref), custom_call_target="tpu_custom_call" | custom-call | tf_op jit(solution)/shard_map/mix_attention/pallas_call | solution.py:305
  56.6 17.9 %all_to_all.15.packed_ref.both_ref = bf16[8,512,128]{2,1,0:T(8,128)(2,1)S(1)} all-to-all(bf16[8,512,128]{2,1,0:T(8,128)(2,1)S(1)} %mix_attention.1), channel_id=1, replica_groups=mesh['seq'=8,'head'=4] {'seq'}, dimensions={0} | all-to-all | bytes 2097152 | tf_op jit(solution)/shard_map/all_to_all | solution.py:620
  74.5 2.3 %mix_grad.1 = (bf16[4096,128]{1,0:T(8,128)(2,1)S(1)}, bf16[4096,128]{1,0:T(8,128)(2,1)S(1)}) custom-call(bf16[4096,128]{1,0:T(8,128)(2,1)S(1)} %get-tuple-element.46.own_ref, bf16[4096,128]{1,0:T(8,128)(2,1)S(1)} %collective-permute-done.4.peer_ref, bf16[8,512,128]{2,1,0:T(8,128)(2,1)S(1)} %all_to_all.15.packed_ref.both_ref), custom_call_target="tpu_custom_call" | custom-call | tf_op jit(solution)/shard_map/mix_grad/pallas_call | solution.py:316
  76.8 0.1 collective-permute-start.5
  76.8 1.6 %project.1 = (bf16[1024,256]{1,0:T(8,128)(2,1)S(1)}, bf16[1024,256]{1,0:T(8,128)(2,1)S(1)}, bf16[1024,256]{1,0:T(8,128)(2,1)S(1)}, bf16[1024,256]{1,0:T(8,128)(2,1)}, bf16[1024,256]{1,0:T(8,128)(2,1)S(1)}) custom-call(bf16[256,1024]{1,0:T(8,128)(2,1)S(1)} %copy-done, bf16[8,512,128]{2,1,0:T(8,128)(2,1)S(1)} %all_to_all.15.packed_ref.both_ref), custom_call_target="tpu_custom_call" | custom-call | tf_op jit(solution)/shard_map/project/pallas_call | solution.py:424
  78.5 0.8 weight_grad.1
  79.3 0.5 collective-permute-start.6
  79.8 1.5 %collective-permute-start.10 = (bf16[1024,256]{1,0:T(8,128)(2,1)S(1)}, bf16[1024,256]{1,0:T(8,128)(2,1)S(1)}, u32[]{:S(2)}, u32[]{:S(2)}) collective-permute-start(bf16[1024,256]{1,0:T(8,128)(2,1)S(1)} %get-tuple-element.64), channel_id=1, source_target_pairs={{0,1},{1,2},{2,3},{3,0},{4,5},{5,6},{6,7},{7,4},{8,9},{9,10},{10,1... | collective-permute-start | bytes 1572872 | tf_op jit(solution)/shard_map/ppermute | solution.py:625
  81.3 2.3 %collective-permute-start.11 = (bf16[1024,256]{1,0:T(8,128)(2,1)S(1)}, bf16[1024,256]{1,0:T(8,128)(2,1)S(1)}, u32[]{:S(2)}, u32[]{:S(2)}) collective-permute-start(bf16[1024,256]{1,0:T(8,128)(2,1)S(1)} %get-tuple-element.65), channel_id=1, source_target_pairs={{0,3},{1,0},{2,1},{3,2},{4,7},{5,4},{6,5},{7,6},{8,11},{9,8},{10,9... | collective-permute-start | bytes 1572872 | tf_op jit(solution)/shard_map/ppermute | solution.py:625
  83.6 0.0 collective-permute-done.6
  83.6 0.1 add_convert_fusion.3
  83.7 0.6 collective-permute-start.9
  84.3 1.5 %collective-permute-start.8 = (bf16[128,1024]{1,0:T(8,128)(2,1)S(1)}, bf16[128,1024]{1,0:T(8,128)(2,1)S(1)}, u32[]{:S(2)}, u32[]{:S(2)}) collective-permute-start(bf16[128,1024]{1,0:T(8,128)(2,1)S(1)} %add_convert_fusion.3), channel_id=1, source_target_pairs={{0,16},{4,20},{8,24},{12,28},{16,0},{20,4},{24,8},{28,12},{1,17},{... | collective-permute-start | bytes 786440 | tf_op jit(solution)/shard_map/ppermute | solution.py:616
  85.8 0.0 collective-permute-done.5.other_ref
  85.8 1.5 %collective-permute-start.7 = (bf16[128,1024]{1,0:T(8,128)(2,1)S(1)}, bf16[128,1024]{1,0:T(8,128)(2,1)S(1)}, u32[]{:S(2)}, u32[]{:S(2)}) collective-permute-start(bf16[128,1024]{1,0:T(8,128)(2,1)S(1)} %add_convert_fusion.3), channel_id=1, source_target_pairs={{0,8},{4,12},{8,0},{12,4},{16,24},{20,28},{24,16},{28,20},{1,9},{5... | collective-permute-start | bytes 786440 | tf_op jit(solution)/shard_map/ppermute | solution.py:616
  87.3 20.7 %span_backward.1 = (bf16[4096,128]{1,0:T(8,128)(2,1)S(1)}, bf16[4096,128]{1,0:T(8,128)(2,1)S(1)}) custom-call(s32[64,128]{1,0:T(8,128)S(1)} %get-tuple-element.41.addr_ref, bf16[4096,128]{1,0:T(8,128)(2,1)S(1)} %get-tuple-element.54.mine_ref, bf16[4096,128]{1,0:T(8,128)(2,1)S(1)} %collective-permute-done.5.other_ref, ...), custom_call_target="tpu_custom_call" | custom-call | bytes 67108864 | tf_op jit(solution)/shard_map/span_backward/pallas_call | solution.py:582
  108.0 0.0 collective-permute-done.8
  108.0 0.0 copy-start.3
  108.1 0.0 copy-start.4
  108.1 0.0 collective-permute-done.10
  108.1 0.7 copy-done.4
  108.8 0.0 collective-permute-done.11
  108.8 0.4 collective-permute-start.12
  109.3 2.2 %collective-permute-done.13 = bf16[4096,128]{1,0:T(8,128)(2,1)S(1)} collective-permute-done((bf16[4096,128]{1,0:T(8,128)(2,1)S(1)}, bf16[4096,128]{1,0:T(8,128)(2,1)S(1)}, u32[]{:S(2)}, u32[]{:S(2)}) %collective-permute-start.13) | collective-permute-done | bytes 1048608 | tf_op jit(solution)/shard_map/ppermute | solution.py:616
  111.5 1.3 add_convert_fusion
  112.7 3.6 %all-to-all-start.2 = ((bf16[8,512,128]{2,1,0:T(8,128)(2,1)}), bf16[8,512,128]{2,1,0:T(8,128)(2,1)S(1)}, u32[]{:S(2)}, u32[]{:S(2)}) async-start(bf16[8,512,128]{2,1,0:T(8,128)(2,1)} %bitcast), calls=%async_computation.2 | async-start | bytes 2097152 | tf_op jit(solution)/shard_map/all_to_all | solution.py:620
  116.3 1.2 add_convert_fusion.2
  117.5 0.5 collective-permute-start.14
  118.0 1.2 collective-permute-done.14
  119.1 1.1 convert_multiply_fusion
  120.3 14.6 %collective-permute-done.12 = bf16[1024,256]{1,0:T(8,128)(2,1)} collective-permute-done((bf16[1024,256]{1,0:T(8,128)(2,1)}, bf16[1024,256]{1,0:T(8,128)(2,1)}, u32[]{:S(2)}, u32[]{:S(2)}) %collective-permute-start.12) | collective-permute-done | bytes 524320 | tf_op jit(solution)/shard_map/ppermute | solution.py:625
  134.9 2.1 %add_convert_fusion.1 = bf16[1024,256]{1,0:T(8,128)(2,1)} fusion(bf16[1024,256]{1,0:T(8,128)(2,1)} %collective-permute-done.12, bf16[1024,256]{1,0:T(8,128)(2,1)S(1)} %collective-permute-done.11, bf16[1024,256]{1,0:T(8,128)(2,1)S(1)} %collective-permute-done.10, bf16[1024,256]{1,0:T(8,128)(2,1)S(1)} %get-tuple-element.53), kind=kLoop, calls=%fused_computation.2 | loop fusion | flops 2097152 | bytes 2621440 | tf_op jit(solution)/shard_map/convert_element_type | solution.py:688
  137.0 1.4 %unpack_heads.1 = (bf16[1024,256]{1,0:T(8,128)(2,1)}, bf16[1024,256]{1,0:T(8,128)(2,1)}) custom-call(bf16[4,1024,128]{2,1,0:T(8,128)(2,1)S(1)} %bitcast.2), custom_call_target="tpu_custom_call" | custom-call | tf_op jit(solution)/shard_map/unpack_heads/pallas_call | solution.py:360
  (12 shorter events, 0.0 us)
Async XLA Ops:
  0.6 8.5 %copy-start.1 = (bf16[1024,256]{1,0:T(8,128)(2,1)S(1)}, bf16[1024,256]{1,0:T(8,128)(2,1)}, u32[]{:S(2)}) copy-start(bf16[1024,256]{1,0:T(8,128)(2,1)} %refs_0_.1) | copy-start | bytes 1572868
  0.6 0.8 copy-start.2
  4.0 21.4 %all-to-all-start = ((bf16[8,528,128]{2,1,0:T(8,128)(2,1)}), bf16[8,528,128]{2,1,0:T(8,128)(2,1)S(1)}, u32[]{:S(2)}, u32[]{:S(2)}) async-start(bf16[8,528,128]{2,1,0:T(8,128)(2,1)} %pack_heads.1), calls=%async_computation | async-start | bytes 2162688 | tf_op jit(solution)/shard_map/all_to_all | solution.py:620
  9.2 43.5 %copy-start = (bf16[256,1024]{1,0:T(8,128)(2,1)S(1)}, bf16[256,1024]{1,0:T(8,128)(2,1)}, u32[]{:S(2)}) copy-start(bf16[256,1024]{1,0:T(8,128)(2,1)} %weight_ref.3) | copy-start | bytes 1572868
  9.2 16.2 %collective-permute-start = (bf16[1024,256]{1,0:T(8,128)(2,1)S(1)}, bf16[1024,256]{1,0:T(8,128)(2,1)S(1)}, u32[]{:S(2)}, u32[]{:S(2)}) collective-permute-start(bf16[1024,256]{1,0:T(8,128)(2,1)S(1)} %copy-done.1), channel_id=1, source_target_pairs={{0,1},{1,2},{2,3},{3,0},{4,5},{5,6},{6,7},{7,4},{8,9},{9,10},{10,1... | collective-permute-start | bytes 1572872 | tf_op jit(solution)/shard_map/ppermute | solution.py:625
  25.4 4.3 %collective-permute-start.1 = (bf16[8,528,128]{2,1,0:T(8,128)(2,1)S(1)}, bf16[8,528,128]{2,1,0:T(8,128)(2,1)S(1)}, u32[]{:S(2)}, u32[]{:S(2)}) collective-permute-start(bf16[8,528,128]{2,1,0:T(8,128)(2,1)S(1)} %all-to-all-done.mine_ref), channel_id=1, source_target_pairs={{0,4},{4,0},{8,12},{12,8},{16,20},{20,16},{24,28},{28,24},{1,5},{5... | collective-permute-start | bytes 3244040 | tf_op jit(solution)/shard_map/ppermute | solution.py:616
  25.4 27.0 %collective-permute-start.3 = (bf16[1024,256]{1,0:T(8,128)(2,1)S(1)}, bf16[1024,256]{1,0:T(8,128)(2,1)S(1)}, u32[]{:S(2)}, u32[]{:S(2)}) collective-permute-start(bf16[1024,256]{1,0:T(8,128)(2,1)S(1)} %copy-done.1), channel_id=1, source_target_pairs={{0,3},{1,0},{2,1},{3,2},{4,7},{5,4},{6,5},{7,6},{8,11},{9,8},{10,9... | collective-permute-start | bytes 1572872 | tf_op jit(solution)/shard_map/ppermute | solution.py:625
  28.5 24.0 %collective-permute-start.2 = (bf16[1024,256]{1,0:T(8,128)(2,1)S(1)}, bf16[1024,256]{1,0:T(8,128)(2,1)S(1)}, u32[]{:S(2)}, u32[]{:S(2)}) collective-permute-start(bf16[1024,256]{1,0:T(8,128)(2,1)S(1)} %collective-permute-done.refs_1_), channel_id=1, source_target_pairs={{0,1},{1,2},{2,3},{3,0},{4,5},{5,6},{6,7},{7,4},{8,9},{9,10},{10,1... | collective-permute-start | bytes 1572872 | tf_op jit(solution)/shard_map/ppermute | solution.py:625
  52.5 2.7 %collective-permute-start.4 = (bf16[4096,128]{1,0:T(8,128)(2,1)S(1)}, bf16[4096,128]{1,0:T(8,128)(2,1)S(1)}, u32[]{:S(2)}, u32[]{:S(2)}) collective-permute-start(bf16[4096,128]{1,0:T(8,128)(2,1)S(1)} %get-tuple-element.48), channel_id=1, source_target_pairs={{0,4},{4,0},{8,12},{12,8},{16,20},{20,16},{24,28},{28,24},{1,5},{5... | collective-permute-start | bytes 3145736 | tf_op jit(solution)/shard_map/ppermute | solution.py:616
  76.8 9.0 %collective-permute-start.5 = (bf16[4096,128]{1,0:T(8,128)(2,1)S(1)}, bf16[4096,128]{1,0:T(8,128)(2,1)S(1)}, u32[]{:S(2)}, u32[]{:S(2)}) collective-permute-start(bf16[4096,128]{1,0:T(8,128)(2,1)S(1)} %get-tuple-element.55), channel_id=1, source_target_pairs={{0,4},{4,0},{8,12},{12,8},{16,20},{20,16},{24,28},{28,24},{1,5},{5... | collective-permute-start | bytes 3145736 | tf_op jit(solution)/shard_map/ppermute | solution.py:616
  79.3 4.4 %collective-permute-start.6 = (bf16[128,1024]{1,0:T(8,128)(2,1)S(1)}, bf16[128,1024]{1,0:T(8,128)(2,1)S(1)}, u32[]{:S(2)}, u32[]{:S(2)}) collective-permute-start(bf16[128,1024]{1,0:T(8,128)(2,1)S(1)} %get-tuple-element.62), channel_id=1, source_target_pairs={{0,4},{4,0},{8,12},{12,8},{16,20},{20,16},{24,28},{28,24},{1,5},{5... | collective-permute-start | bytes 786440 | tf_op jit(solution)/shard_map/ppermute | solution.py:616
  79.8 28.3 %collective-permute-start.10 = (bf16[1024,256]{1,0:T(8,128)(2,1)S(1)}, bf16[1024,256]{1,0:T(8,128)(2,1)S(1)}, u32[]{:S(2)}, u32[]{:S(2)}) collective-permute-start(bf16[1024,256]{1,0:T(8,128)(2,1)S(1)} %get-tuple-element.64), channel_id=1, source_target_pairs={{0,1},{1,2},{2,3},{3,0},{4,5},{5,6},{6,7},{7,4},{8,9},{9,10},{10,1... | collective-permute-start | bytes 1572872 | tf_op jit(solution)/shard_map/ppermute | solution.py:625
  81.3 27.5 %collective-permute-start.11 = (bf16[1024,256]{1,0:T(8,128)(2,1)S(1)}, bf16[1024,256]{1,0:T(8,128)(2,1)S(1)}, u32[]{:S(2)}, u32[]{:S(2)}) collective-permute-start(bf16[1024,256]{1,0:T(8,128)(2,1)S(1)} %get-tuple-element.65), channel_id=1, source_target_pairs={{0,3},{1,0},{2,1},{3,2},{4,7},{5,4},{6,5},{7,6},{8,11},{9,8},{10,9... | collective-permute-start | bytes 1572872 | tf_op jit(solution)/shard_map/ppermute | solution.py:625
  83.7 24.3 %collective-permute-start.9 = (bf16[128,1024]{1,0:T(8,128)(2,1)S(1)}, bf16[128,1024]{1,0:T(8,128)(2,1)S(1)}, u32[]{:S(2)}, u32[]{:S(2)}) collective-permute-start(bf16[128,1024]{1,0:T(8,128)(2,1)S(1)} %add_convert_fusion.3), channel_id=1, source_target_pairs={{0,24},{4,28},{8,16},{12,20},{16,8},{20,12},{24,0},{28,4},{1,25},{... | collective-permute-start | bytes 786440 | tf_op jit(solution)/shard_map/ppermute | solution.py:616
  84.3 23.7 %collective-permute-start.8 = (bf16[128,1024]{1,0:T(8,128)(2,1)S(1)}, bf16[128,1024]{1,0:T(8,128)(2,1)S(1)}, u32[]{:S(2)}, u32[]{:S(2)}) collective-permute-start(bf16[128,1024]{1,0:T(8,128)(2,1)S(1)} %add_convert_fusion.3), channel_id=1, source_target_pairs={{0,16},{4,20},{8,24},{12,28},{16,0},{20,4},{24,8},{28,12},{1,17},{... | collective-permute-start | bytes 786440 | tf_op jit(solution)/shard_map/ppermute | solution.py:616
  85.8 22.2 %collective-permute-start.7 = (bf16[128,1024]{1,0:T(8,128)(2,1)S(1)}, bf16[128,1024]{1,0:T(8,128)(2,1)S(1)}, u32[]{:S(2)}, u32[]{:S(2)}) collective-permute-start(bf16[128,1024]{1,0:T(8,128)(2,1)S(1)} %add_convert_fusion.3), channel_id=1, source_target_pairs={{0,8},{4,12},{8,0},{12,4},{16,24},{20,28},{24,16},{28,20},{1,9},{5... | collective-permute-start | bytes 786440 | tf_op jit(solution)/shard_map/ppermute | solution.py:616
  108.0 4.7 %copy-start.3 = (bf16[128,1024]{1,0:T(8,128)(2,1)}, bf16[128,1024]{1,0:T(8,128)(2,1)S(1)}, u32[]{:S(2)}) copy-start(bf16[128,1024]{1,0:T(8,128)(2,1)S(1)} %collective-permute-done.8) | copy-start | bytes 786436
  108.1 0.8 copy-start.4
  108.8 2.7 %collective-permute-start.13 = (bf16[4096,128]{1,0:T(8,128)(2,1)S(1)}, bf16[4096,128]{1,0:T(8,128)(2,1)S(1)}, u32[]{:S(2)}, u32[]{:S(2)}) collective-permute-start(bf16[4096,128]{1,0:T(8,128)(2,1)S(1)} %get-tuple-element.71), channel_id=1, source_target_pairs={{0,4},{4,0},{8,12},{12,8},{16,20},{20,16},{24,28},{28,24},{1,5},{5... | collective-permute-start | bytes 3145736 | tf_op jit(solution)/shard_map/ppermute | solution.py:616
  108.8 26.1 %collective-permute-start.12 = (bf16[1024,256]{1,0:T(8,128)(2,1)}, bf16[1024,256]{1,0:T(8,128)(2,1)}, u32[]{:S(2)}, u32[]{:S(2)}) collective-permute-start(bf16[1024,256]{1,0:T(8,128)(2,1)} %get-tuple-element.70), channel_id=1, source_target_pairs={{0,2},{1,3},{2,0},{3,1},{4,6},{5,7},{6,4},{7,5},{8,10},{9,11},{10,... | collective-permute-start | bytes 1572872 | tf_op jit(solution)/shard_map/ppermute | solution.py:625
  112.7 24.2 %all-to-all-start.2 = ((bf16[8,512,128]{2,1,0:T(8,128)(2,1)}), bf16[8,512,128]{2,1,0:T(8,128)(2,1)S(1)}, u32[]{:S(2)}, u32[]{:S(2)}) async-start(bf16[8,512,128]{2,1,0:T(8,128)(2,1)} %bitcast), calls=%async_computation.2 | async-start | bytes 2097152 | tf_op jit(solution)/shard_map/all_to_all | solution.py:620
  117.5 1.6 %collective-permute-start.14 = (bf16[128,1024]{1,0:T(8,128)(2,1)S(1)}, bf16[128,1024]{1,0:T(8,128)(2,1)S(1)}, u32[]{:S(2)}, u32[]{:S(2)}) collective-permute-start(bf16[128,1024]{1,0:T(8,128)(2,1)S(1)} %add_convert_fusion.2), channel_id=1, source_target_pairs={{0,4},{4,0},{8,12},{12,8},{16,20},{20,16},{24,28},{28,24},{1,5},{5... | collective-permute-start | bytes 786440 | tf_op jit(solution)/shard_map/ppermute | solution.py:616

commit v3 on v2

--- a/solution.py
+++ b/solution.py
@@ -25,10 +25,6 @@
 
 def in_hbm(value):
     return pltpu.with_memory_space_constraint(value, pltpu.HBM)
-
-
-def fixed(shape):
-    return pl.BlockSpec(shape, lambda g: (0,) * len(shape), pipeline_mode=pl.Buffered(1))
 
 
 def lane_of(shape):
@@ -225,15 +221,15 @@
         ],
         in_specs=[
             whole(pltpu.SMEM),
-            fixed(mine.shape),
-            fixed(mine.shape),
+            whole(pltpu.VMEM),
+            whole(pltpu.VMEM),
             pl.BlockSpec((GROUP, 1, 2 * SPAN), lambda g: (g, 0, 0)),
             pl.BlockSpec((1, SPAN, GROUP), lambda g: (g, 0, 0)),
             pl.BlockSpec((1, SPAN, GROUP), lambda g: (g, 0, 0)),
         ],
         out_specs=[
-            fixed((half, LANES)),
-            fixed((half, LANES)),
+            whole(pltpu.VMEM),
+            whole(pltpu.VMEM),
             pl.BlockSpec((GROUP, SPAN, 2 * SPAN), lambda g: (g, 0, 0)),
             pl.BlockSpec((rows, LANES), lambda g: (g, 0)),
             pl.BlockSpec((rows, LANES), lambda g: (g, 0)),
@@ -345,7 +341,7 @@
         out_shape=jax.ShapeDtypeStruct((rounds * heads, rows // 2 + 16, 2 * DH), BF16),
         compiler_params=pltpu.CompilerParams(vmem_limit_bytes=10 * MIB),
         name="pack_heads",
-    )(in_hbm(queries), in_hbm(values), slots)
+    )(in_hbm(queries), in_hbm(values), in_hbm(slots))
 
 
 def unpack_kernel(in_ref, query_ref, value_ref):
@@ -423,7 +419,9 @@
     groups = weight.shape[1] // width
     return pl.pallas_call(
         project_kernel,
-        out_shape=[jax.ShapeDtypeStruct((rows, width), BF16)] * (1 + groups),
+        out_shape=[jax.ShapeDtypeStruct((rows, width), BF16)] * 3
+        + [pltpu.HBM((rows, width), BF16)]
+        + [jax.ShapeDtypeStruct((rows, width), BF16)] * (groups - 3),
         compiler_params=pltpu.CompilerParams(vmem_limit_bytes=10 * MIB),
         name="project",
     )(weight, packed)
@@ -585,15 +583,15 @@
         out_shape=[jax.ShapeDtypeStruct((half, LANES), BF16)] * 2,
         in_specs=[
             whole(pltpu.SMEM),
-            fixed((half, LANES)),
-            fixed((half, LANES)),
+            whole(pltpu.VMEM),
+            whole(pltpu.VMEM),
             pl.BlockSpec((GROUP, SPAN, 2 * SPAN), lambda g: (g, 0, 0)),
             by_rows,
             before,
             by_rows,
             before,
         ],
-        out_specs=[fixed((half, LANES))] * 2,
+        out_specs=[whole(pltpu.VMEM)] * 2,
         scratch_shapes=[
             pltpu.VMEM((total, LANES), F32),
             pltpu.VMEM((total, LANES), F32),

time: 139 us -> 138 us (level)
  no operation moved by 1% of the time
where the time goes in v3:
time: 138 us
  Pallas kernels  55.6 us (40%)
  waiting for transfers between devices  34.4 us (25%)
  starting transfers between devices  22.5 us (16%)
  blocking collectives  17.9 us (13%)
  other arithmetic  5.74 us (4%)
    ppermute x6, waiting for transfers between devices, rotate(): lax.ppermute(value, 'head', [(i, (i + step) % count) for i in range(count)])  29.4 us
    pallas_call x1, Pallas kernels, forward(): pl.pallas_call(forward_kernel, grid=(blocks // GROUP,), out_shape=[jax.Sh...  22.7 us
    pallas_call x1, Pallas kernels, backward(): pl.pallas_call(backward_kernel, grid=(blocks // GROUP,), out_shape=[jax.S...  20.7 us
    all_to_all x1, blocking collectives, to_all(): return lax.all_to_all(value, 'seq', split_axis=0, concat_axis=0, tiled=True)  17.9 us
    ppermute x6, starting transfers between devices, rotate(): lax.ppermute(value, 'head', [(i, (i + step) % count) for i in range(count)])  8.99 us
    all_to_all x2, starting transfers between devices, to_all(): return lax.all_to_all(value, 'seq', split_axis=0, concat_axis=0, tiled=True)  8.73 us
    ppermute x9, waiting for transfers between devices, swap(): return lax.ppermute(value, 'seq', [(i, i ^ distance) for i in range(count)])  5.07 us
    ppermute x9, starting transfers between devices, swap(): return lax.ppermute(value, 'seq', [(i, i ^ distance) for i in range(count)])  4.82 us
  transfers between devices with their start and end apart: 17, of which 6 were waited for; matrix products, arithmetic and copies ran while one was open for 4% of the time, Pallas kernels for 35%

profile of v3, /device:TPU:0, one launch (start us, length us, event | category | flops | bytes accessed | tf_op | source)
XLA Modules:
  0.0 137.7 jit_solution(17138688378152974673)
XLA Ops:
  0.6 2.6 %pack_heads.1 = bf16[8,528,128]{2,1,0:T(8,128)(2,1)} custom-call(bf16[1024,256]{1,0:T(8,128)(2,1)} %query_ref.1, bf16[1024,256]{1,0:T(8,128)(2,1)} %value_ref.1, s32[2,4,1024]{2,1,0:T(4,128)} %slot_ref.1), custom_call_target="tpu_custom_call" | custom-call | tf_op jit(solution)/shard_map/pack_heads/pallas_call | solution.py:339
  3.2 5.2 %all-to-all-start = ((bf16[8,528,128]{2,1,0:T(8,128)(2,1)}), bf16[8,528,128]{2,1,0:T(8,128)(2,1)S(1)}, u32[]{:S(2)}, u32[]{:S(2)}) async-start(bf16[8,528,128]{2,1,0:T(8,128)(2,1)} %pack_heads.1), calls=%async_computation | async-start | bytes 2162688 | tf_op jit(solution)/shard_map/all_to_all | solution.py:618
  8.4 0.0 copy-start
  8.4 1.6 %collective-permute-start = (bf16[1024,256]{1,0:T(8,128)(2,1)S(1)}, bf16[1024,256]{1,0:T(8,128)(2,1)S(1)}, u32[]{:S(2)}, u32[]{:S(2)}) collective-permute-start(bf16[1024,256]{1,0:T(8,128)(2,1)S(1)} %copy-done.1), channel_id=1, source_target_pairs={{0,1},{1,2},{2,3},{3,0},{4,5},{5,6},{6,7},{7,4},{8,9},{9,10},{10,1... | collective-permute-start | bytes 1572872 | tf_op jit(solution)/shard_map/ppermute | solution.py:623
  10.1 14.6 %collective-permute-done.refs_1_ = bf16[1024,256]{1,0:T(8,128)(2,1)S(1)} collective-permute-done((bf16[1024,256]{1,0:T(8,128)(2,1)S(1)}, bf16[1024,256]{1,0:T(8,128)(2,1)S(1)}, u32[]{:S(2)}, u32[]{:S(2)}) %collective-permute-start) | collective-permute-done | bytes 524320 | tf_op jit(solution)/shard_map/ppermute | solution.py:623
  24.7 0.0 all-to-all-done.mine_ref
  24.7 0.0 collective-permute-start.1
  24.7 3.1 %collective-permute-start.3 = (bf16[1024,256]{1,0:T(8,128)(2,1)S(1)}, bf16[1024,256]{1,0:T(8,128)(2,1)S(1)}, u32[]{:S(2)}, u32[]{:S(2)}) collective-permute-start(bf16[1024,256]{1,0:T(8,128)(2,1)S(1)} %copy-done.1), channel_id=1, source_target_pairs={{0,3},{1,0},{2,1},{3,2},{4,7},{5,4},{6,5},{7,6},{8,11},{9,8},{10,9... | collective-permute-start | bytes 1572872 | tf_op jit(solution)/shard_map/ppermute | solution.py:623
  27.8 1.2 find_places.1
  29.0 0.0 collective-permute-done.1.other_ref
  29.0 22.7 %span_forward.1 = (bf16[4096,128]{1,0:T(8,128)(2,1)S(1)}, bf16[4096,128]{1,0:T(8,128)(2,1)S(1)}, bf16[64,128,256]{2,1,0:T(8,128)(2,1)}, bf16[8192,128]{1,0:T(8,128)(2,1)}, bf16[8192,128]{1,0:T(8,128)(2,1)}) custom-call(s32[64,128]{1,0:T(8,128)S(1)} %get-tuple-element.41.addr_ref, bf16[8,528,128]{2,1,0:T(8,128)(2,1)S(1)} %all-to-all-done.mine_ref, ...), custom_call_target="tpu_custom_call" | custom-call | bytes 67108864 | tf_op jit(solution)/shard_map/span_forward/pallas_call | solution.py:212
  51.6 0.1 collective-permute-done.2.refs_2_
  51.8 0.2 collective-permute-start.4
  52.0 0.8 back_projection.1.grad_ref
  52.8 1.7 %collective-permute-done.4.peer_ref = bf16[4096,128]{1,0:T(8,128)(2,1)S(1)} collective-permute-done((bf16[4096,128]{1,0:T(8,128)(2,1)S(1)}, bf16[4096,128]{1,0:T(8,128)(2,1)S(1)}, u32[]{:S(2)}, u32[]{:S(2)}) %collective-permute-start.4) | collective-permute-done | bytes 1048608 | tf_op jit(solution)/shard_map/ppermute | solution.py:614
  54.4 1.4 %mix_attention.1 = bf16[8,512,128]{2,1,0:T(8,128)(2,1)S(1)} custom-call(bf16[4096,128]{1,0:T(8,128)(2,1)S(1)} %get-tuple-element.46.own_ref, bf16[4096,128]{1,0:T(8,128)(2,1)S(1)} %collective-permute-done.4.peer_ref, bf16[8,256,128]{2,1,0:T(8,128)(2,1)S(1)} %back_projection.1.grad_ref), custom_call_target="tpu_custom_call" | custom-call | tf_op jit(solution)/shard_map/mix_attention/pallas_call | solution.py:301
  55.8 17.9 %all_to_all.15.packed_ref.both_ref = bf16[8,512,128]{2,1,0:T(8,128)(2,1)S(1)} all-to-all(bf16[8,512,128]{2,1,0:T(8,128)(2,1)S(1)} %mix_attention.1), channel_id=1, replica_groups=mesh['seq'=8,'head'=4] {'seq'}, dimensions={0} | all-to-all | bytes 2097152 | tf_op jit(solution)/shard_map/all_to_all | solution.py:618
  73.7 2.3 %mix_grad.1 = (bf16[4096,128]{1,0:T(8,128)(2,1)S(1)}, bf16[4096,128]{1,0:T(8,128)(2,1)S(1)}) custom-call(bf16[4096,128]{1,0:T(8,128)(2,1)S(1)} %get-tuple-element.46.own_ref, bf16[4096,128]{1,0:T(8,128)(2,1)S(1)} %collective-permute-done.4.peer_ref, bf16[8,512,128]{2,1,0:T(8,128)(2,1)S(1)} %all_to_all.15.packed_ref.both_ref), custom_call_target="tpu_custom_call" | custom-call | tf_op jit(solution)/shard_map/mix_grad/pallas_call | solution.py:312
  76.0 0.1 collective-permute-start.5
  76.1 1.6 %project.1 = (bf16[1024,256]{1,0:T(8,128)(2,1)S(1)}, bf16[1024,256]{1,0:T(8,128)(2,1)S(1)}, bf16[1024,256]{1,0:T(8,128)(2,1)S(1)}, bf16[1024,256]{1,0:T(8,128)(2,1)}, bf16[1024,256]{1,0:T(8,128)(2,1)S(1)}) custom-call(bf16[256,1024]{1,0:T(8,128)(2,1)S(1)} %copy-done, bf16[8,512,128]{2,1,0:T(8,128)(2,1)S(1)} %all_to_all.15.packed_ref.both_ref), custom_call_target="tpu_custom_call" | custom-call | tf_op jit(solution)/shard_map/project/pallas_call | solution.py:420
  77.7 0.8 weight_grad.1
  78.5 0.5 collective-permute-start.6
  79.1 1.5 %collective-permute-start.10 = (bf16[1024,256]{1,0:T(8,128)(2,1)S(1)}, bf16[1024,256]{1,0:T(8,128)(2,1)S(1)}, u32[]{:S(2)}, u32[]{:S(2)}) collective-permute-start(bf16[1024,256]{1,0:T(8,128)(2,1)S(1)} %get-tuple-element.64), channel_id=1, source_target_pairs={{0,1},{1,2},{2,3},{3,0},{4,5},{5,6},{6,7},{7,4},{8,9},{9,10},{10,1... | collective-permute-start | bytes 1572872 | tf_op jit(solution)/shard_map/ppermute | solution.py:623
  80.6 2.3 %collective-permute-start.11 = (bf16[1024,256]{1,0:T(8,128)(2,1)S(1)}, bf16[1024,256]{1,0:T(8,128)(2,1)S(1)}, u32[]{:S(2)}, u32[]{:S(2)}) collective-permute-start(bf16[1024,256]{1,0:T(8,128)(2,1)S(1)} %get-tuple-element.65), channel_id=1, source_target_pairs={{0,3},{1,0},{2,1},{3,2},{4,7},{5,4},{6,5},{7,6},{8,11},{9,8},{10,9... | collective-permute-start | bytes 1572872 | tf_op jit(solution)/shard_map/ppermute | solution.py:623
  82.9 0.0 collective-permute-done.6
  82.9 0.1 add_convert_fusion.3
  83.0 0.6 collective-permute-start.9
  83.6 1.5 %collective-permute-start.8 = (bf16[128,1024]{1,0:T(8,128)(2,1)S(1)}, bf16[128,1024]{1,0:T(8,128)(2,1)S(1)}, u32[]{:S(2)}, u32[]{:S(2)}) collective-permute-start(bf16[128,1024]{1,0:T(8,128)(2,1)S(1)} %add_convert_fusion.3), channel_id=1, source_target_pairs={{0,16},{4,20},{8,24},{12,28},{16,0},{20,4},{24,8},{28,12},{1,17},{... | collective-permute-start | bytes 786440 | tf_op jit(solution)/shard_map/ppermute | solution.py:614
  85.0 0.0 collective-permute-done.5.other_ref
  85.1 1.5 %collective-permute-start.7 = (bf16[128,1024]{1,0:T(8,128)(2,1)S(1)}, bf16[128,1024]{1,0:T(8,128)(2,1)S(1)}, u32[]{:S(2)}, u32[]{:S(2)}) collective-permute-start(bf16[128,1024]{1,0:T(8,128)(2,1)S(1)} %add_convert_fusion.3), channel_id=1, source_target_pairs={{0,8},{4,12},{8,0},{12,4},{16,24},{20,28},{24,16},{28,20},{1,9},{5... | collective-permute-start | bytes 786440 | tf_op jit(solution)/shard_map/ppermute | solution.py:614
  86.5 20.7 %span_backward.1 = (bf16[4096,128]{1,0:T(8,128)(2,1)S(1)}, bf16[4096,128]{1,0:T(8,128)(2,1)S(1)}) custom-call(s32[64,128]{1,0:T(8,128)S(1)} %get-tuple-element.41.addr_ref, bf16[4096,128]{1,0:T(8,128)(2,1)S(1)} %get-tuple-element.54.mine_ref, bf16[4096,128]{1,0:T(8,128)(2,1)S(1)} %collective-permute-done.5.other_ref, ...), custom_call_target="tpu_custom_call" | custom-call | bytes 67108864 | tf_op jit(solution)/shard_map/span_backward/pallas_call | solution.py:580
  107.3 0.0 collective-permute-done.9
  107.3 0.0 copy-start.2
  107.3 0.0 collective-permute-done.7
  107.3 0.0 copy-start.3
  107.3 0.7 copy-done.3
  108.1 0.0 collective-permute-done.11
  108.1 0.4 collective-permute-start.12
  108.5 2.2 %collective-permute-done.13 = bf16[4096,128]{1,0:T(8,128)(2,1)S(1)} collective-permute-done((bf16[4096,128]{1,0:T(8,128)(2,1)S(1)}, bf16[4096,128]{1,0:T(8,128)(2,1)S(1)}, u32[]{:S(2)}, u32[]{:S(2)}) %collective-permute-start.13) | collective-permute-done | bytes 1048608 | tf_op jit(solution)/shard_map/ppermute | solution.py:614
  110.7 1.3 add_convert_fusion
  112.0 3.6 %all-to-all-start.2 = ((bf16[8,512,128]{2,1,0:T(8,128)(2,1)}), bf16[8,512,128]{2,1,0:T(8,128)(2,1)S(1)}, u32[]{:S(2)}, u32[]{:S(2)}) async-start(bf16[8,512,128]{2,1,0:T(8,128)(2,1)} %bitcast), calls=%async_computation.2 | async-start | bytes 2097152 | tf_op jit(solution)/shard_map/all_to_all | solution.py:618
  115.6 1.2 add_convert_fusion.2
  116.8 0.5 collective-permute-start.14
  117.2 1.2 collective-permute-done.14
  118.4 1.1 convert_multiply_fusion
  119.5 14.6 %collective-permute-done.12 = bf16[1024,256]{1,0:T(8,128)(2,1)} collective-permute-done((bf16[1024,256]{1,0:T(8,128)(2,1)}, bf16[1024,256]{1,0:T(8,128)(2,1)}, u32[]{:S(2)}, u32[]{:S(2)}) %collective-permute-start.12) | collective-permute-done | bytes 524320 | tf_op jit(solution)/shard_map/ppermute | solution.py:623
  134.1 2.1 %add_convert_fusion.1 = bf16[1024,256]{1,0:T(8,128)(2,1)} fusion(bf16[1024,256]{1,0:T(8,128)(2,1)} %collective-permute-done.12, bf16[1024,256]{1,0:T(8,128)(2,1)S(1)} %collective-permute-done.11, bf16[1024,256]{1,0:T(8,128)(2,1)S(1)} %collective-permute-done.10, bf16[1024,256]{1,0:T(8,128)(2,1)S(1)} %get-tuple-element.53), kind=kLoop, calls=%fused_computation.2 | loop fusion | flops 2097152 | bytes 2621440 | tf_op jit(solution)/shard_map/convert_element_type | solution.py:686
  136.2 1.4 %unpack_heads.1 = (bf16[1024,256]{1,0:T(8,128)(2,1)}, bf16[1024,256]{1,0:T(8,128)(2,1)}) custom-call(bf16[4,1024,128]{2,1,0:T(8,128)(2,1)S(1)} %bitcast.2), custom_call_target="tpu_custom_call" | custom-call | tf_op jit(solution)/shard_map/unpack_heads/pallas_call | solution.py:356
  (10 shorter events, 0.0 us)
Async XLA Ops:
  0.6 7.8 %copy-start.1 = (bf16[1024,256]{1,0:T(8,128)(2,1)S(1)}, bf16[1024,256]{1,0:T(8,128)(2,1)}, u32[]{:S(2)}) copy-start(bf16[1024,256]{1,0:T(8,128)(2,1)} %refs_0_.1) | copy-start | bytes 1572868
  3.2 21.4 %all-to-all-start = ((bf16[8,528,128]{2,1,0:T(8,128)(2,1)}), bf16[8,528,128]{2,1,0:T(8,128)(2,1)S(1)}, u32[]{:S(2)}, u32[]{:S(2)}) async-start(bf16[8,528,128]{2,1,0:T(8,128)(2,1)} %pack_heads.1), calls=%async_computation | async-start | bytes 2162688 | tf_op jit(solution)/shard_map/all_to_all | solution.py:618
  8.4 43.5 %copy-start = (bf16[256,1024]{1,0:T(8,128)(2,1)S(1)}, bf16[256,1024]{1,0:T(8,128)(2,1)}, u32[]{:S(2)}) copy-start(bf16[256,1024]{1,0:T(8,128)(2,1)} %weight_ref.3) | copy-start | bytes 1572868
  8.4 16.2 %collective-permute-start = (bf16[1024,256]{1,0:T(8,128)(2,1)S(1)}, bf16[1024,256]{1,0:T(8,128)(2,1)S(1)}, u32[]{:S(2)}, u32[]{:S(2)}) collective-permute-start(bf16[1024,256]{1,0:T(8,128)(2,1)S(1)} %copy-done.1), channel_id=1, source_target_pairs={{0,1},{1,2},{2,3},{3,0},{4,5},{5,6},{6,7},{7,4},{8,9},{9,10},{10,1... | collective-permute-start | bytes 1572872 | tf_op jit(solution)/shard_map/ppermute | solution.py:623
  24.7 4.3 %collective-permute-start.1 = (bf16[8,528,128]{2,1,0:T(8,128)(2,1)S(1)}, bf16[8,528,128]{2,1,0:T(8,128)(2,1)S(1)}, u32[]{:S(2)}, u32[]{:S(2)}) collective-permute-start(bf16[8,528,128]{2,1,0:T(8,128)(2,1)S(1)} %all-to-all-done.mine_ref), channel_id=1, source_target_pairs={{0,4},{4,0},{8,12},{12,8},{16,20},{20,16},{24,28},{28,24},{1,5},{5... | collective-permute-start | bytes 3244040 | tf_op jit(solution)/shard_map/ppermute | solution.py:614
  24.7 27.0 %collective-permute-start.3 = (bf16[1024,256]{1,0:T(8,128)(2,1)S(1)}, bf16[1024,256]{1,0:T(8,128)(2,1)S(1)}, u32[]{:S(2)}, u32[]{:S(2)}) collective-permute-start(bf16[1024,256]{1,0:T(8,128)(2,1)S(1)} %copy-done.1), channel_id=1, source_target_pairs={{0,3},{1,0},{2,1},{3,2},{4,7},{5,4},{6,5},{7,6},{8,11},{9,8},{10,9... | collective-permute-start | bytes 1572872 | tf_op jit(solution)/shard_map/ppermute | solution.py:623
  27.8 24.0 %collective-permute-start.2 = (bf16[1024,256]{1,0:T(8,128)(2,1)S(1)}, bf16[1024,256]{1,0:T(8,128)(2,1)S(1)}, u32[]{:S(2)}, u32[]{:S(2)}) collective-permute-start(bf16[1024,256]{1,0:T(8,128)(2,1)S(1)} %collective-permute-done.refs_1_), channel_id=1, source_target_pairs={{0,1},{1,2},{2,3},{3,0},{4,5},{5,6},{6,7},{7,4},{8,9},{9,10},{10,1... | collective-permute-start | bytes 1572872 | tf_op jit(solution)/shard_map/ppermute | solution.py:623
  51.8 2.7 %collective-permute-start.4 = (bf16[4096,128]{1,0:T(8,128)(2,1)S(1)}, bf16[4096,128]{1,0:T(8,128)(2,1)S(1)}, u32[]{:S(2)}, u32[]{:S(2)}) collective-permute-start(bf16[4096,128]{1,0:T(8,128)(2,1)S(1)} %get-tuple-element.48), channel_id=1, source_target_pairs={{0,4},{4,0},{8,12},{12,8},{16,20},{20,16},{24,28},{28,24},{1,5},{5... | collective-permute-start | bytes 3145736 | tf_op jit(solution)/shard_map/ppermute | solution.py:614
  76.0 9.0 %collective-permute-start.5 = (bf16[4096,128]{1,0:T(8,128)(2,1)S(1)}, bf16[4096,128]{1,0:T(8,128)(2,1)S(1)}, u32[]{:S(2)}, u32[]{:S(2)}) collective-permute-start(bf16[4096,128]{1,0:T(8,128)(2,1)S(1)} %get-tuple-element.55), channel_id=1, source_target_pairs={{0,4},{4,0},{8,12},{12,8},{16,20},{20,16},{24,28},{28,24},{1,5},{5... | collective-permute-start | bytes 3145736 | tf_op jit(solution)/shard_map/ppermute | solution.py:614
  78.5 4.4 %collective-permute-start.6 = (bf16[128,1024]{1,0:T(8,128)(2,1)S(1)}, bf16[128,1024]{1,0:T(8,128)(2,1)S(1)}, u32[]{:S(2)}, u32[]{:S(2)}) collective-permute-start(bf16[128,1024]{1,0:T(8,128)(2,1)S(1)} %get-tuple-element.62), channel_id=1, source_target_pairs={{0,4},{4,0},{8,12},{12,8},{16,20},{20,16},{24,28},{28,24},{1,5},{5... | collective-permute-start | bytes 786440 | tf_op jit(solution)/shard_map/ppermute | solution.py:614
  79.1 28.3 %collective-permute-start.10 = (bf16[1024,256]{1,0:T(8,128)(2,1)S(1)}, bf16[1024,256]{1,0:T(8,128)(2,1)S(1)}, u32[]{:S(2)}, u32[]{:S(2)}) collective-permute-start(bf16[1024,256]{1,0:T(8,128)(2,1)S(1)} %get-tuple-element.64), channel_id=1, source_target_pairs={{0,1},{1,2},{2,3},{3,0},{4,5},{5,6},{6,7},{7,4},{8,9},{9,10},{10,1... | collective-permute-start | bytes 1572872 | tf_op jit(solution)/shard_map/ppermute | solution.py:623
  80.6 27.5 %collective-permute-start.11 = (bf16[1024,256]{1,0:T(8,128)(2,1)S(1)}, bf16[1024,256]{1,0:T(8,128)(2,1)S(1)}, u32[]{:S(2)}, u32[]{:S(2)}) collective-permute-start(bf16[1024,256]{1,0:T(8,128)(2,1)S(1)} %get-tuple-element.65), channel_id=1, source_target_pairs={{0,3},{1,0},{2,1},{3,2},{4,7},{5,4},{6,5},{7,6},{8,11},{9,8},{10,9... | collective-permute-start | bytes 1572872 | tf_op jit(solution)/shard_map/ppermute | solution.py:623
  83.0 24.3 %collective-permute-start.9 = (bf16[128,1024]{1,0:T(8,128)(2,1)S(1)}, bf16[128,1024]{1,0:T(8,128)(2,1)S(1)}, u32[]{:S(2)}, u32[]{:S(2)}) collective-permute-start(bf16[128,1024]{1,0:T(8,128)(2,1)S(1)} %add_convert_fusion.3), channel_id=1, source_target_pairs={{0,24},{4,28},{8,16},{12,20},{16,8},{20,12},{24,0},{28,4},{1,25},{... | collective-permute-start | bytes 786440 | tf_op jit(solution)/shard_map/ppermute | solution.py:614
  83.6 23.7 %collective-permute-start.8 = (bf16[128,1024]{1,0:T(8,128)(2,1)S(1)}, bf16[128,1024]{1,0:T(8,128)(2,1)S(1)}, u32[]{:S(2)}, u32[]{:S(2)}) collective-permute-start(bf16[128,1024]{1,0:T(8,128)(2,1)S(1)} %add_convert_fusion.3), channel_id=1, source_target_pairs={{0,16},{4,20},{8,24},{12,28},{16,0},{20,4},{24,8},{28,12},{1,17},{... | collective-permute-start | bytes 786440 | tf_op jit(solution)/shard_map/ppermute | solution.py:614
  85.1 22.3 %collective-permute-start.7 = (bf16[128,1024]{1,0:T(8,128)(2,1)S(1)}, bf16[128,1024]{1,0:T(8,128)(2,1)S(1)}, u32[]{:S(2)}, u32[]{:S(2)}) collective-permute-start(bf16[128,1024]{1,0:T(8,128)(2,1)S(1)} %add_convert_fusion.3), channel_id=1, source_target_pairs={{0,8},{4,12},{8,0},{12,4},{16,24},{20,28},{24,16},{28,20},{1,9},{5... | collective-permute-start | bytes 786440 | tf_op jit(solution)/shard_map/ppermute | solution.py:614
  107.3 4.7 %copy-start.2 = (bf16[128,1024]{1,0:T(8,128)(2,1)}, bf16[128,1024]{1,0:T(8,128)(2,1)S(1)}, u32[]{:S(2)}) copy-start(bf16[128,1024]{1,0:T(8,128)(2,1)S(1)} %collective-permute-done.8) | copy-start | bytes 786436
  107.3 0.8 copy-start.3
  108.1 2.7 %collective-permute-start.13 = (bf16[4096,128]{1,0:T(8,128)(2,1)S(1)}, bf16[4096,128]{1,0:T(8,128)(2,1)S(1)}, u32[]{:S(2)}, u32[]{:S(2)}) collective-permute-start(bf16[4096,128]{1,0:T(8,128)(2,1)S(1)} %get-tuple-element.71), channel_id=1, source_target_pairs={{0,4},{4,0},{8,12},{12,8},{16,20},{20,16},{24,28},{28,24},{1,5},{5... | collective-permute-start | bytes 3145736 | tf_op jit(solution)/shard_map/ppermute | solution.py:614
  108.1 26.1 %collective-permute-start.12 = (bf16[1024,256]{1,0:T(8,128)(2,1)}, bf16[1024,256]{1,0:T(8,128)(2,1)}, u32[]{:S(2)}, u32[]{:S(2)}) collective-permute-start(bf16[1024,256]{1,0:T(8,128)(2,1)} %get-tuple-element.70), channel_id=1, source_target_pairs={{0,2},{1,3},{2,0},{3,1},{4,6},{5,7},{6,4},{7,5},{8,10},{9,11},{10,... | collective-permute-start | bytes 1572872 | tf_op jit(solution)/shard_map/ppermute | solution.py:623
  112.0 24.2 %all-to-all-start.2 = ((bf16[8,512,128]{2,1,0:T(8,128)(2,1)}), bf16[8,512,128]{2,1,0:T(8,128)(2,1)S(1)}, u32[]{:S(2)}, u32[]{:S(2)}) async-start(bf16[8,512,128]{2,1,0:T(8,128)(2,1)} %bitcast), calls=%async_computation.2 | async-start | bytes 2097152 | tf_op jit(solution)/shard_map/all_to_all | solution.py:618
  116.8 1.6 %collective-permute-start.14 = (bf16[128,1024]{1,0:T(8,128)(2,1)S(1)}, bf16[128,1024]{1,0:T(8,128)(2,1)S(1)}, u32[]{:S(2)}, u32[]{:S(2)}) collective-permute-start(bf16[128,1024]{1,0:T(8,128)(2,1)S(1)} %add_convert_fusion.2), channel_id=1, source_target_pairs={{0,4},{4,0},{8,12},{12,8},{16,20},{20,16},{24,28},{28,24},{1,5},{5... | collective-permute-start | bytes 786440 | tf_op jit(solution)/shard_map/ppermute | solution.py:614

commit v4 on v3

--- a/solution.py
+++ b/solution.py
@@ -95,6 +95,7 @@
             column,
         ],
         compiler_params=pltpu.CompilerParams(vmem_limit_bytes=10 * MIB),
+        out_specs=[whole(pltpu.VMEM)] * 4,
         name="find_places",
     )(mine)
 
@@ -340,6 +341,7 @@
         pack_kernel,
         out_shape=jax.ShapeDtypeStruct((rounds * heads, rows // 2 + 16, 2 * DH), BF16),
         compiler_params=pltpu.CompilerParams(vmem_limit_bytes=10 * MIB),
+        out_specs=whole(pltpu.VMEM),
         name="pack_heads",
     )(in_hbm(queries), in_hbm(values), in_hbm(slots))
 
@@ -394,6 +396,7 @@
         back_kernel,
         out_shape=jax.ShapeDtypeStruct((2 * width // DH, rows // 4, 2 * DH), BF16),
         compiler_params=pltpu.CompilerParams(vmem_limit_bytes=10 * MIB),
+        out_specs=whole(pltpu.VMEM),
         name="back_projection",
     )(weight, *grads)
 
@@ -423,6 +426,8 @@
         + [pltpu.HBM((rows, width), BF16)]
         + [jax.ShapeDtypeStruct((rows, width), BF16)] * (groups - 3),
         compiler_params=pltpu.CompilerParams(vmem_limit_bytes=10 * MIB),
+        in_specs=[whole(pltpu.VMEM)] * 2,
+        out_specs=[whole(pltpu.VMEM)] * 3 + [pl.BlockSpec()] + [whole(pltpu.VMEM)] * (groups - 3),
         name="project",
     )(weight, packed)
 
@@ -466,6 +471,7 @@
         weight_grad_kernel,
         out_shape=[jax.ShapeDtypeStruct((width // 2, width * groups), BF16)] * 2,
         compiler_params=pltpu.CompilerParams(vmem_limit_bytes=10 * MIB),
+        out_specs=[whole(pltpu.VMEM)] * 2,
         name="weight_grad",
     )(att, *grads)
 

time: 138 us -> 138 us (level)
  no operation moved by 1% of the time
where the time goes in v4:
time: 138 us
  Pallas kernels  55.6 us (40%)
  waiting for transfers between devices  34.4 us (25%)
  starting transfers between devices  22.6 us (16%)
  blocking collectives  17.9 us (13%)
  other arithmetic  5.74 us (4%)
    ppermute x6, waiting for transfers between devices, rotate(): lax.ppermute(value, 'head', [(i, (i + step) % count) for i in range(count)])  29.3 us
    pallas_call x1, Pallas kernels, forward(): pl.pallas_call(forward_kernel, grid=(blocks // GROUP,), out_shape=[jax.Sh...  22.7 us
    pallas_call x1, Pallas kernels, backward(): pl.pallas_call(backward_kernel, grid=(blocks // GROUP,), out_shape=[jax.S...  20.7 us
    all_to_all x1, blocking collectives, to_all(): return lax.all_to_all(value, 'seq', split_axis=0, concat_axis=0, tiled=True)  17.9 us
    ppermute x6, starting transfers between devices, rotate(): lax.ppermute(value, 'head', [(i, (i + step) % count) for i in range(count)])  9.01 us
    all_to_all x2, starting transfers between devices, to_all(): return lax.all_to_all(value, 'seq', split_axis=0, concat_axis=0, tiled=True)  8.73 us
    ppermute x9, waiting for transfers between devices, swap(): return lax.ppermute(value, 'seq', [(i, i ^ distance) for i in range(count)])  5.04 us
    ppermute x9, starting transfers between devices, swap(): return lax.ppermute(value, 'seq', [(i, i ^ distance) for i in range(count)])  4.83 us
  transfers between devices with their start and end apart: 17, of which 6 were waited for; matrix products, arithmetic and copies ran while one was open for 4% of the time, Pallas kernels for 35%

profile of v4, /device:TPU:0, one launch (start us, length us, event | category | flops | bytes accessed | tf_op | source)
XLA Modules:
  0.0 137.6 jit_solution(17138688378152974673)
XLA Ops:
  0.6 2.6 %pack_heads.1 = bf16[8,528,128]{2,1,0:T(8,128)(2,1)} custom-call(bf16[1024,256]{1,0:T(8,128)(2,1)} %query_ref.1, bf16[1024,256]{1,0:T(8,128)(2,1)} %value_ref.1, s32[2,4,1024]{2,1,0:T(4,128)} %slot_ref.1), custom_call_target="tpu_custom_call" | custom-call | tf_op jit(solution)/shard_map/pack_heads/pallas_call | solution.py:340
  3.2 5.2 %all-to-all-start = ((bf16[8,528,128]{2,1,0:T(8,128)(2,1)}), bf16[8,528,128]{2,1,0:T(8,128)(2,1)S(1)}, u32[]{:S(2)}, u32[]{:S(2)}) async-start(bf16[8,528,128]{2,1,0:T(8,128)(2,1)} %pack_heads.1), calls=%async_computation | async-start | bytes 2162688 | tf_op jit(solution)/shard_map/all_to_all | solution.py:624
  8.4 0.0 copy-start
  8.4 1.6 %collective-permute-start = (bf16[1024,256]{1,0:T(8,128)(2,1)S(1)}, bf16[1024,256]{1,0:T(8,128)(2,1)S(1)}, u32[]{:S(2)}, u32[]{:S(2)}) collective-permute-start(bf16[1024,256]{1,0:T(8,128)(2,1)S(1)} %copy-done.1), channel_id=1, source_target_pairs={{0,1},{1,2},{2,3},{3,0},{4,5},{5,6},{6,7},{7,4},{8,9},{9,10},{10,1... | collective-permute-start | bytes 1572872 | tf_op jit(solution)/shard_map/ppermute | solution.py:629
  10.1 14.6 %collective-permute-done.refs_1_ = bf16[1024,256]{1,0:T(8,128)(2,1)S(1)} collective-permute-done((bf16[1024,256]{1,0:T(8,128)(2,1)S(1)}, bf16[1024,256]{1,0:T(8,128)(2,1)S(1)}, u32[]{:S(2)}, u32[]{:S(2)}) %collective-permute-start) | collective-permute-done | bytes 524320 | tf_op jit(solution)/shard_map/ppermute | solution.py:629
  24.7 0.0 all-to-all-done.mine_ref
  24.7 3.1 %collective-permute-start.3 = (bf16[1024,256]{1,0:T(8,128)(2,1)S(1)}, bf16[1024,256]{1,0:T(8,128)(2,1)S(1)}, u32[]{:S(2)}, u32[]{:S(2)}) collective-permute-start(bf16[1024,256]{1,0:T(8,128)(2,1)S(1)} %copy-done.1), channel_id=1, source_target_pairs={{0,3},{1,0},{2,1},{3,2},{4,7},{5,4},{6,5},{7,6},{8,11},{9,8},{10,9... | collective-permute-start | bytes 1572872 | tf_op jit(solution)/shard_map/ppermute | solution.py:629
  27.8 0.0 collective-permute-start.2
  27.8 1.2 find_places.1
  29.0 0.0 collective-permute-done.1.other_ref
  29.0 22.7 %span_forward.1 = (bf16[4096,128]{1,0:T(8,128)(2,1)S(1)}, bf16[4096,128]{1,0:T(8,128)(2,1)S(1)}, bf16[64,128,256]{2,1,0:T(8,128)(2,1)}, bf16[8192,128]{1,0:T(8,128)(2,1)}, bf16[8192,128]{1,0:T(8,128)(2,1)}) custom-call(s32[64,128]{1,0:T(8,128)S(1)} %get-tuple-element.41.addr_ref, bf16[8,528,128]{2,1,0:T(8,128)(2,1)S(1)} %all-to-all-done.mine_ref, ...), custom_call_target="tpu_custom_call" | custom-call | bytes 67108864 | tf_op jit(solution)/shard_map/span_forward/pallas_call | solution.py:213
  51.7 0.0 collective-permute-done.3.refs_3_
  51.7 0.1 collective-permute-done.2.refs_2_
  51.8 0.2 collective-permute-start.4
  52.0 0.8 back_projection.1.grad_ref
  52.8 1.6 %collective-permute-done.4.peer_ref = bf16[4096,128]{1,0:T(8,128)(2,1)S(1)} collective-permute-done((bf16[4096,128]{1,0:T(8,128)(2,1)S(1)}, bf16[4096,128]{1,0:T(8,128)(2,1)S(1)}, u32[]{:S(2)}, u32[]{:S(2)}) %collective-permute-start.4) | collective-permute-done | bytes 1048608 | tf_op jit(solution)/shard_map/ppermute | solution.py:620
  54.4 1.4 %mix_attention.1 = bf16[8,512,128]{2,1,0:T(8,128)(2,1)S(1)} custom-call(bf16[4096,128]{1,0:T(8,128)(2,1)S(1)} %get-tuple-element.46.own_ref, bf16[4096,128]{1,0:T(8,128)(2,1)S(1)} %collective-permute-done.4.peer_ref, bf16[8,256,128]{2,1,0:T(8,128)(2,1)S(1)} %back_projection.1.grad_ref), custom_call_target="tpu_custom_call" | custom-call | tf_op jit(solution)/shard_map/mix_attention/pallas_call | solution.py:302
  55.8 17.9 %all_to_all.15.packed_ref.both_ref = bf16[8,512,128]{2,1,0:T(8,128)(2,1)S(1)} all-to-all(bf16[8,512,128]{2,1,0:T(8,128)(2,1)S(1)} %mix_attention.1), channel_id=1, replica_groups=mesh['seq'=8,'head'=4] {'seq'}, dimensions={0} | all-to-all | bytes 2097152 | tf_op jit(solution)/shard_map/all_to_all | solution.py:624
  73.7 2.3 %mix_grad.1 = (bf16[4096,128]{1,0:T(8,128)(2,1)S(1)}, bf16[4096,128]{1,0:T(8,128)(2,1)S(1)}) custom-call(bf16[4096,128]{1,0:T(8,128)(2,1)S(1)} %get-tuple-element.46.own_ref, bf16[4096,128]{1,0:T(8,128)(2,1)S(1)} %collective-permute-done.4.peer_ref, bf16[8,512,128]{2,1,0:T(8,128)(2,1)S(1)} %all_to_all.15.packed_ref.both_ref), custom_call_target="tpu_custom_call" | custom-call | tf_op jit(solution)/shard_map/mix_grad/pallas_call | solution.py:313
  76.0 0.1 collective-permute-start.5
  76.1 1.6 %project.1 = (bf16[1024,256]{1,0:T(8,128)(2,1)S(1)}, bf16[1024,256]{1,0:T(8,128)(2,1)S(1)}, bf16[1024,256]{1,0:T(8,128)(2,1)S(1)}, bf16[1024,256]{1,0:T(8,128)(2,1)}, bf16[1024,256]{1,0:T(8,128)(2,1)S(1)}) custom-call(bf16[256,1024]{1,0:T(8,128)(2,1)S(1)} %copy-done, bf16[8,512,128]{2,1,0:T(8,128)(2,1)S(1)} %all_to_all.15.packed_ref.both_ref), custom_call_target="tpu_custom_call" | custom-call | tf_op jit(solution)/shard_map/project/pallas_call | solution.py:423
  77.7 0.8 weight_grad.1
  78.5 0.5 collective-permute-start.6
  79.1 1.5 %collective-permute-start.10 = (bf16[1024,256]{1,0:T(8,128)(2,1)S(1)}, bf16[1024,256]{1,0:T(8,128)(2,1)S(1)}, u32[]{:S(2)}, u32[]{:S(2)}) collective-permute-start(bf16[1024,256]{1,0:T(8,128)(2,1)S(1)} %get-tuple-element.64), channel_id=1, source_target_pairs={{0,1},{1,2},{2,3},{3,0},{4,5},{5,6},{6,7},{7,4},{8,9},{9,10},{10,1... | collective-permute-start | bytes 1572872 | tf_op jit(solution)/shard_map/ppermute | solution.py:629
  80.6 2.3 %collective-permute-start.11 = (bf16[1024,256]{1,0:T(8,128)(2,1)S(1)}, bf16[1024,256]{1,0:T(8,128)(2,1)S(1)}, u32[]{:S(2)}, u32[]{:S(2)}) collective-permute-start(bf16[1024,256]{1,0:T(8,128)(2,1)S(1)} %get-tuple-element.65), channel_id=1, source_target_pairs={{0,3},{1,0},{2,1},{3,2},{4,7},{5,4},{6,5},{7,6},{8,11},{9,8},{10,9... | collective-permute-start | bytes 1572872 | tf_op jit(solution)/shard_map/ppermute | solution.py:629
  82.9 0.0 collective-permute-done.6
  82.9 0.1 add_convert_fusion.3
  83.0 0.6 collective-permute-start.9
  83.6 1.5 %collective-permute-start.8 = (bf16[128,1024]{1,0:T(8,128)(2,1)S(1)}, bf16[128,1024]{1,0:T(8,128)(2,1)S(1)}, u32[]{:S(2)}, u32[]{:S(2)}) collective-permute-start(bf16[128,1024]{1,0:T(8,128)(2,1)S(1)} %add_convert_fusion.3), channel_id=1, source_target_pairs={{0,16},{4,20},{8,24},{12,28},{16,0},{20,4},{24,8},{28,12},{1,17},{... | collective-permute-start | bytes 786440 | tf_op jit(solution)/shard_map/ppermute | solution.py:620
  85.0 0.0 collective-permute-done.5.other_ref
  85.1 1.5 %collective-permute-start.7 = (bf16[128,1024]{1,0:T(8,128)(2,1)S(1)}, bf16[128,1024]{1,0:T(8,128)(2,1)S(1)}, u32[]{:S(2)}, u32[]{:S(2)}) collective-permute-start(bf16[128,1024]{1,0:T(8,128)(2,1)S(1)} %add_convert_fusion.3), channel_id=1, source_target_pairs={{0,8},{4,12},{8,0},{12,4},{16,24},{20,28},{24,16},{28,20},{1,9},{5... | collective-permute-start | bytes 786440 | tf_op jit(solution)/shard_map/ppermute | solution.py:620
  86.5 20.7 %span_backward.1 = (bf16[4096,128]{1,0:T(8,128)(2,1)S(1)}, bf16[4096,128]{1,0:T(8,128)(2,1)S(1)}) custom-call(s32[64,128]{1,0:T(8,128)S(1)} %get-tuple-element.41.addr_ref, bf16[4096,128]{1,0:T(8,128)(2,1)S(1)} %get-tuple-element.54.mine_ref, bf16[4096,128]{1,0:T(8,128)(2,1)S(1)} %collective-permute-done.5.other_ref, ...), custom_call_target="tpu_custom_call" | custom-call | bytes 67108864 | tf_op jit(solution)/shard_map/span_backward/pallas_call | solution.py:586
  107.3 0.0 collective-permute-done.9
  107.3 0.0 copy-start.2
  107.3 0.0 collective-permute-done.7
  107.3 0.0 copy-start.3
  107.3 0.7 copy-done.3
  108.1 0.4 collective-permute-start.12
  108.5 2.2 %collective-permute-done.13 = bf16[4096,128]{1,0:T(8,128)(2,1)S(1)} collective-permute-done((bf16[4096,128]{1,0:T(8,128)(2,1)S(1)}, bf16[4096,128]{1,0:T(8,128)(2,1)S(1)}, u32[]{:S(2)}, u32[]{:S(2)}) %collective-permute-start.13) | collective-permute-done | bytes 1048608 | tf_op jit(solution)/shard_map/ppermute | solution.py:620
  110.7 1.3 add_convert_fusion
  112.0 3.6 %all-to-all-start.2 = ((bf16[8,512,128]{2,1,0:T(8,128)(2,1)}), bf16[8,512,128]{2,1,0:T(8,128)(2,1)S(1)}, u32[]{:S(2)}, u32[]{:S(2)}) async-start(bf16[8,512,128]{2,1,0:T(8,128)(2,1)} %bitcast), calls=%async_computation.2 | async-start | bytes 2097152 | tf_op jit(solution)/shard_map/all_to_all | solution.py:624
  115.6 1.2 add_convert_fusion.2
  116.8 0.5 collective-permute-start.14
  117.2 1.2 collective-permute-done.14
  118.4 1.1 convert_multiply_fusion
  119.5 14.6 %collective-permute-done.12 = bf16[1024,256]{1,0:T(8,128)(2,1)} collective-permute-done((bf16[1024,256]{1,0:T(8,128)(2,1)}, bf16[1024,256]{1,0:T(8,128)(2,1)}, u32[]{:S(2)}, u32[]{:S(2)}) %collective-permute-start.12) | collective-permute-done | bytes 524320 | tf_op jit(solution)/shard_map/ppermute | solution.py:629
  134.1 2.1 %add_convert_fusion.1 = bf16[1024,256]{1,0:T(8,128)(2,1)} fusion(bf16[1024,256]{1,0:T(8,128)(2,1)} %collective-permute-done.12, bf16[1024,256]{1,0:T(8,128)(2,1)S(1)} %collective-permute-done.11, bf16[1024,256]{1,0:T(8,128)(2,1)S(1)} %collective-permute-done.10, bf16[1024,256]{1,0:T(8,128)(2,1)S(1)} %get-tuple-element.53), kind=kLoop, calls=%fused_computation.2 | loop fusion | flops 2097152 | bytes 2621440 | tf_op jit(solution)/shard_map/convert_element_type | solution.py:692
  136.2 1.4 %unpack_heads.1 = (bf16[1024,256]{1,0:T(8,128)(2,1)}, bf16[1024,256]{1,0:T(8,128)(2,1)}) custom-call(bf16[4,1024,128]{2,1,0:T(8,128)(2,1)S(1)} %bitcast.2), custom_call_target="tpu_custom_call" | custom-call | tf_op jit(solution)/shard_map/unpack_heads/pallas_call | solution.py:358
  (10 shorter events, 0.0 us)
Async XLA Ops:
  0.6 7.8 %copy-start.1 = (bf16[1024,256]{1,0:T(8,128)(2,1)S(1)}, bf16[1024,256]{1,0:T(8,128)(2,1)}, u32[]{:S(2)}) copy-start(bf16[1024,256]{1,0:T(8,128)(2,1)} %refs_0_.1) | copy-start | bytes 1572868
  3.2 21.4 %all-to-all-start = ((bf16[8,528,128]{2,1,0:T(8,128)(2,1)}), bf16[8,528,128]{2,1,0:T(8,128)(2,1)S(1)}, u32[]{:S(2)}, u32[]{:S(2)}) async-start(bf16[8,528,128]{2,1,0:T(8,128)(2,1)} %pack_heads.1), calls=%async_computation | async-start | bytes 2162688 | tf_op jit(solution)/shard_map/all_to_all | solution.py:624
  8.4 43.5 %copy-start = (bf16[256,1024]{1,0:T(8,128)(2,1)S(1)}, bf16[256,1024]{1,0:T(8,128)(2,1)}, u32[]{:S(2)}) copy-start(bf16[256,1024]{1,0:T(8,128)(2,1)} %weight_ref.3) | copy-start | bytes 1572868
  8.4 16.2 %collective-permute-start = (bf16[1024,256]{1,0:T(8,128)(2,1)S(1)}, bf16[1024,256]{1,0:T(8,128)(2,1)S(1)}, u32[]{:S(2)}, u32[]{:S(2)}) collective-permute-start(bf16[1024,256]{1,0:T(8,128)(2,1)S(1)} %copy-done.1), channel_id=1, source_target_pairs={{0,1},{1,2},{2,3},{3,0},{4,5},{5,6},{6,7},{7,4},{8,9},{9,10},{10,1... | collective-permute-start | bytes 1572872 | tf_op jit(solution)/shard_map/ppermute | solution.py:629
  24.7 4.3 %collective-permute-start.1 = (bf16[8,528,128]{2,1,0:T(8,128)(2,1)S(1)}, bf16[8,528,128]{2,1,0:T(8,128)(2,1)S(1)}, u32[]{:S(2)}, u32[]{:S(2)}) collective-permute-start(bf16[8,528,128]{2,1,0:T(8,128)(2,1)S(1)} %all-to-all-done.mine_ref), channel_id=1, source_target_pairs={{0,4},{4,0},{8,12},{12,8},{16,20},{20,16},{24,28},{28,24},{1,5},{5... | collective-permute-start | bytes 3244040 | tf_op jit(solution)/shard_map/ppermute | solution.py:620
  24.7 27.0 %collective-permute-start.3 = (bf16[1024,256]{1,0:T(8,128)(2,1)S(1)}, bf16[1024,256]{1,0:T(8,128)(2,1)S(1)}, u32[]{:S(2)}, u32[]{:S(2)}) collective-permute-start(bf16[1024,256]{1,0:T(8,128)(2,1)S(1)} %copy-done.1), channel_id=1, source_target_pairs={{0,3},{1,0},{2,1},{3,2},{4,7},{5,4},{6,5},{7,6},{8,11},{9,8},{10,9... | collective-permute-start | bytes 1572872 | tf_op jit(solution)/shard_map/ppermute | solution.py:629
  27.8 24.0 %collective-permute-start.2 = (bf16[1024,256]{1,0:T(8,128)(2,1)S(1)}, bf16[1024,256]{1,0:T(8,128)(2,1)S(1)}, u32[]{:S(2)}, u32[]{:S(2)}) collective-permute-start(bf16[1024,256]{1,0:T(8,128)(2,1)S(1)} %collective-permute-done.refs_1_), channel_id=1, source_target_pairs={{0,1},{1,2},{2,3},{3,0},{4,5},{5,6},{6,7},{7,4},{8,9},{9,10},{10,1... | collective-permute-start | bytes 1572872 | tf_op jit(solution)/shard_map/ppermute | solution.py:629
  51.8 2.7 %collective-permute-start.4 = (bf16[4096,128]{1,0:T(8,128)(2,1)S(1)}, bf16[4096,128]{1,0:T(8,128)(2,1)S(1)}, u32[]{:S(2)}, u32[]{:S(2)}) collective-permute-start(bf16[4096,128]{1,0:T(8,128)(2,1)S(1)} %get-tuple-element.48), channel_id=1, source_target_pairs={{0,4},{4,0},{8,12},{12,8},{16,20},{20,16},{24,28},{28,24},{1,5},{5... | collective-permute-start | bytes 3145736 | tf_op jit(solution)/shard_map/ppermute | solution.py:620
  76.0 9.0 %collective-permute-start.5 = (bf16[4096,128]{1,0:T(8,128)(2,1)S(1)}, bf16[4096,128]{1,0:T(8,128)(2,1)S(1)}, u32[]{:S(2)}, u32[]{:S(2)}) collective-permute-start(bf16[4096,128]{1,0:T(8,128)(2,1)S(1)} %get-tuple-element.55), channel_id=1, source_target_pairs={{0,4},{4,0},{8,12},{12,8},{16,20},{20,16},{24,28},{28,24},{1,5},{5... | collective-permute-start | bytes 3145736 | tf_op jit(solution)/shard_map/ppermute | solution.py:620
  78.5 4.4 %collective-permute-start.6 = (bf16[128,1024]{1,0:T(8,128)(2,1)S(1)}, bf16[128,1024]{1,0:T(8,128)(2,1)S(1)}, u32[]{:S(2)}, u32[]{:S(2)}) collective-permute-start(bf16[128,1024]{1,0:T(8,128)(2,1)S(1)} %get-tuple-element.62), channel_id=1, source_target_pairs={{0,4},{4,0},{8,12},{12,8},{16,20},{20,16},{24,28},{28,24},{1,5},{5... | collective-permute-start | bytes 786440 | tf_op jit(solution)/shard_map/ppermute | solution.py:620
  79.1 28.3 %collective-permute-start.10 = (bf16[1024,256]{1,0:T(8,128)(2,1)S(1)}, bf16[1024,256]{1,0:T(8,128)(2,1)S(1)}, u32[]{:S(2)}, u32[]{:S(2)}) collective-permute-start(bf16[1024,256]{1,0:T(8,128)(2,1)S(1)} %get-tuple-element.64), channel_id=1, source_target_pairs={{0,1},{1,2},{2,3},{3,0},{4,5},{5,6},{6,7},{7,4},{8,9},{9,10},{10,1... | collective-permute-start | bytes 1572872 | tf_op jit(solution)/shard_map/ppermute | solution.py:629
  80.6 27.5 %collective-permute-start.11 = (bf16[1024,256]{1,0:T(8,128)(2,1)S(1)}, bf16[1024,256]{1,0:T(8,128)(2,1)S(1)}, u32[]{:S(2)}, u32[]{:S(2)}) collective-permute-start(bf16[1024,256]{1,0:T(8,128)(2,1)S(1)} %get-tuple-element.65), channel_id=1, source_target_pairs={{0,3},{1,0},{2,1},{3,2},{4,7},{5,4},{6,5},{7,6},{8,11},{9,8},{10,9... | collective-permute-start | bytes 1572872 | tf_op jit(solution)/shard_map/ppermute | solution.py:629
  83.0 24.3 %collective-permute-start.9 = (bf16[128,1024]{1,0:T(8,128)(2,1)S(1)}, bf16[128,1024]{1,0:T(8,128)(2,1)S(1)}, u32[]{:S(2)}, u32[]{:S(2)}) collective-permute-start(bf16[128,1024]{1,0:T(8,128)(2,1)S(1)} %add_convert_fusion.3), channel_id=1, source_target_pairs={{0,24},{4,28},{8,16},{12,20},{16,8},{20,12},{24,0},{28,4},{1,25},{... | collective-permute-start | bytes 786440 | tf_op jit(solution)/shard_map/ppermute | solution.py:620
  83.6 23.7 %collective-permute-start.8 = (bf16[128,1024]{1,0:T(8,128)(2,1)S(1)}, bf16[128,1024]{1,0:T(8,128)(2,1)S(1)}, u32[]{:S(2)}, u32[]{:S(2)}) collective-permute-start(bf16[128,1024]{1,0:T(8,128)(2,1)S(1)} %add_convert_fusion.3), channel_id=1, source_target_pairs={{0,16},{4,20},{8,24},{12,28},{16,0},{20,4},{24,8},{28,12},{1,17},{... | collective-permute-start | bytes 786440 | tf_op jit(solution)/shard_map/ppermute | solution.py:620
  85.1 22.2 %collective-permute-start.7 = (bf16[128,1024]{1,0:T(8,128)(2,1)S(1)}, bf16[128,1024]{1,0:T(8,128)(2,1)S(1)}, u32[]{:S(2)}, u32[]{:S(2)}) collective-permute-start(bf16[128,1024]{1,0:T(8,128)(2,1)S(1)} %add_convert_fusion.3), channel_id=1, source_target_pairs={{0,8},{4,12},{8,0},{12,4},{16,24},{20,28},{24,16},{28,20},{1,9},{5... | collective-permute-start | bytes 786440 | tf_op jit(solution)/shard_map/ppermute | solution.py:620
  107.3 4.7 %copy-start.2 = (bf16[128,1024]{1,0:T(8,128)(2,1)}, bf16[128,1024]{1,0:T(8,128)(2,1)S(1)}, u32[]{:S(2)}) copy-start(bf16[128,1024]{1,0:T(8,128)(2,1)S(1)} %collective-permute-done.8) | copy-start | bytes 786436
  107.3 0.8 copy-start.3
  108.1 2.7 %collective-permute-start.13 = (bf16[4096,128]{1,0:T(8,128)(2,1)S(1)}, bf16[4096,128]{1,0:T(8,128)(2,1)S(1)}, u32[]{:S(2)}, u32[]{:S(2)}) collective-permute-start(bf16[4096,128]{1,0:T(8,128)(2,1)S(1)} %get-tuple-element.71), channel_id=1, source_target_pairs={{0,4},{4,0},{8,12},{12,8},{16,20},{20,16},{24,28},{28,24},{1,5},{5... | collective-permute-start | bytes 3145736 | tf_op jit(solution)/shard_map/ppermute | solution.py:620
  108.1 26.0 %collective-permute-start.12 = (bf16[1024,256]{1,0:T(8,128)(2,1)}, bf16[1024,256]{1,0:T(8,128)(2,1)}, u32[]{:S(2)}, u32[]{:S(2)}) collective-permute-start(bf16[1024,256]{1,0:T(8,128)(2,1)} %get-tuple-element.70), channel_id=1, source_target_pairs={{0,2},{1,3},{2,0},{3,1},{4,6},{5,7},{6,4},{7,5},{8,10},{9,11},{10,... | collective-permute-start | bytes 1572872 | tf_op jit(solution)/shard_map/ppermute | solution.py:629
  112.0 24.2 %all-to-all-start.2 = ((bf16[8,512,128]{2,1,0:T(8,128)(2,1)}), bf16[8,512,128]{2,1,0:T(8,128)(2,1)S(1)}, u32[]{:S(2)}, u32[]{:S(2)}) async-start(bf16[8,512,128]{2,1,0:T(8,128)(2,1)} %bitcast), calls=%async_computation.2 | async-start | bytes 2097152 | tf_op jit(solution)/shard_map/all_to_all | solution.py:624
  116.8 1.6 %collective-permute-start.14 = (bf16[128,1024]{1,0:T(8,128)(2,1)S(1)}, bf16[128,1024]{1,0:T(8,128)(2,1)S(1)}, u32[]{:S(2)}, u32[]{:S(2)}) collective-permute-start(bf16[128,1024]{1,0:T(8,128)(2,1)S(1)} %add_convert_fusion.2), channel_id=1, source_target_pairs={{0,4},{4,0},{8,12},{12,8},{16,20},{20,16},{24,28},{28,24},{1,5},{5... | collective-permute-start | bytes 786440 | tf_op jit(solution)/shard_map/ppermute | solution.py:620
